TPU v7x, 128 devices: a whole 4x4x4 slice. The times are simulated.
128 devices in a mesh: gx: 16 (over y, z), gy: 8 (over x, core).
Axes of the slice: x: 4, y: 4, z: 4, core: 2. Of those that a mesh axis runs over, the one named last changes fastest.
Arguments:
- particle_feat: bfloat16 [2048, 64, 128], P(('gx', 'gy')), may hold values from -6 to 6
- block_counts: int32 [2048], P(('gx', 'gy')), may hold values from 1 to 128, 196608 in all
- entry_block: int32 [4096], P(('gx', 'gy')), may hold values from 0 to 15
- entry_dest: int32 [4096, 1], P(('gx', 'gy')), may hold values from 0 to 127, as said below
- entry_nodes: int32 [4096, 128], P(('gx', 'gy')), may hold values from 0 to 4095
- entry_weights: bfloat16 [4096, 128, 128], P(('gx', 'gy')), may hold values from 0 to 0.1796875
- conv_in: bfloat16 [3, 64, 576], replicated, may hold values from -0.15625 to 0.15625
- conv_mid: bfloat16 [3, 64, 576], replicated, may hold values from -0.15625 to 0.15625
- conv_out: bfloat16 [3, 64, 576], replicated, may hold values from -0.15625 to 0.15625
- head_weight: float32 [3, 64], replicated, may hold values from -0.75 to 0.75
Outputs:
- velocity: float32 [2048, 3, 128], P(('gx', 'gy'))
Inputs may be any that keep to these rules, and one draw needn't show every extreme that they name: `entry_dest`: linear index 8 * (x index) + (y index) of the tile; it is the sending device's own tile or a tile beside it in x, y or both (one step each way, no wrap); among the rows of one device no tile is named more than 8 times, and the sender's own tile exactly 8 times. `block_counts`: the first that many slots of the block are live; some block is full.
All inputs are finite; a program needn't handle non-finite values.
Results may differ from a plain program's by a relative error of at most 0.0045.
Values may be sent and summed in bfloat16 or wider, within the bound.
No kernel may reach another device: no remote copies, remote signals or barrier semaphores. Data moves between devices by JAX's collectives and lax.ppermute only.
A program may use at most 128 MiB of HBM per device.

v0:
```python
import functools

import jax
import jax.numpy as jnp
from jax import lax
from jax.experimental import pallas as pl
from jax.experimental.pallas import tpu as pltpu
from jax.sharding import PartitionSpec as P

BF = jnp.bfloat16
F32 = jnp.float32
I32 = jnp.int32

CHAN = 64
LANES = 128
TILE_X = 4
TILE_Y = 8
SLOTS = 8
GROUP = 4
VMEM_LIMIT = 40 * 1024 * 1024

VM = pl.BlockSpec(memory_space=pltpu.VMEM)
SM = pl.BlockSpec(memory_space=pltpu.SMEM)
NT = (((1,), (1,)), ((), ()))


def call(kernel, outs, ins, scratch, flops):
    return pl.pallas_call(
        kernel,
        out_shape=[jax.ShapeDtypeStruct(s, d) for s, d in outs],
        in_specs=ins,
        out_specs=[VM] * len(outs),
        scratch_shapes=scratch,
        compiler_params=pltpu.CompilerParams(vmem_limit_bytes=VMEM_LIMIT),
        cost_estimate=pl.CostEstimate(flops=flops, bytes_accessed=2000000, transcendentals=0),
    )


def partial_kernel(
    where_ref, counts_ref, block_ref, dest_ref, feat_ref, nodes_ref, weight_ref, *rest
):
    outs = rest[:9]
    part, hi_all, lo_all, index, taken, entry_of = rest[9:]
    entries = weight_ref.shape[0]
    lane = lax.broadcasted_iota(I32, (CHAN, LANES), 1)
    for e in range(entries):
        block = block_ref[e]
        feat = jnp.where(lane < counts_ref[block], feat_ref[block].astype(F32), 0.0).astype(BF)
        value = jnp.dot(feat, weight_ref[e], preferred_element_type=F32)
        part[e] = value.astype(BF)
    nodes = nodes_ref[...]
    hi_all[...] = (nodes >> 8).astype(F32)
    lo_all[...] = (nodes & 255).astype(F32)
    index[...] = jnp.full(index.shape, -1.0, F32)
    for d in range(9):
        taken[d] = 0

    def place(e, carry):
        tile = dest_ref[e]
        d = (tile // where_ref[2] - where_ref[0] + 1) * 3 + (tile % where_ref[2] - where_ref[1] + 1)
        s = taken[d]
        taken[d] = s + 1
        entry_of[d * SLOTS + s] = e
        index[pl.ds(d * 16 + s, 1), :] = hi_all[pl.ds(e, 1), :]
        index[pl.ds(d * 16 + 8 + s, 1), :] = lo_all[pl.ds(e, 1), :]
        return carry

    lax.fori_loop(0, entries, place, 0)
    for d in range(9):
        count = taken[d]

        def copy(s, carry, d=d):
            outs[d][s] = part[entry_of[d * SLOTS + s]]
            return carry

        lax.fori_loop(0, count, copy, 0)
        outs[d][SLOTS, 0:16, :] = index[d * 16 : d * 16 + 16, :].astype(BF)
        outs[d][SLOTS, 16:32, :] = jnp.full((16, LANES), count.astype(F32), F32).astype(BF)
        outs[d][SLOTS, 32:64, :] = jnp.zeros((32, LANES), BF)


def scatter_kernel(*refs):
    got = refs[:9]
    grid_ref, low_ref, high_ref = refs[9:12]
    values, index, hi_all, lo_all, acc = refs[12:]
    hi_all[...] = jnp.full(hi_all.shape, -1.0, F32)
    lo_all[...] = jnp.full(lo_all.shape, -1.0, F32)
    acc[...] = jnp.zeros(acc.shape, F32)
    counts = []
    for d in range(9):
        index[d * 16 : d * 16 + 16, :] = got[d][SLOTS, 0:16, :].astype(F32)
        counts.append(jnp.max(got[d][SLOTS, 16:32, :].astype(F32)).astype(I32))
    filled = jnp.int32(0)
    for d in range(9):

        def copy(s, pos, d=d):
            values[pos] = got[d][s]
            hi_all[pl.ds(pos, 1), :] = index[pl.ds(d * 16 + s, 1), :]
            lo_all[pl.ds(pos, 1), :] = index[pl.ds(d * 16 + 8 + s, 1), :]
            return pos + 1

        filled = lax.fori_loop(0, counts[d], copy, filled)
    row = lax.broadcasted_iota(I32, (256, LANES), 0).astype(F32)

    def step(g, carry):
        left = [[] for _ in range(16)]
        right = []
        for j in range(GROUP):
            e = g * GROUP + j
            value = values[e]
            hi = jnp.broadcast_to(hi_all[pl.ds(e, 1), :], (CHAN, LANES)).astype(BF)
            lo = lo_all[pl.ds(e, 1), :]
            right.append(jnp.where(row == lo, 1.0, 0.0).astype(BF))
            for t in range(16):
                left[t].append(jnp.where(hi == jnp.array(t, BF), value, jnp.array(0, BF)))
        a = jnp.concatenate([jnp.concatenate(rows, axis=1) for rows in left], axis=0)
        b = jnp.concatenate(right, axis=1)
        acc[...] += lax.dot_general(a, b, NT, preferred_element_type=F32)
        return carry

    lax.fori_loop(0, (filled + GROUP - 1) // GROUP, step, 0)
    for t in range(16):
        for half in range(2):
            column = acc[t * CHAN : (t + 1) * CHAN, half * LANES : (half + 1) * LANES].astype(BF)
            x = t // 4
            y = (t % 4) * 2 + half
            grid_ref[x, y] = column
            if x == 0:
                low_ref[y] = column
            if x == TILE_X - 1:
                high_ref[y] = column


def shifted(column):
    lane = lax.broadcasted_iota(I32, column.shape, 1)
    wide = column.astype(F32)
    before = jnp.where(lane == 0, 0.0, pltpu.roll(wide, 1, 1)).astype(BF)
    after = jnp.where(lane == LANES - 1, 0.0, pltpu.roll(wide, LANES - 1, 1)).astype(BF)
    return jnp.concatenate([before, column, after], axis=0)


def conv_rows(stack, weight_ref, size_x, size_y, put):
    weight = weight_ref[...]
    for y in range(0, size_y, 2):
        sums = [None] * size_x
        for x in range(size_x + 2):
            rhs = jnp.concatenate(
                [
                    stack[x, y : y + 3].reshape(9 * CHAN, LANES),
                    stack[x, y + 1 : y + 4].reshape(9 * CHAN, LANES),
                ],
                axis=1,
            )
            first = max(0, x - size_x + 1)
            last = min(2, x)
            prod = jnp.dot(
                weight[first * CHAN : (last + 1) * CHAN], rhs, preferred_element_type=F32
            )
            for a in range(first, last + 1):
                piece = prod[(a - first) * CHAN : (a - first + 1) * CHAN]
                out = x - a
                sums[out] = piece if sums[out] is None else sums[out] + piece
            if x >= 2:
                put(x - 2, y, sums[x - 2][:, :LANES])
                put(x - 2, y + 1, sums[x - 2][:, LANES:])
                sums[x - 2] = None


def silu(v):
    return v / (1.0 + jnp.exp(-v))


def edges(where_ref):
    x_lo = where_ref[0] > 0
    x_hi = where_ref[0] < where_ref[3] - 1
    y_lo = where_ref[1] > 0
    y_hi = where_ref[1] < where_ref[2] - 1
    return x_lo, x_hi, y_lo, y_hi


def masked(column, *conditions):
    keep = functools.reduce(jnp.logical_and, conditions)
    return jnp.where(keep, column.astype(F32), 0.0).astype(BF)


def first_conv_kernel(
    where_ref, grid_ref, xl_ref, xh_ref, yl_ref, yh_ref, weight_ref,
    act_ref, coarse_ref, low_ref, high_ref, stack,
):
    x_lo, x_hi, y_lo, y_hi = edges(where_ref)
    for x in range(TILE_X):
        for y in range(TILE_Y):
            stack[x + 1, y + 1] = shifted(grid_ref[x, y])
    for y in range(TILE_Y):
        stack[0, y + 1] = shifted(masked(xl_ref[y], x_lo))
        stack[TILE_X + 1, y + 1] = shifted(masked(xh_ref[y], x_hi))
    for x in range(TILE_X + 2):
        more = (x_lo,) if x == 0 else (x_hi,) if x == TILE_X + 1 else ()
        stack[x, 0] = shifted(masked(yl_ref[x], y_lo, *more))
        stack[x, TILE_Y + 1] = shifted(masked(yh_ref[x], y_hi, *more))

    def put(x, y, value):
        result = (silu(value) + grid_ref[x, y].astype(F32)).astype(BF)
        act_ref[x, y] = result
        if x == 0:
            low_ref[y] = result
        if x == TILE_X - 1:
            high_ref[y] = result

    conv_rows(stack, weight_ref, TILE_X, TILE_Y, put)
    for x in range(TILE_X // 2):
        for y in range(TILE_Y // 2):
            total = (
                act_ref[2 * x, 2 * y].astype(F32)
                + act_ref[2 * x, 2 * y + 1].astype(F32)
                + act_ref[2 * x + 1, 2 * y].astype(F32)
                + act_ref[2 * x + 1, 2 * y + 1].astype(F32)
            )
            result = (total * 0.25).astype(BF)
            coarse_ref[x, y] = result
            low_ref[TILE_Y + x * 4 + y] = result
            high_ref[TILE_Y + x * 4 + y] = result


def second_conv_kernel(
    where_ref, act_ref, coarse_ref, xl_ref, xh_ref, yl_ref, yh_ref, mid_weight_ref, out_weight_ref,
    field_ref, stack, merged, mid_ref, taps,
):
    x_lo, x_hi, y_lo, y_hi = edges(where_ref)
    half_x = TILE_X // 2
    half_y = TILE_Y // 2
    for x in range(half_x):
        for y in range(half_y):
            stack[x + 2, y + 2] = shifted(coarse_ref[x, y])
            stack[x, y + 2] = shifted(masked(xl_ref[TILE_Y + x * half_y + y], x_lo))
            stack[x + 2 + half_x, y + 2] = shifted(
                masked(xh_ref[TILE_Y + x * half_y + y], x_hi)
            )
    for x in range(half_x + 4):
        more = (x_lo,) if x < 2 else (x_hi,) if x >= half_x + 2 else ()
        for y in range(2):
            stack[x, y] = shifted(masked(yl_ref[TILE_X + 2 + x * 2 + y], y_lo, *more))
            stack[x, half_y + 2 + y] = shifted(
                masked(yh_ref[TILE_X + 2 + x * 2 + y], y_hi, *more)
            )

    def put(x, y, value):
        mid_ref[x, y] = silu(value).astype(BF)

    conv_rows(stack, mid_weight_ref, half_x + 2, half_y + 2, put)
    for x in range(TILE_X + 2):
        for y in range(TILE_Y + 2):
            more = ()
            if x == 0:
                more += (x_lo,)
            if x == TILE_X + 1:
                more += (x_hi,)
            if y == 0:
                fine = yl_ref[x]
                more += (y_lo,)
            elif y == TILE_Y + 1:
                fine = yh_ref[x]
                more += (y_hi,)
            elif x == 0:
                fine = xl_ref[y - 1]
            elif x == TILE_X + 1:
                fine = xh_ref[y - 1]
            else:
                fine = act_ref[x - 1, y - 1]
            value = fine.astype(F32) + mid_ref[(x + 1) // 2, (y + 1) // 2].astype(F32)
            if more:
                value = jnp.where(functools.reduce(jnp.logical_and, more), value, 0.0)
            merged[x, y] = value.astype(BF)
    weight = out_weight_ref[...]
    for x in range(TILE_X + 2):
        for y in range(0, TILE_Y + 2, 2):
            pair = jnp.concatenate([merged[x, y], merged[x, y + 1]], axis=1)
            prod = jnp.dot(weight, pair, preferred_element_type=F32)
            taps[x, y] = prod[:, :LANES]
            taps[x, y + 1] = prod[:, LANES:]
    lane = lax.broadcasted_iota(I32, (8, LANES), 1)
    for x in range(TILE_X):
        for y in range(TILE_Y):
            total = None
            for a in range(3):
                for b in range(3):
                    start = (a * 3 + b) * 24
                    piece = taps[x + a, y + b, start : start + 24, :]
                    total = piece if total is None else total + piece
            before = jnp.where(lane == 0, 0.0, pltpu.roll(total[0:8], 1, 1))
            after = jnp.where(lane == LANES - 1, 0.0, pltpu.roll(total[16:24], LANES - 1, 1))
            both = before + total[8:16] + after
            both = both[0:3] + both[3:6]
            for d in range(3):
                field_ref[d, x * TILE_Y + y : x * TILE_Y + y + 1, :] = both[d : d + 1]


def gather_kernel(
    where_ref, counts_ref, block_ref, dest_ref, own_ref, xl_ref, xh_ref, yl_ref, yh_ref,
    nodes_ref, weight_ref, out_ref, frame, total,
):
    entries = weight_ref.shape[0]
    blocks = out_ref.shape[0]
    frame[1] = yl_ref[0]
    frame[4] = yl_ref[1]
    frame[7] = yl_ref[2]
    frame[2] = xl_ref[...]
    frame[5] = own_ref[...]
    frame[8] = xh_ref[...]
    frame[3] = yh_ref[0]
    frame[6] = yh_ref[1]
    frame[9] = yh_ref[2]
    total[...] = jnp.zeros(total.shape, F32)
    sub = lax.broadcasted_iota(I32, (8, LANES), 0)
    for e in range(entries):
        tile = dest_ref[e]
        d = (tile // where_ref[2] - where_ref[0] + 1) * 3 + (tile % where_ref[2] - where_ref[1] + 1)
        node = jnp.broadcast_to(nodes_ref[e : e + 1, :], (8, LANES))
        z = node & (LANES - 1)
        column = node >> 7
        rows = []
        for c in range(3):
            picked = None
            for q in range(4):
                table = frame[d + 1, c, q * 8 : q * 8 + 8, :]
                value = jnp.take_along_axis(table, z, axis=1)
                value = jnp.where(column == sub + q * 8, value, 0.0)
                picked = value if picked is None else picked + value
            rows.append(picked)
        wide = jnp.concatenate(rows, axis=0)
        high = wide.astype(BF)
        low = (wide - high.astype(F32)).astype(BF)
        both = jnp.concatenate([high, low], axis=0)
        value = lax.dot_general(both, weight_ref[e], NT, preferred_element_type=F32)
        block = block_ref[e]
        total[block] += value[0:24] + value[24:48]
    lane = lax.broadcasted_iota(I32, (1, LANES), 1)
    for b in range(blocks):
        live = lane < counts_ref[b]
        for c in range(3):
            value = jnp.sum(total[b, c * 8 : c * 8 + 8, :], axis=0, keepdims=True)
            out_ref[b, c : c + 1, :] = jnp.where(live, value, 0.0)


def moved(value, step_x, step_y):
    size_x = lax.axis_size("gx")
    size_y = lax.axis_size("gy")
    pairs = [
        (x * size_y + y, (x + step_x) % size_x * size_y + (y + step_y) % size_y)
        for x in range(size_x)
        for y in range(size_y)
    ]
    return lax.ppermute(value, ("gx", "gy"), pairs)


def shards(
    particle_feat, block_counts, entry_block, entry_dest, entry_nodes, entry_weights,
    conv_in, conv_mid, conv_out, head_weight,
):
    size_x = lax.axis_size("gx")
    size_y = lax.axis_size("gy")
    where = jnp.stack(
        [
            lax.axis_index("gx").astype(I32),
            lax.axis_index("gy").astype(I32),
            jnp.int32(size_y),
            jnp.int32(size_x),
        ]
    )
    blocks = particle_feat.shape[0]
    entries = entry_weights.shape[0]
    dest = entry_dest.reshape(entries)
    in_weight = conv_in.reshape(3 * CHAN, 9 * CHAN)
    mid_weight = conv_mid.reshape(3 * CHAN, 9 * CHAN)
    folded = jnp.einsum(
        "do,aox->adx", head_weight, conv_out.astype(F32), precision=lax.Precision.HIGHEST
    )
    high = lax.reduce_precision(folded, 8, 7)
    both = jnp.concatenate([high, folded - high, jnp.zeros((3, 2, 9 * CHAN), F32)], axis=1)
    out_weight = (
        both.reshape(3, 8, 9, CHAN).transpose(0, 2, 1, 3).reshape(27 * 8, CHAN).astype(BF)
    )

    packed = (SLOTS + 1, CHAN, LANES)
    sent = call(
        partial_kernel,
        [(packed, BF)] * 9,
        [SM] * 4 + [VM] * 3,
        [
            pltpu.VMEM((entries, CHAN, LANES), BF),
            pltpu.VMEM((entries, LANES), F32),
            pltpu.VMEM((entries, LANES), F32),
            pltpu.VMEM((9 * 16, LANES), F32),
            pltpu.SMEM((9,), I32),
            pltpu.SMEM((9 * SLOTS,), I32),
        ],
        70000000,
    )(where, block_counts, entry_block, dest, particle_feat, entry_nodes, entry_weights)
    got = [None] * 9
    got[4] = sent[4]
    for d in (7, 1, 5, 3, 8, 0, 6, 2):
        got[d] = moved(sent[d], d // 3 - 1, d % 3 - 1)
    most = 9 * SLOTS + GROUP
    grid, grid_low, grid_high = call(
        scatter_kernel,
        [((TILE_X, TILE_Y, CHAN, LANES), BF)] + [((TILE_Y, CHAN, LANES), BF)] * 2,
        [VM] * 9,
        [
            pltpu.VMEM((most, CHAN, LANES), BF),
            pltpu.VMEM((9 * 16, LANES), F32),
            pltpu.VMEM((most, LANES), F32),
            pltpu.VMEM((most, LANES), F32),
            pltpu.VMEM((16 * CHAN, 256), F32),
        ],
        2400000000,
    )(*got)

    xl = moved(grid_high, 1, 0)
    xh = moved(grid_low, -1, 0)
    yl = moved(jnp.concatenate([xl[-1:], grid[:, -1], xh[-1:]], axis=0), 0, 1)
    yh = moved(jnp.concatenate([xl[:1], grid[:, 0], xh[:1]], axis=0), 0, -1)
    act, coarse, act_low, act_high = call(
        first_conv_kernel,
        [
            ((TILE_X, TILE_Y, CHAN, LANES), BF),
            ((TILE_X // 2, TILE_Y // 2, CHAN, LANES), BF),
            ((2 * TILE_Y, CHAN, LANES), BF),
            ((2 * TILE_Y, CHAN, LANES), BF),
        ],
        [SM] + [VM] * 6,
        [pltpu.VMEM((TILE_X + 2, TILE_Y + 2, 3 * CHAN, LANES), BF)],
        1300000000,
    )(where, grid, xl, xh, yl, yh, in_weight)

    xl = moved(act_high, 1, 0)
    xh = moved(act_low, -1, 0)
    cxl = xl[TILE_Y:].reshape(2, 4, CHAN, LANES)
    cxh = xh[TILE_Y:].reshape(2, 4, CHAN, LANES)
    yl = moved(
        jnp.concatenate(
            [
                xl[TILE_Y - 1 : TILE_Y],
                act[:, -1],
                xh[TILE_Y - 1 : TILE_Y],
                jnp.concatenate([cxl[:, 2:], coarse[:, 2:], cxh[:, 2:]], axis=0).reshape(
                    12, CHAN, LANES
                ),
            ],
            axis=0,
        ),
        0,
        1,
    )
    yh = moved(
        jnp.concatenate(
            [
                xl[:1],
                act[:, 0],
                xh[:1],
                jnp.concatenate([cxl[:, :2], coarse[:, :2], cxh[:, :2]], axis=0).reshape(
                    12, CHAN, LANES
                ),
            ],
            axis=0,
        ),
        0,
        -1,
    )
    field = call(
        second_conv_kernel,
        [((3, TILE_X * TILE_Y, LANES), F32)],
        [SM] + [VM] * 8,
        [
            pltpu.VMEM((6, 8, 3 * CHAN, LANES), BF),
            pltpu.VMEM((TILE_X + 2, TILE_Y + 2, CHAN, LANES), BF),
            pltpu.VMEM((4, 6, CHAN, LANES), BF),
            pltpu.VMEM((TILE_X + 2, TILE_Y + 2, 27 * 8, LANES), F32),
        ],
        1300000000,
    )(where, act, coarse, xl, xh, yl, yh, mid_weight, out_weight)[0]

    xl = moved(field, 1, 0)
    xh = moved(field, -1, 0)
    row = jnp.stack([xl, field, xh], axis=0)
    yl = moved(row, 0, 1)
    yh = moved(row, 0, -1)
    return call(
        gather_kernel,
        [((blocks, 3, LANES), F32)],
        [SM] * 4 + [VM] * 7,
        [
            pltpu.VMEM((10, 3, TILE_X * TILE_Y, LANES), F32),
            pltpu.VMEM((blocks, 24, LANES), F32),
        ],
        70000000,
    )(
        where, block_counts, entry_block, dest, field, xl, xh, yl, yh, entry_nodes, entry_weights
    )[0]


def solution(mesh):
    in_specs = (
        P(("gx", "gy"), None, None),
        P(("gx", "gy")),
        P(("gx", "gy")),
        P(("gx", "gy"), None),
        P(("gx", "gy"), None),
        P(("gx", "gy"), None, None),
        P(),
        P(),
        P(),
        P(),
    )
    out_specs = P(("gx", "gy"), None, None)
    return jax.shard_map(shards, mesh=mesh, in_specs=in_specs, out_specs=out_specs, check_vma=False)
```

profile of v0, /device:TPU:7, one launch (start us, length us, event | category | flops | bytes accessed | tf_op | source)
XLA Modules:
  0.0 94.7 jit_solution(17050289461228149673)
XLA Ops:
  0.0 0.1 pad_add_fusion.where_ref
  0.1 0.7 copy-done.4
  0.8 1.2 %copy-done.1 = bf16[32,128,128]{2,1,0:T(8,128)(2,1)S(1)} copy-done((bf16[32,128,128]{2,1,0:T(8,128)(2,1)S(1)}, bf16[32,128,128]{2,1,0:T(8,128)(2,1)}, u32[]{:S(2)}) %copy-start.1) | copy-done | bytes 1048600
  2.0 0.9 %copy-done.3 = bf16[16,64,128]{2,1,0:T(8,128)(2,1)S(1)} copy-done((bf16[16,64,128]{2,1,0:T(8,128)(2,1)S(1)}, bf16[16,64,128]{2,1,0:T(8,128)(2,1)}, u32[]{:S(2)}) %copy-start.3) | copy-done | bytes 262168
  2.9 2.3 %shard_map.100 = (bf16[9,64,128]{2,1,0:T(8,128)(2,1)S(1)}, bf16[9,64,128]{2,1,0:T(8,128)(2,1)S(1)}, bf16[9,64,128]{2,1,0:T(8,128)(2,1)S(1)}, bf16[9,64,128]{2,1,...) custom-call(s32[4]{0:T(128)S(1)} %pad_add_fusion.where_ref, ...), custom_call_target="tpu_custom_call" | custom-call | flops 70000000 | bytes 2000000 | tf_op jit(solution)/shard_map/pallas_call | solution.py:385
  5.3 6.8 %collective-permute-start = (bf16[9,64,128]{2,1,0:T(8,128)(2,1)S(1)}, bf16[9,64,128]{2,1,0:T(8,128)(2,1)S(1)}, u32[]{:S(2)}, u32[]{:S(2)}) collective-permute-start(bf16[9,64,128]{2,1,0:T(8,128)(2,1)S(1)} %get-tuple-element.21), channel_id=1, source_target_pairs={{0,127},{1,120},{2,121},{3,122},{4,123},{5,124},{6,125},{7,126},{8... | collective-permute-start | bytes 442376 | tf_op jit(solution)/shard_map/ppermute | solution.py:353
  12.1 0.1 collective-permute-start.1
  12.2 1.9 %collective-permute-start.2 = (bf16[9,64,128]{2,1,0:T(8,128)(2,1)S(1)}, bf16[9,64,128]{2,1,0:T(8,128)(2,1)S(1)}, u32[]{:S(2)}, u32[]{:S(2)}) collective-permute-start(bf16[9,64,128]{2,1,0:T(8,128)(2,1)S(1)} %get-tuple-element.23), channel_id=1, source_target_pairs={{0,121},{1,122},{2,123},{3,124},{4,125},{5,126},{6,127},{7,120},{8... | collective-permute-start | bytes 442376 | tf_op jit(solution)/shard_map/ppermute | solution.py:353
  14.2 3.0 %collective-permute-start.4 = (bf16[9,64,128]{2,1,0:T(8,128)(2,1)S(1)}, bf16[9,64,128]{2,1,0:T(8,128)(2,1)S(1)}, u32[]{:S(2)}, u32[]{:S(2)}) collective-permute-start(bf16[9,64,128]{2,1,0:T(8,128)(2,1)S(1)} %get-tuple-element.26), channel_id=1, source_target_pairs={{0,1},{1,2},{2,3},{3,4},{4,5},{5,6},{6,7},{7,0},{8,9},{9,10},{10,1... | collective-permute-start | bytes 442376 | tf_op jit(solution)/shard_map/ppermute | solution.py:353
  17.1 1.0 %collective-permute-done.refs_0_ = bf16[9,64,128]{2,1,0:T(8,128)(2,1)S(1)} collective-permute-done((bf16[9,64,128]{2,1,0:T(8,128)(2,1)S(1)}, bf16[9,64,128]{2,1,0:T(8,128)(2,1)S(1)}, u32[]{:S(2)}, u32[]{:S(2)}) %collective-permute-start) | collective-permute-done | bytes 147488 | tf_op jit(solution)/shard_map/ppermute | solution.py:353
  18.1 0.0 collective-permute-start.5
  18.1 3.3 %collective-permute-done.1.refs_1_ = bf16[9,64,128]{2,1,0:T(8,128)(2,1)S(1)} collective-permute-done((bf16[9,64,128]{2,1,0:T(8,128)(2,1)S(1)}, bf16[9,64,128]{2,1,0:T(8,128)(2,1)S(1)}, u32[]{:S(2)}, u32[]{:S(2)}) %collective-permute-start.1) | collective-permute-done | bytes 147488 | tf_op jit(solution)/shard_map/ppermute | solution.py:353
  21.5 1.1 %collective-permute-start.7 = (bf16[9,64,128]{2,1,0:T(8,128)(2,1)S(1)}, bf16[9,64,128]{2,1,0:T(8,128)(2,1)S(1)}, u32[]{:S(2)}, u32[]{:S(2)}) collective-permute-start(bf16[9,64,128]{2,1,0:T(8,128)(2,1)S(1)} %get-tuple-element.29), channel_id=1, source_target_pairs={{0,9},{1,10},{2,11},{3,12},{4,13},{5,14},{6,15},{7,8},{8,17},{9,18... | collective-permute-start | bytes 442376 | tf_op jit(solution)/shard_map/ppermute | solution.py:353
  22.6 5.7 %collective-permute-done.5.refs_6_ = bf16[9,64,128]{2,1,0:T(8,128)(2,1)S(1)} collective-permute-done((bf16[9,64,128]{2,1,0:T(8,128)(2,1)S(1)}, bf16[9,64,128]{2,1,0:T(8,128)(2,1)S(1)}, u32[]{:S(2)}, u32[]{:S(2)}) %collective-permute-start.5) | collective-permute-done | bytes 147488 | tf_op jit(solution)/shard_map/ppermute | solution.py:353
  28.2 4.8 %collective-permute-done.6.refs_7_ = bf16[9,64,128]{2,1,0:T(8,128)(2,1)S(1)} collective-permute-done((bf16[9,64,128]{2,1,0:T(8,128)(2,1)S(1)}, bf16[9,64,128]{2,1,0:T(8,128)(2,1)S(1)}, u32[]{:S(2)}, u32[]{:S(2)}) %collective-permute-start.6) | collective-permute-done | bytes 147488 | tf_op jit(solution)/shard_map/ppermute | solution.py:353
  33.1 1.4 %collective-permute-done.7.refs_8_ = bf16[9,64,128]{2,1,0:T(8,128)(2,1)S(1)} collective-permute-done((bf16[9,64,128]{2,1,0:T(8,128)(2,1)S(1)}, bf16[9,64,128]{2,1,0:T(8,128)(2,1)S(1)}, u32[]{:S(2)}, u32[]{:S(2)}) %collective-permute-start.7) | collective-permute-done | bytes 147488 | tf_op jit(solution)/shard_map/ppermute | solution.py:353
  34.5 3.2 %shard_map.101 = (bf16[4,8,64,128]{3,2,1,0:T(8,128)(2,1)S(1)}, bf16[8,64,128]{2,1,0:T(8,128)(2,1)S(1)}, bf16[8,64,128]{2,1,0:T(8,128)(2,1)S(1)}) custom-call(bf16[9,64,128]{2,1,0:T(8,128)(2,1)S(1)} %collective-permute-done.refs_0_, bf16[9,64,128]{2,1,0:T(8,128)(2,1)S(1)} %collective-permute-done.1.refs_1_, ...), custom_call_target="tpu_custom_call" | custom-call | flops 2400000000 | bytes 2000000 | tf_op jit(solution)/shard_map/pallas_call | solution.py:404
  37.7 0.1 collective-permute-start.8
  37.8 4.8 %collective-permute-start.9 = (bf16[8,64,128]{2,1,0:T(8,128)(2,1)S(1)}, bf16[8,64,128]{2,1,0:T(8,128)(2,1)S(1)}, u32[]{:S(2)}, u32[]{:S(2)}) collective-permute-start(bf16[8,64,128]{2,1,0:T(8,128)(2,1)S(1)} %get-tuple-element.32), channel_id=1, source_target_pairs={{0,120},{1,121},{2,122},{3,123},{4,124},{5,125},{6,126},{7,127},{8... | collective-permute-start | bytes 393224 | tf_op jit(solution)/shard_map/ppermute | solution.py:353
  42.6 3.6 %collective-permute-done.8.xl_ref = bf16[8,64,128]{2,1,0:T(8,128)(2,1)S(1)} collective-permute-done((bf16[8,64,128]{2,1,0:T(8,128)(2,1)S(1)}, bf16[8,64,128]{2,1,0:T(8,128)(2,1)S(1)}, u32[]{:S(2)}, u32[]{:S(2)}) %collective-permute-start.8) | collective-permute-done | bytes 131104 | tf_op jit(solution)/shard_map/ppermute | solution.py:353
  46.3 0.8 collective-permute-start.11
  47.1 2.2 %collective-permute-start.10 = (bf16[6,64,128]{2,1,0:T(8,128)(2,1)S(1)}, bf16[6,64,128]{2,1,0:T(8,128)(2,1)S(1)}, u32[]{:S(2)}, u32[]{:S(2)}) collective-permute-start(bf16[6,64,128]{2,1,0:T(8,128)(2,1)S(1)} %pad_maximum_fusion.5), channel_id=1, source_target_pairs={{0,1},{1,2},{2,3},{3,4},{4,5},{5,6},{6,7},{7,0},{8,9},{9,10},{10,1... | collective-permute-start | bytes 294920 | tf_op jit(solution)/shard_map/ppermute | solution.py:353
  49.3 2.3 %collective-permute-done.11.yh_ref = bf16[6,64,128]{2,1,0:T(8,128)(2,1)S(1)} collective-permute-done((bf16[6,64,128]{2,1,0:T(8,128)(2,1)S(1)}, bf16[6,64,128]{2,1,0:T(8,128)(2,1)S(1)}, u32[]{:S(2)}, u32[]{:S(2)}) %collective-permute-start.11) | collective-permute-done | bytes 98336 | tf_op jit(solution)/shard_map/ppermute | solution.py:353
  51.5 2.4 %shard_map.102 = (bf16[4,8,64,128]{3,2,1,0:T(8,128)(2,1)S(1)}, bf16[2,4,64,128]{3,2,1,0:T(8,128)(2,1)S(1)}, bf16[16,64,128]{2,1,0:T(8,128)(2,1)S(1)}, bf16[16,64,128]{2,1,0:T(8,128)(2,1)S(1)}) custom-call(s32[4]{0:T(128)S(1)} %pad_add_fusion.where_ref, bf16[4,8,64,128]{3,2,1,0:T(8,128)(2,1)S(1)} %get-tuple-element.30.grid_ref, ...), custom_call_target="tpu_custom_call" | custom-call | flops 1300000000 | bytes 2000000 | tf_op jit(solution)/shard_map/pallas_call | solution.py:422
  54.0 0.1 collective-permute-start.12
  54.0 4.8 %collective-permute-start.13 = (bf16[16,64,128]{2,1,0:T(8,128)(2,1)S(1)}, bf16[16,64,128]{2,1,0:T(8,128)(2,1)S(1)}, u32[]{:S(2)}, u32[]{:S(2)}) collective-permute-start(bf16[16,64,128]{2,1,0:T(8,128)(2,1)S(1)} %get-tuple-element.36), channel_id=1, source_target_pairs={{0,120},{1,121},{2,122},{3,123},{4,124},{5,125},{6,126},{7,127},{8... | collective-permute-start | bytes 786440 | tf_op jit(solution)/shard_map/ppermute | solution.py:353
  58.9 6.7 %collective-permute-done.12.xl_ref = bf16[16,64,128]{2,1,0:T(8,128)(2,1)S(1)} collective-permute-done((bf16[16,64,128]{2,1,0:T(8,128)(2,1)S(1)}, bf16[16,64,128]{2,1,0:T(8,128)(2,1)S(1)}, u32[]{:S(2)}, u32[]{:S(2)}) %collective-permute-start.12) | collective-permute-done | bytes 262176 | tf_op jit(solution)/shard_map/ppermute | solution.py:353
  65.6 0.0 collective-permute-done.13.xh_ref
  65.8 0.5 collective-permute-start.15
  66.3 2.5 %collective-permute-start.14 = (bf16[18,64,128]{2,1,0:T(8,128)(2,1)S(1)}, bf16[18,64,128]{2,1,0:T(8,128)(2,1)S(1)}, u32[]{:S(2)}, u32[]{:S(2)}) collective-permute-start(bf16[18,64,128]{2,1,0:T(8,128)(2,1)S(1)} %pad_maximum_fusion), channel_id=1, source_target_pairs={{0,1},{1,2},{2,3},{3,4},{4,5},{5,6},{6,7},{7,0},{8,9},{9,10},{10,1... | collective-permute-start | bytes 884744 | tf_op jit(solution)/shard_map/ppermute | solution.py:353
  68.8 0.2 reduce-precision_convert_fusion
  69.0 0.0 copy-start.9
  69.1 0.1 pad.5.clone
  69.1 0.1 maximum_maximum_fusion
  69.2 0.1 convert_element_type.8
  69.3 3.8 %collective-permute-done.15.yh_ref = bf16[18,64,128]{2,1,0:T(8,128)(2,1)S(1)} collective-permute-done((bf16[18,64,128]{2,1,0:T(8,128)(2,1)S(1)}, bf16[18,64,128]{2,1,0:T(8,128)(2,1)S(1)}, u32[]{:S(2)}, u32[]{:S(2)}) %collective-permute-start.15) | collective-permute-done | bytes 294944 | tf_op jit(solution)/shard_map/ppermute | solution.py:353
  73.2 0.0 collective-permute-done.14.yl_ref
  73.2 3.2 %shard_map.103.own_ref = f32[3,32,128]{2,1,0:T(8,128)S(1)} custom-call(s32[4]{0:T(128)S(1)} %pad_add_fusion.where_ref, bf16[4,8,64,128]{3,2,1,0:T(8,128)(2,1)S(1)} %get-tuple-element.33.act_ref, bf16[2,4,64,128]{3,2,1,0:T(8,128)(2,1)S(1)} %get-tuple-element.34.coarse_ref, bf16[16,64,128]{2,1,0:T(8,128)(2,1)S(1)} %collective-permute-done.12.xl_ref, ...), custom_call_target="tpu_custom_call" | custom-call | flops 1300000000 | bytes 2000000 | tf_op jit(solution)/shard_map/pallas_call | solution.py:469
  76.4 0.1 collective-permute-start.16
  76.4 4.8 %collective-permute-start.17 = (f32[3,32,128]{2,1,0:T(8,128)S(1)}, f32[3,32,128]{2,1,0:T(8,128)S(1)}, u32[]{:S(2)}, u32[]{:S(2)}) collective-permute-start(f32[3,32,128]{2,1,0:T(8,128)S(1)} %shard_map.103.own_ref), channel_id=1, source_target_pairs={{0,120},{1,121},{2,122},{3,123},{4,124},{5,125},{6,126},{7,127},{8... | collective-permute-start | bytes 147464 | tf_op jit(solution)/shard_map/ppermute | solution.py:353
  81.2 1.9 %collective-permute-done.16.xl_ref = f32[3,32,128]{2,1,0:T(8,128)S(1)} collective-permute-done((f32[3,32,128]{2,1,0:T(8,128)S(1)}, f32[3,32,128]{2,1,0:T(8,128)S(1)}, u32[]{:S(2)}, u32[]{:S(2)}) %collective-permute-start.16) | collective-permute-done | bytes 49184 | tf_op jit(solution)/shard_map/ppermute | solution.py:353
  83.1 0.0 collective-permute-done.17.xh_ref
  83.1 3.7 %collective-permute-start.18 = (f32[3,3,32,128]{3,2,1,0:T(8,128)S(1)}, f32[3,3,32,128]{3,2,1,0:T(8,128)S(1)}, u32[]{:S(2)}, u32[]{:S(2)}) collective-permute-start(f32[3,3,32,128]{3,2,1,0:T(8,128)S(1)} %pad_maximum_fusion.4), channel_id=1, source_target_pairs={{0,1},{1,2},{2,3},{3,4},{4,5},{5,6},{6,7},{7,0},{8,9},{9,10},{10,1... | collective-permute-start | bytes 442376 | tf_op jit(solution)/shard_map/ppermute | solution.py:353
  86.8 0.0 collective-permute-start.19
  86.8 2.1 %collective-permute-done.18.yl_ref = f32[3,3,32,128]{3,2,1,0:T(8,128)S(1)} collective-permute-done((f32[3,3,32,128]{3,2,1,0:T(8,128)S(1)}, f32[3,3,32,128]{3,2,1,0:T(8,128)S(1)}, u32[]{:S(2)}, u32[]{:S(2)}) %collective-permute-start.18) | collective-permute-done | bytes 147488 | tf_op jit(solution)/shard_map/ppermute | solution.py:353
  88.9 3.7 %collective-permute-done.19.yh_ref = f32[3,3,32,128]{3,2,1,0:T(8,128)S(1)} collective-permute-done((f32[3,3,32,128]{3,2,1,0:T(8,128)S(1)}, f32[3,3,32,128]{3,2,1,0:T(8,128)S(1)}, u32[]{:S(2)}, u32[]{:S(2)}) %collective-permute-start.19) | collective-permute-done | bytes 147488 | tf_op jit(solution)/shard_map/ppermute | solution.py:353
  92.6 1.4 %shard_map.104 = f32[16,3,128]{2,1,0:T(4,128)S(1)} custom-call(s32[4]{0:T(128)S(1)} %pad_add_fusion.where_ref, s32[16]{0:T(128)S(1)} %copy-done.5, s32[32]{0:T(128)S(1)} %copy-done.6, s32[32]{0:T(128)S(1)} %bitcast.35, f32[3,32,128]{2,1,0:T(8,128)S(1)} %shard_map.103.own_ref, f32[3,32,128]{2,1,0:T(8,128)S(1)} %collective-permute-done.16.xl_ref, ...), custom_call_target="tpu_custom_call" | custom-call | flops 70000000 | bytes 2000000 | tf_op jit(solution)/shard_map/pallas_call | solution.py:487
  94.0 0.6 copy.22
  (44 shorter events, 0.3 us)
Async XLA Ops:
  0.0 68.8 %copy-start = (bf16[3,64,576]{2,1,0:T(8,128)(2,1)S(1)}, bf16[3,64,576]{2,1,0:T(8,128)(2,1)}, u32[]{:S(2)}) copy-start(bf16[3,64,576]{2,1,0:T(8,128)(2,1)} %param.18) | copy-start | bytes 663556
  0.0 0.8 copy-start.4
  0.1 0.7 copy-start.5
  0.1 0.7 copy-start.6
  0.1 0.7 copy-start.7
  0.8 1.2 %copy-start.1 = (bf16[32,128,128]{2,1,0:T(8,128)(2,1)S(1)}, bf16[32,128,128]{2,1,0:T(8,128)(2,1)}, u32[]{:S(2)}) copy-start(bf16[32,128,128]{2,1,0:T(8,128)(2,1)} %weight_ref.3) | copy-start | bytes 3145732
  2.0 0.9 %copy-start.3 = (bf16[16,64,128]{2,1,0:T(8,128)(2,1)S(1)}, bf16[16,64,128]{2,1,0:T(8,128)(2,1)}, u32[]{:S(2)}) copy-start(bf16[16,64,128]{2,1,0:T(8,128)(2,1)} %feat_ref.1) | copy-start | bytes 786436
  5.3 12.9 %collective-permute-start = (bf16[9,64,128]{2,1,0:T(8,128)(2,1)S(1)}, bf16[9,64,128]{2,1,0:T(8,128)(2,1)S(1)}, u32[]{:S(2)}, u32[]{:S(2)}) collective-permute-start(bf16[9,64,128]{2,1,0:T(8,128)(2,1)S(1)} %get-tuple-element.21), channel_id=1, source_target_pairs={{0,127},{1,120},{2,121},{3,122},{4,123},{5,124},{6,125},{7,126},{8... | collective-permute-start | bytes 442376 | tf_op jit(solution)/shard_map/ppermute | solution.py:353
  12.1 9.4 %collective-permute-start.1 = (bf16[9,64,128]{2,1,0:T(8,128)(2,1)S(1)}, bf16[9,64,128]{2,1,0:T(8,128)(2,1)S(1)}, u32[]{:S(2)}, u32[]{:S(2)}) collective-permute-start(bf16[9,64,128]{2,1,0:T(8,128)(2,1)S(1)} %get-tuple-element.22), channel_id=1, source_target_pairs={{0,120},{1,121},{2,122},{3,123},{4,124},{5,125},{6,126},{7,127},{8... | collective-permute-start | bytes 442376 | tf_op jit(solution)/shard_map/ppermute | solution.py:353
  12.2 9.2 %collective-permute-start.2 = (bf16[9,64,128]{2,1,0:T(8,128)(2,1)S(1)}, bf16[9,64,128]{2,1,0:T(8,128)(2,1)S(1)}, u32[]{:S(2)}, u32[]{:S(2)}) collective-permute-start(bf16[9,64,128]{2,1,0:T(8,128)(2,1)S(1)} %get-tuple-element.23), channel_id=1, source_target_pairs={{0,121},{1,122},{2,123},{3,124},{4,125},{5,126},{6,127},{7,120},{8... | collective-permute-start | bytes 442376 | tf_op jit(solution)/shard_map/ppermute | solution.py:353
  14.2 8.4 %collective-permute-start.3 = (bf16[9,64,128]{2,1,0:T(8,128)(2,1)S(1)}, bf16[9,64,128]{2,1,0:T(8,128)(2,1)S(1)}, u32[]{:S(2)}, u32[]{:S(2)}) collective-permute-start(bf16[9,64,128]{2,1,0:T(8,128)(2,1)S(1)} %get-tuple-element.24), channel_id=1, source_target_pairs={{0,7},{1,0},{2,1},{3,2},{4,3},{5,4},{6,5},{7,6},{8,15},{9,8},{10,9... | collective-permute-start | bytes 442376 | tf_op jit(solution)/shard_map/ppermute | solution.py:353
  14.2 8.4 %collective-permute-start.4 = (bf16[9,64,128]{2,1,0:T(8,128)(2,1)S(1)}, bf16[9,64,128]{2,1,0:T(8,128)(2,1)S(1)}, u32[]{:S(2)}, u32[]{:S(2)}) collective-permute-start(bf16[9,64,128]{2,1,0:T(8,128)(2,1)S(1)} %get-tuple-element.26), channel_id=1, source_target_pairs={{0,1},{1,2},{2,3},{3,4},{4,5},{5,6},{6,7},{7,0},{8,9},{9,10},{10,1... | collective-permute-start | bytes 442376 | tf_op jit(solution)/shard_map/ppermute | solution.py:353
  18.1 10.1 %collective-permute-start.5 = (bf16[9,64,128]{2,1,0:T(8,128)(2,1)S(1)}, bf16[9,64,128]{2,1,0:T(8,128)(2,1)S(1)}, u32[]{:S(2)}, u32[]{:S(2)}) collective-permute-start(bf16[9,64,128]{2,1,0:T(8,128)(2,1)S(1)} %get-tuple-element.27), channel_id=1, source_target_pairs={{0,15},{1,8},{2,9},{3,10},{4,11},{5,12},{6,13},{7,14},{8,23},{9,16... | collective-permute-start | bytes 442376 | tf_op jit(solution)/shard_map/ppermute | solution.py:353
  21.4 11.6 %collective-permute-start.6 = (bf16[9,64,128]{2,1,0:T(8,128)(2,1)S(1)}, bf16[9,64,128]{2,1,0:T(8,128)(2,1)S(1)}, u32[]{:S(2)}, u32[]{:S(2)}) collective-permute-start(bf16[9,64,128]{2,1,0:T(8,128)(2,1)S(1)} %get-tuple-element.28), channel_id=1, source_target_pairs={{0,8},{1,9},{2,10},{3,11},{4,12},{5,13},{6,14},{7,15},{8,16},{9,17... | collective-permute-start | bytes 442376 | tf_op jit(solution)/shard_map/ppermute | solution.py:353
  21.5 13.0 %collective-permute-start.7 = (bf16[9,64,128]{2,1,0:T(8,128)(2,1)S(1)}, bf16[9,64,128]{2,1,0:T(8,128)(2,1)S(1)}, u32[]{:S(2)}, u32[]{:S(2)}) collective-permute-start(bf16[9,64,128]{2,1,0:T(8,128)(2,1)S(1)} %get-tuple-element.29), channel_id=1, source_target_pairs={{0,9},{1,10},{2,11},{3,12},{4,13},{5,14},{6,15},{7,8},{8,17},{9,18... | collective-permute-start | bytes 442376 | tf_op jit(solution)/shard_map/ppermute | solution.py:353
  37.7 8.5 %collective-permute-start.8 = (bf16[8,64,128]{2,1,0:T(8,128)(2,1)S(1)}, bf16[8,64,128]{2,1,0:T(8,128)(2,1)S(1)}, u32[]{:S(2)}, u32[]{:S(2)}) collective-permute-start(bf16[8,64,128]{2,1,0:T(8,128)(2,1)S(1)} %get-tuple-element.31), channel_id=1, source_target_pairs={{0,8},{1,9},{2,10},{3,11},{4,12},{5,13},{6,14},{7,15},{8,16},{9,17... | collective-permute-start | bytes 393224 | tf_op jit(solution)/shard_map/ppermute | solution.py:353
  37.8 8.4 %collective-permute-start.9 = (bf16[8,64,128]{2,1,0:T(8,128)(2,1)S(1)}, bf16[8,64,128]{2,1,0:T(8,128)(2,1)S(1)}, u32[]{:S(2)}, u32[]{:S(2)}) collective-permute-start(bf16[8,64,128]{2,1,0:T(8,128)(2,1)S(1)} %get-tuple-element.32), channel_id=1, source_target_pairs={{0,120},{1,121},{2,122},{3,123},{4,124},{5,125},{6,126},{7,127},{8... | collective-permute-start | bytes 393224 | tf_op jit(solution)/shard_map/ppermute | solution.py:353
  46.2 5.3 %copy-start.8 = (bf16[3,64,576]{2,1,0:T(8,128)(2,1)S(1)}, bf16[3,64,576]{2,1,0:T(8,128)(2,1)}, u32[]{:S(2)}) copy-start(bf16[3,64,576]{2,1,0:T(8,128)(2,1)} %param.16) | copy-start | bytes 663556
  46.3 5.3 %collective-permute-start.11 = (bf16[6,64,128]{2,1,0:T(8,128)(2,1)S(1)}, bf16[6,64,128]{2,1,0:T(8,128)(2,1)S(1)}, u32[]{:S(2)}, u32[]{:S(2)}) collective-permute-start(bf16[6,64,128]{2,1,0:T(8,128)(2,1)S(1)} %pad_maximum_fusion.6), channel_id=1, source_target_pairs={{0,7},{1,0},{2,1},{3,2},{4,3},{5,4},{6,5},{7,6},{8,15},{9,8},{10,9... | collective-permute-start | bytes 294920 | tf_op jit(solution)/shard_map/ppermute | solution.py:353
  47.1 4.4 %collective-permute-start.10 = (bf16[6,64,128]{2,1,0:T(8,128)(2,1)S(1)}, bf16[6,64,128]{2,1,0:T(8,128)(2,1)S(1)}, u32[]{:S(2)}, u32[]{:S(2)}) collective-permute-start(bf16[6,64,128]{2,1,0:T(8,128)(2,1)S(1)} %pad_maximum_fusion.5), channel_id=1, source_target_pairs={{0,1},{1,2},{2,3},{3,4},{4,5},{5,6},{6,7},{7,0},{8,9},{9,10},{10,1... | collective-permute-start | bytes 294920 | tf_op jit(solution)/shard_map/ppermute | solution.py:353
  54.0 11.6 %collective-permute-start.12 = (bf16[16,64,128]{2,1,0:T(8,128)(2,1)S(1)}, bf16[16,64,128]{2,1,0:T(8,128)(2,1)S(1)}, u32[]{:S(2)}, u32[]{:S(2)}) collective-permute-start(bf16[16,64,128]{2,1,0:T(8,128)(2,1)S(1)} %get-tuple-element.35), channel_id=1, source_target_pairs={{0,8},{1,9},{2,10},{3,11},{4,12},{5,13},{6,14},{7,15},{8,16},{9,17... | collective-permute-start | bytes 786440 | tf_op jit(solution)/shard_map/ppermute | solution.py:353
  54.0 11.6 %collective-permute-start.13 = (bf16[16,64,128]{2,1,0:T(8,128)(2,1)S(1)}, bf16[16,64,128]{2,1,0:T(8,128)(2,1)S(1)}, u32[]{:S(2)}, u32[]{:S(2)}) collective-permute-start(bf16[16,64,128]{2,1,0:T(8,128)(2,1)S(1)} %get-tuple-element.36), channel_id=1, source_target_pairs={{0,120},{1,121},{2,122},{3,123},{4,124},{5,125},{6,126},{7,127},{8... | collective-permute-start | bytes 786440 | tf_op jit(solution)/shard_map/ppermute | solution.py:353
  65.8 7.4 %collective-permute-start.15 = (bf16[18,64,128]{2,1,0:T(8,128)(2,1)S(1)}, bf16[18,64,128]{2,1,0:T(8,128)(2,1)S(1)}, u32[]{:S(2)}, u32[]{:S(2)}) collective-permute-start(bf16[18,64,128]{2,1,0:T(8,128)(2,1)S(1)} %pad_maximum_fusion.1), channel_id=1, source_target_pairs={{0,7},{1,0},{2,1},{3,2},{4,3},{5,4},{6,5},{7,6},{8,15},{9,8},{10,9... | collective-permute-start | bytes 884744 | tf_op jit(solution)/shard_map/ppermute | solution.py:353
  66.3 2.5 %copy-start.10 = (f32[3,64]{1,0:T(4,128)S(1)}, f32[3,64]{1,0:T(4,128)}, u32[]{:S(2)}) copy-start(f32[3,64]{1,0:T(4,128)} %param.19) | copy-start | bytes 2308
  66.3 6.8 %collective-permute-start.14 = (bf16[18,64,128]{2,1,0:T(8,128)(2,1)S(1)}, bf16[18,64,128]{2,1,0:T(8,128)(2,1)S(1)}, u32[]{:S(2)}, u32[]{:S(2)}) collective-permute-start(bf16[18,64,128]{2,1,0:T(8,128)(2,1)S(1)} %pad_maximum_fusion), channel_id=1, source_target_pairs={{0,1},{1,2},{2,3},{3,4},{4,5},{5,6},{6,7},{7,0},{8,9},{9,10},{10,1... | collective-permute-start | bytes 884744 | tf_op jit(solution)/shard_map/ppermute | solution.py:353
  69.0 4.1 %copy-start.9 = (bf16[3,64,576]{2,1,0:T(8,128)(2,1)S(1)}, bf16[3,64,576]{2,1,0:T(8,128)(2,1)}, u32[]{:S(2)}) copy-start(bf16[3,64,576]{2,1,0:T(8,128)(2,1)} %param.17) | copy-start | bytes 663556
  73.2 19.5 %copy-start.2 = (bf16[32,128,128]{2,1,0:T(8,128)(2,1)S(1)}, bf16[32,128,128]{2,1,0:T(8,128)(2,1)}, u32[]{:S(2)}) copy-start(bf16[32,128,128]{2,1,0:T(8,128)(2,1)} %weight_ref.3) | copy-start | bytes 3145732
  76.4 6.7 %collective-permute-start.16 = (f32[3,32,128]{2,1,0:T(8,128)S(1)}, f32[3,32,128]{2,1,0:T(8,128)S(1)}, u32[]{:S(2)}, u32[]{:S(2)}) collective-permute-start(f32[3,32,128]{2,1,0:T(8,128)S(1)} %shard_map.103.own_ref), channel_id=1, source_target_pairs={{0,8},{1,9},{2,10},{3,11},{4,12},{5,13},{6,14},{7,15},{8,16},{9,17... | collective-permute-start | bytes 147464 | tf_op jit(solution)/shard_map/ppermute | solution.py:353
  76.4 6.7 %collective-permute-start.17 = (f32[3,32,128]{2,1,0:T(8,128)S(1)}, f32[3,32,128]{2,1,0:T(8,128)S(1)}, u32[]{:S(2)}, u32[]{:S(2)}) collective-permute-start(f32[3,32,128]{2,1,0:T(8,128)S(1)} %shard_map.103.own_ref), channel_id=1, source_target_pairs={{0,120},{1,121},{2,122},{3,123},{4,124},{5,125},{6,126},{7,127},{8... | collective-permute-start | bytes 147464 | tf_op jit(solution)/shard_map/ppermute | solution.py:353
  83.1 5.8 %collective-permute-start.18 = (f32[3,3,32,128]{3,2,1,0:T(8,128)S(1)}, f32[3,3,32,128]{3,2,1,0:T(8,128)S(1)}, u32[]{:S(2)}, u32[]{:S(2)}) collective-permute-start(f32[3,3,32,128]{3,2,1,0:T(8,128)S(1)} %pad_maximum_fusion.4), channel_id=1, source_target_pairs={{0,1},{1,2},{2,3},{3,4},{4,5},{5,6},{6,7},{7,0},{8,9},{9,10},{10,1... | collective-permute-start | bytes 442376 | tf_op jit(solution)/shard_map/ppermute | solution.py:353
  86.8 5.8 %collective-permute-start.19 = (f32[3,3,32,128]{3,2,1,0:T(8,128)S(1)}, f32[3,3,32,128]{3,2,1,0:T(8,128)S(1)}, u32[]{:S(2)}, u32[]{:S(2)}) collective-permute-start(f32[3,3,32,128]{3,2,1,0:T(8,128)S(1)} %pad_maximum_fusion.4), channel_id=1, source_target_pairs={{0,7},{1,0},{2,1},{3,2},{4,3},{5,4},{6,5},{7,6},{8,15},{9,8},{10,9... | collective-permute-start | bytes 442376 | tf_op jit(solution)/shard_map/ppermute | solution.py:353
where the time goes:
time: 94 us; the launch traced here: 94.7 us
  waiting for transfers between devices  40.4 us (43%)
  starting transfers between devices  37.2 us (40%)
  Pallas kernels  12.6 us (13%)
  local copies, waits for them, and re-layouts  3.79 us (4%)
    ppermute x20, waiting for transfers between devices, moved(): return lax.ppermute(value, ('gx', 'gy'), pairs)  40.4 us
    ppermute x20, starting transfers between devices, moved(): return lax.ppermute(value, ('gx', 'gy'), pairs)  37.2 us
    pallas_call x1, Pallas kernels, shards(): call(scatter_kernel, [((TILE_X, TILE_Y, CHAN, LANES), BF)] + [((TILE_Y, C...  3.25 us
    pallas_call x1, Pallas kernels, shards(): call(second_conv_kernel, [((3, TILE_X * TILE_Y, LANES), F32)], [SM] + [VM...  3.18 us
    unnamed x22, local copies, waits for them, and re-layouts  2.88 us
    pallas_call x1, Pallas kernels, shards(): call(first_conv_kernel, [((TILE_X, TILE_Y, CHAN, LANES), BF), ((TILE_X //...  2.41 us
    pallas_call x1, Pallas kernels, shards(): call(partial_kernel, [(packed, BF)] * 9, [SM] * 4 + [VM] * 3, [pltpu.VMEM...  2.3 us
  transfers between devices with their start and end apart: 20, of which 12 were waited for; matrix products, arithmetic and copies ran while one was open for 1% of the time, Pallas kernels for 0%

commit v1 on v0

v1 whole, which is shorter than its diff:
```python
import functools

import jax
import jax.numpy as jnp
from jax import lax
from jax.experimental import pallas as pl
from jax.experimental.pallas import tpu as pltpu
from jax.sharding import PartitionSpec as P

BF = jnp.bfloat16
F32 = jnp.float32
I32 = jnp.int32

CHAN = 64
LANES = 128
TILE_X = 4
TILE_Y = 8
SLOTS = 8
GROUP = 4
CHUNKS = 4
VMEM_LIMIT = 40 * 1024 * 1024

VM = pl.BlockSpec(memory_space=pltpu.VMEM)
SM = pl.BlockSpec(memory_space=pltpu.SMEM)
HB = pl.BlockSpec(memory_space=pltpu.HBM)
NT = (((1,), (1,)), ((), ()))


def call(kernel, outs, ins, scratch, flops, limit=VMEM_LIMIT):
    return pl.pallas_call(
        kernel,
        out_shape=[jax.ShapeDtypeStruct(s, d) for s, d in outs],
        in_specs=ins,
        out_specs=[VM] * len(outs),
        scratch_shapes=scratch,
        compiler_params=pltpu.CompilerParams(vmem_limit_bytes=limit),
        cost_estimate=pl.CostEstimate(flops=flops, bytes_accessed=2000000, transcendentals=0),
    )


def partial_kernel(
    where_ref, counts_ref, block_ref, dest_ref, feat_hbm, nodes_ref, weight_hbm, *rest
):
    outs = rest[:9]
    feat_ref, weight_ref, sem, part, hi_all, lo_all, index, taken, entry_of = rest[9:]
    entries = weight_ref.shape[0]
    size = entries // CHUNKS
    copies = [pltpu.make_async_copy(feat_hbm, feat_ref, sem.at[CHUNKS])]
    for c in range(CHUNKS):
        rows = pl.ds(c * size, size)
        copies.append(pltpu.make_async_copy(weight_hbm.at[rows], weight_ref.at[rows], sem.at[c]))
    for c in copies:
        c.start()
    nodes = nodes_ref[...]
    hi_all[...] = (nodes >> 8).astype(F32)
    lo_all[...] = (nodes & 255).astype(F32)
    index[...] = jnp.full(index.shape, -1.0, F32)
    for d in range(9):
        taken[d] = 0

    def place(e, carry):
        tile = dest_ref[e]
        step_x = tile // where_ref[2] - where_ref[0]
        step_y = tile % where_ref[2] - where_ref[1]
        odd_x = where_ref[0] % 2
        odd_y = where_ref[1] % 2
        by_x = jnp.where(step_x > 0, odd_x, 1 - odd_x)
        by_y = jnp.where(step_y > 0, odd_y, 1 - odd_y)
        d = jnp.where(step_x == step_y, 5 + by_x, 7 + by_x)
        d = jnp.where(step_y == 0, 1 + by_x, d)
        d = jnp.where(step_x == 0, jnp.where(step_y == 0, 0, 3 + by_y), d)
        s = taken[d]
        taken[d] = s + 1
        entry_of[d * SLOTS + s] = e
        index[pl.ds(d * 16 + s, 1), :] = hi_all[pl.ds(e, 1), :]
        index[pl.ds(d * 16 + 8 + s, 1), :] = lo_all[pl.ds(e, 1), :]
        return carry

    lax.fori_loop(0, entries, place, 0)
    copies[0].wait()
    lane = lax.broadcasted_iota(I32, (CHAN, LANES), 1)
    for e in range(entries):
        if e % size == 0:
            copies[1 + e // size].wait()
        block = block_ref[e]
        feat = jnp.where(lane < counts_ref[block], feat_ref[block].astype(F32), 0.0).astype(BF)
        value = jnp.dot(feat, weight_ref[e], preferred_element_type=F32)
        part[e] = value.astype(BF)
    for d in range(9):

        def copy(s, carry, d=d):
            outs[d][pl.ds(pl.multiple_of(s * CHAN, CHAN), CHAN), :] = part[entry_of[d * SLOTS + s]]
            return carry

        lax.fori_loop(0, taken[d], copy, 0)
        outs[d][SLOTS * CHAN :, :] = index[d * 16 : d * 16 + 16, :].astype(BF)


def scatter_kernel(parts, first, last, *refs):
    where_ref = refs[0]
    got = refs[1 : parts + 1]
    refs = refs[parts + 1 :]
    if not first:
        before = refs[0]
        refs = refs[1:]
    if last:
        grid_ref, one_ref, two_ref, values, index, hi_all, lo_all, acc = refs
    else:
        acc, values, index, hi_all, lo_all = refs
    hi_all[...] = jnp.full(hi_all.shape, -1.0, F32)
    lo_all[...] = jnp.full(lo_all.shape, -1.0, F32)
    counts = []
    for d in range(parts):
        rows = got[d][SLOTS * CHAN :, :].astype(F32)
        index[d * 16 : d * 16 + 16, :] = rows
        counts.append(jnp.sum(jnp.where(rows[0:8, 0:1] >= 0.0, 1.0, 0.0)).astype(I32))
    filled = jnp.int32(0)
    for d in range(parts):

        def copy(s, pos, d=d):
            values[pos] = got[d][pl.ds(pl.multiple_of(s * CHAN, CHAN), CHAN), :]
            hi_all[pl.ds(pos, 1), :] = index[pl.ds(d * 16 + s, 1), :]
            lo_all[pl.ds(pos, 1), :] = index[pl.ds(d * 16 + 8 + s, 1), :]
            return pos + 1

        filled = lax.fori_loop(0, counts[d], copy, filled)
    row = lax.broadcasted_iota(I32, (256, LANES), 0).astype(F32)
    if first:
        acc[...] = jnp.zeros(acc.shape, F32)
    else:
        acc[...] = before[...]

    def step(g, carry):
        left = [[] for _ in range(16)]
        right = []
        for j in range(GROUP):
            e = g * GROUP + j
            value = values[e]
            hi = jnp.broadcast_to(hi_all[pl.ds(e, 1), :], (CHAN, LANES)).astype(BF)
            lo = lo_all[pl.ds(e, 1), :]
            right.append(jnp.where(row == lo, 1.0, 0.0).astype(BF))
            for t in range(16):
                left[t].append(jnp.where(hi == jnp.array(t, BF), value, jnp.array(0, BF)))
        a = jnp.concatenate([jnp.concatenate(rows, axis=1) for rows in left], axis=0)
        b = jnp.concatenate(right, axis=1)
        acc[...] += lax.dot_general(a, b, NT, preferred_element_type=F32)
        return carry

    lax.fori_loop(0, (filled + GROUP - 1) // GROUP, step, 0)
    if not last:
        return
    for t in range(16):
        for half in range(2):
            column = acc[t * CHAN : (t + 1) * CHAN, half * LANES : (half + 1) * LANES].astype(BF)
            x = t // 4
            y = (t % 4) * 2 + half
            grid_ref[x, y] = column
    odd = where_ref[0] % 2

    @pl.when(odd == 0)
    def _():
        one_ref[...] = grid_ref[TILE_X - 1]
        two_ref[...] = grid_ref[0]

    @pl.when(odd == 1)
    def _():
        one_ref[...] = grid_ref[0]
        two_ref[...] = grid_ref[TILE_X - 1]


def scatter(where, parts, before, last):
    most = len(parts) * SLOTS + GROUP
    sums = ((16 * CHAN, 256), F32)
    first = before is None
    if last:
        outs = [((TILE_X, TILE_Y, CHAN, LANES), BF)] + [((TILE_Y, CHAN, LANES), BF)] * 2
    else:
        outs = [sums]
    return call(
        functools.partial(scatter_kernel, len(parts), first, last),
        outs,
        [SM] + [VM] * (len(parts) + (not first)),
        [
            pltpu.VMEM((most, CHAN, LANES), BF),
            pltpu.VMEM((len(parts) * 16, LANES), F32),
            pltpu.VMEM((most, LANES), F32),
            pltpu.VMEM((most, LANES), F32),
        ]
        + [pltpu.VMEM(*sums)] * last,
        800000000,
    )(where, *parts, *([] if first else [before]))


def shifted(column):
    lane = lax.broadcasted_iota(I32, column.shape, 1)
    wide = column.astype(F32)
    before = jnp.where(lane == 0, 0.0, pltpu.roll(wide, 1, 1)).astype(BF)
    after = jnp.where(lane == LANES - 1, 0.0, pltpu.roll(wide, LANES - 1, 1)).astype(BF)
    return jnp.concatenate([before, column, after], axis=0)


def conv_rows(picks, weight_ref, size_x, put):
    weight = weight_ref[...]
    sums = [None] * size_x
    for x in range(size_x + 2):
        rhs = jnp.concatenate(picks(x), axis=1)
        first = max(0, x - size_x + 1)
        last = min(2, x)
        prod = jnp.dot(weight[first * CHAN : (last + 1) * CHAN], rhs, preferred_element_type=F32)
        for a in range(first, last + 1):
            piece = prod[(a - first) * CHAN : (a - first + 1) * CHAN]
            out = x - a
            sums[out] = piece if sums[out] is None else sums[out] + piece
        if x >= 2:
            put(x - 2, sums[x - 2])
            sums[x - 2] = None


def flat(taps):
    return taps.reshape(9 * CHAN, LANES)


def silu(v):
    return v / (1.0 + jnp.exp(-v))


def edges(where_ref):
    x_lo = where_ref[0] > 0
    x_hi = where_ref[0] < where_ref[3] - 1
    y_lo = where_ref[1] > 0
    y_hi = where_ref[1] < where_ref[2] - 1
    return x_lo, x_hi, y_lo, y_hi


def in_order(odd, one_ref, two_ref, low_ref, high_ref):
    @pl.when(odd == 0)
    def _():
        one_ref[...] = high_ref[...]
        two_ref[...] = low_ref[...]

    @pl.when(odd == 1)
    def _():
        one_ref[...] = low_ref[...]
        two_ref[...] = high_ref[...]


def sorted_x(where_ref, one_ref, two_ref, xl_ref, xh_ref):
    x_lo, x_hi, _, _ = edges(where_ref)
    odd = where_ref[0] % 2 == 1
    for i in range(xl_ref.shape[0]):
        one = one_ref[i].astype(F32)
        two = two_ref[i].astype(F32)
        xl_ref[i] = jnp.where(x_lo, jnp.where(odd, one, two), 0.0).astype(BF)
        xh_ref[i] = jnp.where(x_hi, jnp.where(odd, two, one), 0.0).astype(BF)


def sorted_y(where_ref, one_ref, two_ref, i):
    _, _, y_lo, y_hi = edges(where_ref)
    odd = where_ref[1] % 2 == 1
    one = one_ref[i].astype(F32)
    two = two_ref[i].astype(F32)
    lower = jnp.where(y_lo, jnp.where(odd, one, two), 0.0).astype(BF)
    higher = jnp.where(y_hi, jnp.where(odd, two, one), 0.0).astype(BF)
    return lower, higher


def grid_side_kernel(
    where_ref, one_ref, two_ref, grid_ref, xl_ref, xh_ref, y_one_ref, y_two_ref, low, high
):
    sorted_x(where_ref, one_ref, two_ref, xl_ref, xh_ref)
    for ref, y in ((low, 0), (high, TILE_Y - 1)):
        ref[0] = xl_ref[y]
        for x in range(TILE_X):
            ref[x + 1] = grid_ref[x, y]
        ref[TILE_X + 1] = xh_ref[y]
    in_order(where_ref[1] % 2, y_one_ref, y_two_ref, low, high)


def coarse_side_kernel(
    where_ref, one_ref, two_ref, coarse_ref, down_ref, up_ref,
    xl_ref, xh_ref, y_one_ref, y_two_ref, low, high,
):
    sorted_x(where_ref, one_ref, two_ref, xl_ref, xh_ref)
    half_y = TILE_Y // 2
    for ref, y, own in ((low, 0, down_ref), (high, half_y - 2, up_ref)):
        for x in range(2):
            for k in range(2):
                ref[x * 2 + k] = xl_ref[x * half_y + y + k]
                ref[4 + x * 2 + k] = coarse_ref[x, y + k]
                ref[8 + x * 2 + k] = xh_ref[x * half_y + y + k]
        ref[12] = own[0]
        ref[13] = xl_ref[9]
        ref[14] = xh_ref[9]
    in_order(where_ref[1] % 2, y_one_ref, y_two_ref, low, high)


def field_side_kernel(where_ref, one_ref, two_ref, own_ref, row_ref):
    odd = where_ref[0] % 2
    row_ref[1] = own_ref[...]

    @pl.when(odd == 0)
    def _():
        row_ref[0] = two_ref[...]
        row_ref[2] = one_ref[...]

    @pl.when(odd == 1)
    def _():
        row_ref[0] = one_ref[...]
        row_ref[2] = two_ref[...]


def masked(column, *conditions):
    keep = functools.reduce(jnp.logical_and, conditions)
    return jnp.where(keep, column.astype(F32), 0.0).astype(BF)


def inner_conv_kernel(grid_ref, xl_ref, xh_ref, weight_ref, stack, act_ref):
    for y in range(TILE_Y):
        for x in range(TILE_X):
            stack[x + 1, y] = shifted(grid_ref[x, y])
        stack[0, y] = shifted(xl_ref[y])
        stack[TILE_X + 1, y] = shifted(xh_ref[y])
    for y in range(1, TILE_Y - 1, 2):

        def picks(x, y=y):
            return [flat(stack[x, y - 1 : y + 2]), flat(stack[x, y : y + 3])]

        def put(x, value, y=y):
            for k in range(2):
                part = value[:, k * LANES : (k + 1) * LANES]
                act_ref[x, y - 1 + k] = (silu(part) + grid_ref[x, y + k].astype(F32)).astype(BF)

        conv_rows(picks, weight_ref, TILE_X, put)


def joined(total):
    lane = lax.broadcasted_iota(I32, (8, LANES), 1)
    before = jnp.where(lane == 0, 0.0, pltpu.roll(total[0:8], 1, 1))
    after = jnp.where(lane == LANES - 1, 0.0, pltpu.roll(total[16:24], LANES - 1, 1))
    both = before + total[8:16] + after
    return both[0:3] + both[3:6]


def two_parts(value):
    high = value.astype(BF).astype(F32)
    return jnp.concatenate([high, value - high, jnp.zeros((2, LANES), F32)], axis=0)


def one_part(column, row):
    piece = column[row : row + 8]
    return piece[0:3] + piece[3:6]


def outer_conv_kernel(
    where_ref, grid_ref, stack, inner_ref, y_one_ref, y_two_ref, weight_ref, out_weight_ref,
    act_ref, coarse_ref, one_ref, two_ref, down_ref, up_ref, edge, taps, low_ref, high_ref,
):
    for x in range(TILE_X + 2):
        lower, higher = sorted_y(where_ref, y_one_ref, y_two_ref, x)
        edge[x, 0] = shifted(lower)
        edge[x, 1] = shifted(higher)
    last_y = TILE_Y - 1

    def picks(x):
        return [
            jnp.concatenate([edge[x, 0], stack[x, 0], stack[x, 1]], axis=0),
            jnp.concatenate([stack[x, last_y - 1], stack[x, last_y], edge[x, 1]], axis=0),
        ]

    def put(x, value):
        for k, y in enumerate((0, last_y)):
            part = value[:, k * LANES : (k + 1) * LANES]
            act_ref[x, y] = (silu(part) + grid_ref[x, y].astype(F32)).astype(BF)

    conv_rows(picks, weight_ref, TILE_X, put)
    for x in range(TILE_X):
        for y in range(1, last_y):
            act_ref[x, y] = inner_ref[x, y - 1]
    half_y = TILE_Y // 2
    for x in range(TILE_X // 2):
        for y in range(half_y):
            total = (
                act_ref[2 * x, 2 * y].astype(F32)
                + act_ref[2 * x, 2 * y + 1].astype(F32)
                + act_ref[2 * x + 1, 2 * y].astype(F32)
                + act_ref[2 * x + 1, 2 * y + 1].astype(F32)
            )
            result = (total * 0.25).astype(BF)
            coarse_ref[x, y] = result
            low_ref[x * half_y + y] = result
            high_ref[x * half_y + y] = result
    pairs = []
    for x in (0, TILE_X - 1):
        pairs += [((x, y), (x, y + 1)) for y in range(0, TILE_Y, 2)]
    pairs += [((1, y), (2, y)) for y in (0, last_y)]
    weight = out_weight_ref[...]
    for first, second in pairs:
        rhs = jnp.concatenate([act_ref[first], act_ref[second]], axis=1)
        prod = jnp.dot(weight, rhs, preferred_element_type=F32)
        taps[first] = prod[:, :LANES]
        taps[second] = prod[:, LANES:]

    def outside(cells):
        total = None
        for x, y, a, b in cells:
            if 0 <= x < TILE_X and 0 <= y < TILE_Y:
                start = (a * 3 + b) * 24
                piece = taps[x, y, start : start + 24, :]
                total = piece if total is None else total + piece
        return two_parts(joined(total))

    def column(pieces):
        rest = CHAN - 8 * len(pieces)
        if rest:
            pieces = pieces + [jnp.zeros((rest, LANES), F32)]
        return jnp.concatenate(pieces, axis=0).astype(BF)

    for ref, x, a in ((low_ref, 0, 2), (high_ref, TILE_X - 1, 0)):
        cells = [
            outside([(x, y + b - 1, a, b) for b in range(3)]) for y in range(-1, TILE_Y + 1)
        ]
        ref[8] = column(cells[1:-1])
        ref[9] = column([cells[0], cells[-1]])
    for ref, y, b in ((down_ref, 0, 2), (up_ref, last_y, 0)):
        ref[0] = column(
            [outside([(x + a - 1, y, a, b) for a in range(3)]) for x in range(TILE_X)]
        )
    in_order(where_ref[0] % 2, one_ref, two_ref, low_ref, high_ref)


def second_conv_kernel(
    where_ref, act_ref, coarse_ref, xl_ref, xh_ref, y_one_ref, y_two_ref,
    mid_weight_ref, out_weight_ref,
    field_ref, sent_ref, stack, merged, mid_ref, taps, yl_ref, yh_ref,
):
    for i in range(15):
        yl_ref[i], yh_ref[i] = sorted_y(where_ref, y_one_ref, y_two_ref, i)
    x_lo, x_hi, y_lo, y_hi = edges(where_ref)
    half_x = TILE_X // 2
    half_y = TILE_Y // 2
    for x in range(half_x):
        for y in range(half_y):
            stack[x + 2, y + 2] = shifted(coarse_ref[x, y])
            stack[x, y + 2] = shifted(xl_ref[x * half_y + y])
            stack[x + 2 + half_x, y + 2] = shifted(xh_ref[x * half_y + y])
    for x in range(half_x + 4):
        for y in range(2):
            stack[x, y] = shifted(yl_ref[x * 2 + y])
            stack[x, half_y + 2 + y] = shifted(yh_ref[x * 2 + y])
    for y in range(0, half_y + 2, 2):

        def picks(x, y=y):
            return [flat(stack[x, y : y + 3]), flat(stack[x, y + 1 : y + 4])]

        def put(x, value, y=y):
            result = silu(value).astype(BF)
            mid_ref[x, y] = result[:, :LANES]
            mid_ref[x, y + 1] = result[:, LANES:]

        conv_rows(picks, mid_weight_ref, half_x + 2, put)
    for x in range(TILE_X + 2):
        for y in range(TILE_Y + 2):
            more = ()
            if x == 0:
                more += (x_lo,)
            if x == TILE_X + 1:
                more += (x_hi,)
            if y == 0:
                more += (y_lo,)
            if y == TILE_Y + 1:
                more += (y_hi,)
            value = mid_ref[(x + 1) // 2, (y + 1) // 2]
            if more:
                merged[x, y] = masked(value, *more)
            else:
                merged[x, y] = (act_ref[x - 1, y - 1].astype(F32) + value.astype(F32)).astype(BF)
    weight = out_weight_ref[...]
    for x in range(TILE_X + 2):
        for y in range(0, TILE_Y + 2, 2):
            pair = jnp.concatenate([merged[x, y], merged[x, y + 1]], axis=1)
            prod = jnp.dot(weight, pair, preferred_element_type=F32)
            taps[x, y] = prod[:, :LANES]
            taps[x, y + 1] = prod[:, LANES:]

    def received(ref, place, row):
        return one_part(ref[place].astype(F32), row)

    for x in range(TILE_X):
        for y in range(TILE_Y):
            total = None
            for a in range(3):
                for b in range(3):
                    start = (a * 3 + b) * 24
                    piece = taps[x + a, y + b, start : start + 24, :]
                    total = piece if total is None else total + piece
            value = joined(total)
            x_ref = xl_ref if x == 0 else xh_ref
            y_ref = yl_ref if y == 0 else yh_ref
            on_x = x in (0, TILE_X - 1)
            on_y = y in (0, TILE_Y - 1)
            if on_x:
                value += received(x_ref, 8, y * 8)
            if on_y:
                value += received(y_ref, 12, x * 8)
            if on_x and on_y:
                value += received(y_ref, 13 + (x > 0), 8 if y == 0 else 0)
            for d in range(3):
                field_ref[d, x * TILE_Y + y : x * TILE_Y + y + 1, :] = value[d : d + 1]
    sent_ref[...] = field_ref[...].astype(BF)


def gather_kernel(
    where_ref, counts_ref, block_ref, dest_ref, own_ref, row_ref, y_one_ref, y_two_ref,
    nodes_ref, weight_ref, out_ref, frame, total,
):
    entries = weight_ref.shape[0]
    blocks = out_ref.shape[0]
    odd = where_ref[1] % 2 == 1
    frame[5] = own_ref[...]
    for i in range(3):
        one = y_one_ref[i].astype(F32)
        two = y_two_ref[i].astype(F32)
        frame[3 * i + 1] = jnp.where(odd, one, two)
        frame[3 * i + 3] = jnp.where(odd, two, one)
        if i != 1:
            frame[3 * i + 2] = row_ref[i].astype(F32)
    total[...] = jnp.zeros(total.shape, F32)
    sub = lax.broadcasted_iota(I32, (8, LANES), 0)
    for e in range(entries):
        tile = dest_ref[e]
        d = (tile // where_ref[2] - where_ref[0] + 1) * 3 + (tile % where_ref[2] - where_ref[1] + 1)
        node = jnp.broadcast_to(nodes_ref[e : e + 1, :], (8, LANES))
        z = node & (LANES - 1)
        column = node >> 7
        rows = []
        for c in range(3):
            picked = None
            for q in range(4):
                table = frame[d + 1, c, q * 8 : q * 8 + 8, :]
                value = jnp.take_along_axis(table, z, axis=1)
                value = jnp.where(column == sub + q * 8, value, 0.0)
                picked = value if picked is None else picked + value
            rows.append(picked)
        wide = jnp.concatenate(rows, axis=0)
        high = wide.astype(BF)
        low = (wide - high.astype(F32)).astype(BF)
        both = jnp.concatenate([high, low], axis=0)
        value = lax.dot_general(both, weight_ref[e], NT, preferred_element_type=F32)
        block = block_ref[e]
        total[block] += value[0:24] + value[24:48]
    lane = lax.broadcasted_iota(I32, (1, LANES), 1)
    for b in range(blocks):
        live = lane < counts_ref[b]
        for c in range(3):
            value = jnp.sum(total[b, c * 8 : c * 8 + 8, :], axis=0, keepdims=True)
            out_ref[b, c : c + 1, :] = jnp.where(live, value, 0.0)


def partners(size_x, size_y, step_x, step_y, parity):
    left = [(0, y) for y in range(size_y)]
    top = [(x, size_y - 1) for x in range(1, size_x)]
    right = [(size_x - 1, y) for y in reversed(range(size_y - 1))]
    bottom = [(x, 0) for x in reversed(range(1, size_x - 1))]
    rim = left + top + right + bottom
    if not step_x:
        rim = rim[size_y - 1 :] + rim[: size_y - 1]
    partner = {}
    for x in range(size_x):
        for y in range(size_y):
            sign = 1 if (x if step_x else y) % 2 == parity else -1
            to = (x + sign * step_x, y + sign * step_y)
            if 0 <= to[0] < size_x and 0 <= to[1] < size_y:
                partner[x, y] = to
    alone = [place for place in rim if place not in partner]
    for one, two in zip(alone[::2], alone[1::2]):
        partner[one] = two
        partner[two] = one
    return partner


def swapped(value, step_x, step_y, parity):
    size_x = lax.axis_size("gx")
    size_y = lax.axis_size("gy")
    partner = partners(size_x, size_y, step_x, step_y, parity)
    pairs = [
        (x * size_y + y, to_x * size_y + to_y) for (x, y), (to_x, to_y) in sorted(partner.items())
    ]
    return lax.ppermute(value, ("gx", "gy"), pairs)


def across_x(one, two):
    return swapped(one, 1, 0, 0), swapped(two, 1, 0, 1)


def across_y(one, two):
    return swapped(one, 0, 1, 0), swapped(two, 0, 1, 1)


def shards(
    particle_feat, block_counts, entry_block, entry_dest, entry_nodes, entry_weights,
    conv_in, conv_mid, conv_out, head_weight,
):
    size_x = lax.axis_size("gx")
    size_y = lax.axis_size("gy")
    where = jnp.stack(
        [
            lax.axis_index("gx").astype(I32),
            lax.axis_index("gy").astype(I32),
            jnp.int32(size_y),
            jnp.int32(size_x),
        ]
    )
    blocks = particle_feat.shape[0]
    entries = entry_weights.shape[0]
    dest = entry_dest.reshape(entries)
    in_weight = conv_in.reshape(3 * CHAN, 9 * CHAN)
    mid_weight = conv_mid.reshape(3 * CHAN, 9 * CHAN)
    folded = jnp.einsum(
        "do,aox->adx", head_weight, conv_out.astype(F32), precision=lax.Precision.HIGHEST
    )
    high = lax.reduce_precision(folded, 8, 7)
    both = jnp.concatenate([high, folded - high, jnp.zeros((3, 2, 9 * CHAN), F32)], axis=1)
    out_weight = (
        both.reshape(3, 8, 9, CHAN).transpose(0, 2, 1, 3).reshape(27 * 8, CHAN).astype(BF)
    )

    packed = (SLOTS * CHAN + 16, LANES)
    sent = call(
        partial_kernel,
        [(packed, BF)] * 9,
        [SM] * 4 + [HB, VM, HB],
        [
            pltpu.VMEM(particle_feat.shape, BF),
            pltpu.VMEM(entry_weights.shape, BF),
            pltpu.SemaphoreType.DMA((CHUNKS + 1,)),
            pltpu.VMEM((entries, CHAN, LANES), BF),
            pltpu.VMEM((entries, LANES), F32),
            pltpu.VMEM((entries, LANES), F32),
            pltpu.VMEM((9 * 16, LANES), F32),
            pltpu.SMEM((9,), I32),
            pltpu.SMEM((9 * SLOTS,), I32),
        ],
        70000000,
        limit=60 * 1024 * 1024,
    )(where, block_counts, entry_block, dest, particle_feat, entry_nodes, entry_weights)
    sides = [*across_x(sent[1], sent[2]), *across_y(sent[3], sent[4])]
    sums = scatter(where, [sent[0]], None, False)[0]
    *corners, sums = lax.optimization_barrier((*sent[5:], sums))
    corners = [
        swapped(value, 1, 1 - 2 * (i // 2), i % 2) for i, value in enumerate(corners)
    ]
    sums = scatter(where, sides, sums, False)[0]
    grid, one, two = scatter(where, corners, sums, True)

    column = (CHAN, LANES)
    one, two = across_x(one, two)
    xl, xh, one, two = call(
        grid_side_kernel,
        [((TILE_Y, *column), BF)] * 2 + [((TILE_X + 2, *column), BF)] * 2,
        [SM] + [VM] * 3,
        [pltpu.VMEM((TILE_X + 2, *column), BF)] * 2,
        1000000,
    )(where, one, two, grid)
    one, two = across_y(one, two)
    stack, inner = call(
        inner_conv_kernel,
        [
            ((TILE_X + 2, TILE_Y, 3 * CHAN, LANES), BF),
            ((TILE_X, TILE_Y - 2, CHAN, LANES), BF),
        ],
        [VM] * 4,
        [],
        1000000000,
    )(grid, xl, xh, in_weight)
    act, coarse, one, two, down, up = call(
        outer_conv_kernel,
        [
            ((TILE_X, TILE_Y, *column), BF),
            ((TILE_X // 2, TILE_Y // 2, *column), BF),
            ((10, *column), BF),
            ((10, *column), BF),
            ((1, *column), BF),
            ((1, *column), BF),
        ],
        [SM] + [VM] * 7,
        [
            pltpu.VMEM((TILE_X + 2, 2, 3 * CHAN, LANES), BF),
            pltpu.VMEM((TILE_X, TILE_Y, 27 * 8, LANES), F32),
            pltpu.VMEM((10, *column), BF),
            pltpu.VMEM((10, *column), BF),
        ],
        600000000,
    )(where, grid, stack, inner, one, two, in_weight, out_weight)

    one, two = across_x(one, two)
    xl, xh, one, two = call(
        coarse_side_kernel,
        [((10, *column), BF)] * 2 + [((15, *column), BF)] * 2,
        [SM] + [VM] * 5,
        [pltpu.VMEM((15, *column), BF)] * 2,
        1000000,
    )(where, one, two, coarse, down, up)
    one, two = across_y(one, two)
    field, rounded = call(
        second_conv_kernel,
        [((3, TILE_X * TILE_Y, LANES), F32), ((3, TILE_X * TILE_Y, LANES), BF)],
        [SM] + [VM] * 8,
        [
            pltpu.VMEM((6, 8, 3 * CHAN, LANES), BF),
            pltpu.VMEM((TILE_X + 2, TILE_Y + 2, CHAN, LANES), BF),
            pltpu.VMEM((4, 6, CHAN, LANES), BF),
            pltpu.VMEM((TILE_X + 2, TILE_Y + 2, 27 * 8, LANES), F32),
            pltpu.VMEM((15, *column), BF),
            pltpu.VMEM((15, *column), BF),
        ],
        1300000000,
    )(where, act, coarse, xl, xh, one, two, mid_weight, out_weight)

    one, two = across_x(rounded, rounded)
    row = call(
        field_side_kernel,
        [((3, 3, TILE_X * TILE_Y, LANES), BF)],
        [SM] + [VM] * 3,
        [],
        1000000,
    )(where, one, two, rounded)[0]
    one, two = across_y(row, row)
    return call(
        gather_kernel,
        [((blocks, 3, LANES), F32)],
        [SM] * 4 + [VM] * 6,
        [
            pltpu.VMEM((10, 3, TILE_X * TILE_Y, LANES), F32),
            pltpu.VMEM((blocks, 24, LANES), F32),
        ],
        70000000,
    )(
        where, block_counts, entry_block, dest, field, row, one, two, entry_nodes, entry_weights
    )[0]


def solution(mesh):
    in_specs = (
        P(("gx", "gy"), None, None),
        P(("gx", "gy")),
        P(("gx", "gy")),
        P(("gx", "gy"), None),
        P(("gx", "gy"), None),
        P(("gx", "gy"), None, None),
        P(),
        P(),
        P(),
        P(),
    )
    out_specs = P(("gx", "gy"), None, None)
    return jax.shard_map(shards, mesh=mesh, in_specs=in_specs, out_specs=out_specs, check_vma=False)
```

time: 94 us -> 78.4 us (0.83)
  the two profiles are of different devices: /device:TPU:7 before, /device:TPU:16 now
where the time goes in v1:
time: 78.4 us
  waiting for transfers between devices  32.9 us (42%)
  starting transfers between devices  22.1 us (28%)
  Pallas kernels  20 us (26%)
  local copies, waits for them, and re-layouts  2.36 us (3%)
    ppermute x20, waiting for transfers between devices, swapped(): return lax.ppermute(value, ('gx', 'gy'), pairs)  32.9 us
    ppermute x20, starting transfers between devices, swapped(): return lax.ppermute(value, ('gx', 'gy'), pairs)  22.1 us
    pallas_call x3, Pallas kernels, scatter(): call(functools.partial(scatter_kernel, len(parts), first, last), outs, [S...  5.79 us
    pallas_call x1, Pallas kernels, shards(): call(partial_kernel, [(packed, BF)] * 9, [SM] * 4 + [HB, VM, HB], [pltpu....  4.11 us
    pallas_call x1, Pallas kernels, shards(): call(second_conv_kernel, [((3, TILE_X * TILE_Y, LANES), F32), ((3, TILE_X...  3.31 us
    pallas_call x1, Pallas kernels, shards(): call(outer_conv_kernel, [((TILE_X, TILE_Y, *column), BF), ((TILE_X // 2,...  2.03 us
  transfers between devices with their start and end apart: 20, of which 13 were waited for; matrix products, arithmetic and copies ran while one was open for 1% of the time, Pallas kernels for 7%

profile of v1, /device:TPU:16, one launch (start us, length us, event | category | flops | bytes accessed | tf_op | source)
XLA Modules:
  0.0 78.4 jit_solution(15362042062329888937)
XLA Ops:
  0.0 0.6 pad_add_fusion.where_ref.refs_0_
  0.6 4.1 %shard_map.100 = (bf16[528,128]{1,0:T(8,128)(2,1)}, bf16[528,128]{1,0:T(8,128)(2,1)}, bf16[528,128]{1,0:T(8,128)(2,1)}, bf16[528,128]{1,0:T(8,128)(2,1)}, bf16[5...) custom-call(s32[4]{0:T(128)} %pad_add_fusion.where_ref.refs_0_, ...), custom_call_target="tpu_custom_call" | custom-call | flops 70000000 | bytes 2000000 | tf_op jit(solution)/shard_map/pallas_call | solution.py:628
  4.7 2.0 %collective-permute-start.4 = (bf16[528,128]{1,0:T(8,128)(2,1)}, bf16[528,128]{1,0:T(8,128)(2,1)S(1)}, u32[]{:S(2)}, u32[]{:S(2)}) collective-permute-start(bf16[528,128]{1,0:T(8,128)(2,1)} %get-tuple-element.49), channel_id=1, source_target_pairs={{0,8},{1,9},{2,10},{3,11},{4,12},{5,13},{6,14},{7,15},{8,0},{9,1},... | collective-permute-start | bytes 405512 | tf_op jit(solution)/shard_map/ppermute | solution.py:588
  6.7 2.4 %collective-permute-start.5 = (bf16[528,128]{1,0:T(8,128)(2,1)}, bf16[528,128]{1,0:T(8,128)(2,1)S(1)}, u32[]{:S(2)}, u32[]{:S(2)}) collective-permute-start(bf16[528,128]{1,0:T(8,128)(2,1)} %get-tuple-element.50), channel_id=1, source_target_pairs={{0,1},{1,0},{2,3},{3,2},{4,5},{5,4},{6,7},{7,6},{8,16},{9,17},{10,... | collective-permute-start | bytes 405512 | tf_op jit(solution)/shard_map/ppermute | solution.py:588
  9.1 1.1 %collective-permute-start.7 = (bf16[528,128]{1,0:T(8,128)(2,1)}, bf16[528,128]{1,0:T(8,128)(2,1)S(1)}, u32[]{:S(2)}, u32[]{:S(2)}) collective-permute-start(bf16[528,128]{1,0:T(8,128)(2,1)} %get-tuple-element.52), channel_id=1, source_target_pairs={{0,8},{1,2},{2,1},{3,4},{4,3},{5,6},{6,5},{7,15},{8,0},{9,10},{10,... | collective-permute-start | bytes 405512 | tf_op jit(solution)/shard_map/ppermute | solution.py:588
  10.2 0.6 copy-done.4
  10.8 0.9 %copy-done.10 = bf16[528,128]{1,0:T(8,128)(2,1)S(1)} copy-done((bf16[528,128]{1,0:T(8,128)(2,1)S(1)}, bf16[528,128]{1,0:T(8,128)(2,1)}, u32[]{:S(2)}) %copy-start.10) | copy-done | bytes 135192
  11.7 1.7 %shard_map.101.refs_5_ = f32[1024,256]{1,0:T(8,128)S(1)} custom-call(s32[4]{0:T(128)S(1)} %copy-done.4, bf16[528,128]{1,0:T(8,128)(2,1)S(1)} %copy-done.10), custom_call_target="tpu_custom_call" | custom-call | flops 800000000 | bytes 2000000 | tf_op jit(solution)/shard_map/pallas_call | solution.py:179
  13.5 1.3 %collective-permute-start = (bf16[528,128]{1,0:T(8,128)(2,1)S(1)}, bf16[528,128]{1,0:T(8,128)(2,1)S(1)}, u32[]{:S(2)}, u32[]{:S(2)}) collective-permute-start(bf16[528,128]{1,0:T(8,128)(2,1)S(1)} %copy-done.15), channel_id=1, source_target_pairs={{0,9},{1,10},{2,11},{3,12},{4,13},{5,14},{6,15},{7,23},{8,24},{9,0... | collective-permute-start | bytes 405512 | tf_op jit(solution)/shard_map/ppermute | solution.py:588
  14.8 2.1 %collective-permute-start.1 = (bf16[528,128]{1,0:T(8,128)(2,1)S(1)}, bf16[528,128]{1,0:T(8,128)(2,1)S(1)}, u32[]{:S(2)}, u32[]{:S(2)}) collective-permute-start(bf16[528,128]{1,0:T(8,128)(2,1)S(1)} %copy-done.14), channel_id=1, source_target_pairs={{0,1},{1,0},{2,3},{3,2},{4,5},{5,4},{6,7},{7,6},{8,17},{9,18},{10,... | collective-permute-start | bytes 405512 | tf_op jit(solution)/shard_map/ppermute | solution.py:588
  16.8 2.4 %collective-permute-start.2 = (bf16[528,128]{1,0:T(8,128)(2,1)S(1)}, bf16[528,128]{1,0:T(8,128)(2,1)S(1)}, u32[]{:S(2)}, u32[]{:S(2)}) collective-permute-start(bf16[528,128]{1,0:T(8,128)(2,1)S(1)} %copy-done.13), channel_id=1, source_target_pairs={{0,15},{1,8},{2,9},{3,10},{4,11},{5,12},{6,13},{7,14},{8,1},{9,2},... | collective-permute-start | bytes 405512 | tf_op jit(solution)/shard_map/ppermute | solution.py:588
  19.2 0.4 collective-permute-start.3
  19.7 2.2 %shard_map.102.refs_5_ = f32[1024,256]{1,0:T(8,128)S(1)} custom-call(s32[4]{0:T(128)S(1)} %copy-done.4, bf16[528,128]{1,0:T(8,128)(2,1)S(1)} %collective-permute-done.4.refs_1_, bf16[528,128]{1,0:T(8,128)(2,1)S(1)} %collective-permute-done.5.refs_2_, bf16[528,128]{1,0:T(8,128)(2,1)S(1)} %collective-permute-done.6.refs_3_, ...), custom_call_target="tpu_custom_call" | custom-call | flops 800000000 | bytes 2000000 | tf_op jit(solution)/shard_map/pallas_call | solution.py:179
  22.0 1.4 %collective-permute-done.1.refs_2_ = bf16[528,128]{1,0:T(8,128)(2,1)S(1)} collective-permute-done((bf16[528,128]{1,0:T(8,128)(2,1)S(1)}, bf16[528,128]{1,0:T(8,128)(2,1)S(1)}, u32[]{:S(2)}, u32[]{:S(2)}) %collective-permute-start.1) | collective-permute-done | bytes 135200 | tf_op jit(solution)/shard_map/ppermute | solution.py:588
  23.4 2.6 %collective-permute-done.2.refs_3_ = bf16[528,128]{1,0:T(8,128)(2,1)S(1)} collective-permute-done((bf16[528,128]{1,0:T(8,128)(2,1)S(1)}, bf16[528,128]{1,0:T(8,128)(2,1)S(1)}, u32[]{:S(2)}, u32[]{:S(2)}) %collective-permute-start.2) | collective-permute-done | bytes 135200 | tf_op jit(solution)/shard_map/ppermute | solution.py:588
  26.0 1.8 %collective-permute-done.3.refs_4_ = bf16[528,128]{1,0:T(8,128)(2,1)S(1)} collective-permute-done((bf16[528,128]{1,0:T(8,128)(2,1)S(1)}, bf16[528,128]{1,0:T(8,128)(2,1)S(1)}, u32[]{:S(2)}, u32[]{:S(2)}) %collective-permute-start.3) | collective-permute-done | bytes 135200 | tf_op jit(solution)/shard_map/ppermute | solution.py:588
  27.8 1.8 %shard_map.103 = (bf16[4,8,64,128]{3,2,1,0:T(8,128)(2,1)S(1)}, bf16[8,64,128]{2,1,0:T(8,128)(2,1)S(1)}, bf16[8,64,128]{2,1,0:T(8,128)(2,1)S(1)}) custom-call(s32[4]{0:T(128)S(1)} %copy-done.4, bf16[528,128]{1,0:T(8,128)(2,1)S(1)} %collective-permute-done.refs_1_, bf16[528,128]{1,0:T(8,128)(2,1)S(1)} %collective-permute-done.1.refs_2_, ...), custom_call_target="tpu_custom_call" | custom-call | flops 800000000 | bytes 2000000 | tf_op jit(solution)/shard_map/pallas_call | solution.py:179
  29.6 0.1 collective-permute-start.8
  29.7 2.7 %collective-permute-start.9 = (bf16[8,64,128]{2,1,0:T(8,128)(2,1)S(1)}, bf16[8,64,128]{2,1,0:T(8,128)(2,1)S(1)}, u32[]{:S(2)}, u32[]{:S(2)}) collective-permute-start(bf16[8,64,128]{2,1,0:T(8,128)(2,1)S(1)} %get-tuple-element.56), channel_id=1, source_target_pairs={{0,1},{1,0},{2,3},{3,2},{4,5},{5,4},{6,7},{7,6},{8,16},{9,17},{10,... | collective-permute-start | bytes 393224 | tf_op jit(solution)/shard_map/ppermute | solution.py:588
  32.4 0.2 reduce-precision_convert_fusion
  32.6 2.4 %collective-permute-done.8.one_ref = bf16[8,64,128]{2,1,0:T(8,128)(2,1)S(1)} collective-permute-done((bf16[8,64,128]{2,1,0:T(8,128)(2,1)S(1)}, bf16[8,64,128]{2,1,0:T(8,128)(2,1)S(1)}, u32[]{:S(2)}, u32[]{:S(2)}) %collective-permute-start.8) | collective-permute-done | bytes 131104 | tf_op jit(solution)/shard_map/ppermute | solution.py:588
  35.0 2.5 %collective-permute-done.9.two_ref = bf16[8,64,128]{2,1,0:T(8,128)(2,1)S(1)} collective-permute-done((bf16[8,64,128]{2,1,0:T(8,128)(2,1)S(1)}, bf16[8,64,128]{2,1,0:T(8,128)(2,1)S(1)}, u32[]{:S(2)}, u32[]{:S(2)}) %collective-permute-start.9) | collective-permute-done | bytes 131104 | tf_op jit(solution)/shard_map/ppermute | solution.py:588
  37.6 0.6 shard_map.104
  38.2 0.1 collective-permute-start.10
  38.3 0.1 collective-permute-start.11
  38.5 0.1 convert_element_type.8
  38.6 1.4 %shard_map.105 = (bf16[6,8,192,128]{3,2,1,0:T(8,128)(2,1)S(1)}, bf16[4,6,64,128]{3,2,1,0:T(8,128)(2,1)S(1)}) custom-call(bf16[4,8,64,128]{3,2,1,0:T(8,128)(2,1)S(1)} %get-tuple-element.54.grid_ref, bf16[8,64,128]{2,1,0:T(8,128)(2,1)S(1)} %get-tuple-element.57.xl_ref, bf16[8,64,128]{2,1,0:T(8,128)(2,1)S(1)} %get-tuple-element.58.xh_ref, ...), custom_call_target="tpu_custom_call" | custom-call | flops 1000000000 | bytes 2000000 | tf_op jit(solution)/shard_map/pallas_call | solution.py:665
  40.1 2.9 %collective-permute-done.11.y_two_ref = bf16[6,64,128]{2,1,0:T(8,128)(2,1)S(1)} collective-permute-done((bf16[6,64,128]{2,1,0:T(8,128)(2,1)S(1)}, bf16[6,64,128]{2,1,0:T(8,128)(2,1)S(1)}, u32[]{:S(2)}, u32[]{:S(2)}) %collective-permute-start.11) | collective-permute-done | bytes 98336 | tf_op jit(solution)/shard_map/ppermute | solution.py:588
  43.0 2.0 %shard_map.106 = (bf16[4,8,64,128]{3,2,1,0:T(8,128)(2,1)S(1)}, bf16[2,4,64,128]{3,2,1,0:T(8,128)(2,1)S(1)}, bf16[10,64,128]{2,1,0:T(8,128)(2,1)S(1)}, bf16[10,64...) custom-call(s32[4]{0:T(128)S(1)} %copy-done.5, ...), custom_call_target="tpu_custom_call" | custom-call | flops 600000000 | bytes 2000000 | tf_op jit(solution)/shard_map/pallas_call | solution.py:675
  45.0 0.1 collective-permute-start.12
  45.1 3.4 %collective-permute-start.13 = (bf16[10,64,128]{2,1,0:T(8,128)(2,1)S(1)}, bf16[10,64,128]{2,1,0:T(8,128)(2,1)S(1)}, u32[]{:S(2)}, u32[]{:S(2)}) collective-permute-start(bf16[10,64,128]{2,1,0:T(8,128)(2,1)S(1)} %get-tuple-element.66), channel_id=1, source_target_pairs={{0,1},{1,0},{2,3},{3,2},{4,5},{5,4},{6,7},{7,6},{8,16},{9,17},{10,... | collective-permute-start | bytes 491528 | tf_op jit(solution)/shard_map/ppermute | solution.py:588
  48.5 2.8 %collective-permute-done.12.one_ref = bf16[10,64,128]{2,1,0:T(8,128)(2,1)S(1)} collective-permute-done((bf16[10,64,128]{2,1,0:T(8,128)(2,1)S(1)}, bf16[10,64,128]{2,1,0:T(8,128)(2,1)S(1)}, u32[]{:S(2)}, u32[]{:S(2)}) %collective-permute-start.12) | collective-permute-done | bytes 163872 | tf_op jit(solution)/shard_map/ppermute | solution.py:588
  51.3 2.2 %collective-permute-done.13.two_ref = bf16[10,64,128]{2,1,0:T(8,128)(2,1)S(1)} collective-permute-done((bf16[10,64,128]{2,1,0:T(8,128)(2,1)S(1)}, bf16[10,64,128]{2,1,0:T(8,128)(2,1)S(1)}, u32[]{:S(2)}, u32[]{:S(2)}) %collective-permute-start.13) | collective-permute-done | bytes 163872 | tf_op jit(solution)/shard_map/ppermute | solution.py:588
  53.5 0.7 shard_map.107
  54.2 0.1 collective-permute-start.14
  54.3 0.3 collective-permute-start.15
  54.6 1.2 %collective-permute-done.14.y_one_ref = bf16[15,64,128]{2,1,0:T(8,128)(2,1)S(1)} collective-permute-done((bf16[15,64,128]{2,1,0:T(8,128)(2,1)S(1)}, bf16[15,64,128]{2,1,0:T(8,128)(2,1)S(1)}, u32[]{:S(2)}, u32[]{:S(2)}) %collective-permute-start.14) | collective-permute-done | bytes 245792 | tf_op jit(solution)/shard_map/ppermute | solution.py:588
  55.8 5.0 %collective-permute-done.15.y_two_ref = bf16[15,64,128]{2,1,0:T(8,128)(2,1)S(1)} collective-permute-done((bf16[15,64,128]{2,1,0:T(8,128)(2,1)S(1)}, bf16[15,64,128]{2,1,0:T(8,128)(2,1)S(1)}, u32[]{:S(2)}, u32[]{:S(2)}) %collective-permute-start.15) | collective-permute-done | bytes 245792 | tf_op jit(solution)/shard_map/ppermute | solution.py:588
  60.8 3.3 %shard_map.108 = (f32[3,32,128]{2,1,0:T(8,128)S(1)}, bf16[3,32,128]{2,1,0:T(8,128)(2,1)S(1)}) custom-call(s32[4]{0:T(128)S(1)} %copy-done.5, bf16[4,8,64,128]{3,2,1,0:T(8,128)(2,1)S(1)} %get-tuple-element.63.act_ref, bf16[2,4,64,128]{3,2,1,0:T(8,128)(2,1)S(1)} %get-tuple-element.64.coarse_ref, bf16[10,64,128]{2,1,0:T(8,128)(2,1)S(1)} %get-tuple-element.69.xl_ref, ...), custom_call_target="tpu_custom_call" | custom-call | flops 1300000000 | bytes 2000000 | tf_op jit(solution)/shard_map/pallas_call | solution.py:704
  64.1 3.4 %collective-permute-start.17 = (bf16[3,32,128]{2,1,0:T(8,128)(2,1)S(1)}, bf16[3,32,128]{2,1,0:T(8,128)(2,1)S(1)}, u32[]{:S(2)}, u32[]{:S(2)}) collective-permute-start(bf16[3,32,128]{2,1,0:T(8,128)(2,1)S(1)} %get-tuple-element.74.own_ref), channel_id=1, source_target_pairs={{0,1},{1,0},{2,3},{3,2},{4,5},{5,4},{6,7},{7,6},{8,16},{9,17},{10,... | collective-permute-start | bytes 73736 | tf_op jit(solution)/shard_map/ppermute | solution.py:588
  67.5 2.6 %collective-permute-done.17.two_ref = bf16[3,32,128]{2,1,0:T(8,128)(2,1)S(1)} collective-permute-done((bf16[3,32,128]{2,1,0:T(8,128)(2,1)S(1)}, bf16[3,32,128]{2,1,0:T(8,128)(2,1)S(1)}, u32[]{:S(2)}, u32[]{:S(2)}) %collective-permute-start.17) | collective-permute-done | bytes 24608 | tf_op jit(solution)/shard_map/ppermute | solution.py:588
  70.2 1.2 %collective-permute-done.16.one_ref = bf16[3,32,128]{2,1,0:T(8,128)(2,1)S(1)} collective-permute-done((bf16[3,32,128]{2,1,0:T(8,128)(2,1)S(1)}, bf16[3,32,128]{2,1,0:T(8,128)(2,1)S(1)}, u32[]{:S(2)}, u32[]{:S(2)}) %collective-permute-start.16) | collective-permute-done | bytes 24608 | tf_op jit(solution)/shard_map/ppermute | solution.py:588
  71.3 0.6 shard_map.109.row_ref
  71.9 0.1 collective-permute-start.19
  72.0 0.1 collective-permute-start.18
  72.1 4.2 %collective-permute-done.19.y_two_ref = bf16[3,3,32,128]{3,2,1,0:T(8,128)(2,1)S(1)} collective-permute-done((bf16[3,3,32,128]{3,2,1,0:T(8,128)(2,1)S(1)}, bf16[3,3,32,128]{3,2,1,0:T(8,128)(2,1)S(1)}, u32[]{:S(2)}, u32[]{:S(2)}) %collective-permute-start.19) | collective-permute-done | bytes 73760 | tf_op jit(solution)/shard_map/ppermute | solution.py:588
  76.4 1.4 %shard_map.110 = f32[16,3,128]{2,1,0:T(4,128)S(1)} custom-call(s32[4]{0:T(128)S(1)} %copy-done.5, s32[16]{0:T(128)S(1)} %copy-done.6, s32[32]{0:T(128)S(1)} %copy-done.7, s32[32]{0:T(128)S(1)} %bitcast.20, f32[3,32,128]{2,1,0:T(8,128)S(1)} %get-tuple-element.73.own_ref, bf16[3,3,32,128]{3,2,1,0:T(8,128)(2,1)S(1)} %shard_map.109.row_ref, ...), custom_call_target="tpu_custom_call" | custom-call | flops 70000000 | bytes 2000000 | tf_op jit(solution)/shard_map/pallas_call | solution.py:728
  77.8 0.6 copy.14
  (43 shorter events, 0.3 us)
Async XLA Ops:
  0.0 32.4 %copy-start = (bf16[3,64,576]{2,1,0:T(8,128)(2,1)S(1)}, bf16[3,64,576]{2,1,0:T(8,128)(2,1)}, u32[]{:S(2)}) copy-start(bf16[3,64,576]{2,1,0:T(8,128)(2,1)} %param.18) | copy-start | bytes 663556
  4.7 10.1 %collective-permute-start.4 = (bf16[528,128]{1,0:T(8,128)(2,1)}, bf16[528,128]{1,0:T(8,128)(2,1)S(1)}, u32[]{:S(2)}, u32[]{:S(2)}) collective-permute-start(bf16[528,128]{1,0:T(8,128)(2,1)} %get-tuple-element.49), channel_id=1, source_target_pairs={{0,8},{1,9},{2,10},{3,11},{4,12},{5,13},{6,14},{7,15},{8,0},{9,1},... | collective-permute-start | bytes 405512 | tf_op jit(solution)/shard_map/ppermute | solution.py:588
  6.7 10.1 %collective-permute-start.5 = (bf16[528,128]{1,0:T(8,128)(2,1)}, bf16[528,128]{1,0:T(8,128)(2,1)S(1)}, u32[]{:S(2)}, u32[]{:S(2)}) collective-permute-start(bf16[528,128]{1,0:T(8,128)(2,1)} %get-tuple-element.50), channel_id=1, source_target_pairs={{0,1},{1,0},{2,3},{3,2},{4,5},{5,4},{6,7},{7,6},{8,16},{9,17},{10,... | collective-permute-start | bytes 405512 | tf_op jit(solution)/shard_map/ppermute | solution.py:588
  9.1 10.1 %collective-permute-start.6 = (bf16[528,128]{1,0:T(8,128)(2,1)}, bf16[528,128]{1,0:T(8,128)(2,1)S(1)}, u32[]{:S(2)}, u32[]{:S(2)}) collective-permute-start(bf16[528,128]{1,0:T(8,128)(2,1)} %get-tuple-element.51), channel_id=1, source_target_pairs={{0,1},{1,0},{2,3},{3,2},{4,5},{5,4},{6,7},{7,6},{8,9},{9,8},{10,11... | collective-permute-start | bytes 405512 | tf_op jit(solution)/shard_map/ppermute | solution.py:588
  9.1 10.7 %collective-permute-start.7 = (bf16[528,128]{1,0:T(8,128)(2,1)}, bf16[528,128]{1,0:T(8,128)(2,1)S(1)}, u32[]{:S(2)}, u32[]{:S(2)}) collective-permute-start(bf16[528,128]{1,0:T(8,128)(2,1)} %get-tuple-element.52), channel_id=1, source_target_pairs={{0,8},{1,2},{2,1},{3,4},{4,3},{5,6},{6,5},{7,15},{8,0},{9,10},{10,... | collective-permute-start | bytes 405512 | tf_op jit(solution)/shard_map/ppermute | solution.py:588
  10.2 0.6 copy-start.4
  10.8 0.9 %copy-start.10 = (bf16[528,128]{1,0:T(8,128)(2,1)S(1)}, bf16[528,128]{1,0:T(8,128)(2,1)}, u32[]{:S(2)}) copy-start(bf16[528,128]{1,0:T(8,128)(2,1)} %get-tuple-element.44.refs_1_) | copy-start | bytes 405508
  11.7 1.8 %copy-start.15 = (bf16[528,128]{1,0:T(8,128)(2,1)S(1)}, bf16[528,128]{1,0:T(8,128)(2,1)}, u32[]{:S(2)}) copy-start(bf16[528,128]{1,0:T(8,128)(2,1)} %get-tuple-element.45) | copy-start | bytes 405508
  11.7 3.1 %copy-start.14 = (bf16[528,128]{1,0:T(8,128)(2,1)S(1)}, bf16[528,128]{1,0:T(8,128)(2,1)}, u32[]{:S(2)}) copy-start(bf16[528,128]{1,0:T(8,128)(2,1)} %get-tuple-element.46) | copy-start | bytes 405508
  11.7 5.1 %copy-start.13 = (bf16[528,128]{1,0:T(8,128)(2,1)S(1)}, bf16[528,128]{1,0:T(8,128)(2,1)}, u32[]{:S(2)}) copy-start(bf16[528,128]{1,0:T(8,128)(2,1)} %get-tuple-element.47) | copy-start | bytes 405508
  11.7 7.5 %copy-start.12 = (bf16[528,128]{1,0:T(8,128)(2,1)S(1)}, bf16[528,128]{1,0:T(8,128)(2,1)}, u32[]{:S(2)}) copy-start(bf16[528,128]{1,0:T(8,128)(2,1)} %get-tuple-element.48) | copy-start | bytes 405508
  13.5 8.5 %collective-permute-start = (bf16[528,128]{1,0:T(8,128)(2,1)S(1)}, bf16[528,128]{1,0:T(8,128)(2,1)S(1)}, u32[]{:S(2)}, u32[]{:S(2)}) collective-permute-start(bf16[528,128]{1,0:T(8,128)(2,1)S(1)} %copy-done.15), channel_id=1, source_target_pairs={{0,9},{1,10},{2,11},{3,12},{4,13},{5,14},{6,15},{7,23},{8,24},{9,0... | collective-permute-start | bytes 405512 | tf_op jit(solution)/shard_map/ppermute | solution.py:588
  14.8 8.7 %collective-permute-start.1 = (bf16[528,128]{1,0:T(8,128)(2,1)S(1)}, bf16[528,128]{1,0:T(8,128)(2,1)S(1)}, u32[]{:S(2)}, u32[]{:S(2)}) collective-permute-start(bf16[528,128]{1,0:T(8,128)(2,1)S(1)} %copy-done.14), channel_id=1, source_target_pairs={{0,1},{1,0},{2,3},{3,2},{4,5},{5,4},{6,7},{7,6},{8,17},{9,18},{10,... | collective-permute-start | bytes 405512 | tf_op jit(solution)/shard_map/ppermute | solution.py:588
  16.8 9.2 %collective-permute-start.2 = (bf16[528,128]{1,0:T(8,128)(2,1)S(1)}, bf16[528,128]{1,0:T(8,128)(2,1)S(1)}, u32[]{:S(2)}, u32[]{:S(2)}) collective-permute-start(bf16[528,128]{1,0:T(8,128)(2,1)S(1)} %copy-done.13), channel_id=1, source_target_pairs={{0,15},{1,8},{2,9},{3,10},{4,11},{5,12},{6,13},{7,14},{8,1},{9,2},... | collective-permute-start | bytes 405512 | tf_op jit(solution)/shard_map/ppermute | solution.py:588
  19.2 8.6 %collective-permute-start.3 = (bf16[528,128]{1,0:T(8,128)(2,1)S(1)}, bf16[528,128]{1,0:T(8,128)(2,1)S(1)}, u32[]{:S(2)}, u32[]{:S(2)}) collective-permute-start(bf16[528,128]{1,0:T(8,128)(2,1)S(1)} %copy-done.12), channel_id=1, source_target_pairs={{0,1},{1,0},{2,3},{3,2},{4,5},{5,4},{6,7},{7,6},{8,24},{9,16},{10,... | collective-permute-start | bytes 405512 | tf_op jit(solution)/shard_map/ppermute | solution.py:588
  19.7 12.7 %copy-start.11 = (f32[3,64]{1,0:T(4,128)S(1)}, f32[3,64]{1,0:T(4,128)}, u32[]{:S(2)}) copy-start(f32[3,64]{1,0:T(4,128)} %param.19) | copy-start | bytes 2308
  22.0 16.6 %copy-start.2 = (bf16[3,64,576]{2,1,0:T(8,128)(2,1)S(1)}, bf16[3,64,576]{2,1,0:T(8,128)(2,1)}, u32[]{:S(2)}) copy-start(bf16[3,64,576]{2,1,0:T(8,128)(2,1)} %param.16) | copy-start | bytes 663556
  29.6 5.4 %collective-permute-start.8 = (bf16[8,64,128]{2,1,0:T(8,128)(2,1)S(1)}, bf16[8,64,128]{2,1,0:T(8,128)(2,1)S(1)}, u32[]{:S(2)}, u32[]{:S(2)}) collective-permute-start(bf16[8,64,128]{2,1,0:T(8,128)(2,1)S(1)} %get-tuple-element.55), channel_id=1, source_target_pairs={{0,8},{1,9},{2,10},{3,11},{4,12},{5,13},{6,14},{7,15},{8,0},{9,1},... | collective-permute-start | bytes 393224 | tf_op jit(solution)/shard_map/ppermute | solution.py:588
  29.7 7.9 %collective-permute-start.9 = (bf16[8,64,128]{2,1,0:T(8,128)(2,1)S(1)}, bf16[8,64,128]{2,1,0:T(8,128)(2,1)S(1)}, u32[]{:S(2)}, u32[]{:S(2)}) collective-permute-start(bf16[8,64,128]{2,1,0:T(8,128)(2,1)S(1)} %get-tuple-element.56), channel_id=1, source_target_pairs={{0,1},{1,0},{2,3},{3,2},{4,5},{5,4},{6,7},{7,6},{8,16},{9,17},{10,... | collective-permute-start | bytes 393224 | tf_op jit(solution)/shard_map/ppermute | solution.py:588
  37.5 5.4 %copy-start.5 = (s32[4]{0:T(128)S(1)}, s32[4]{0:T(128)}, u32[]{:S(2)}) copy-start(s32[4]{0:T(128)} %pad_add_fusion.where_ref.refs_0_) | copy-start | bytes 52
  38.2 1.9 %collective-permute-start.10 = (bf16[6,64,128]{2,1,0:T(8,128)(2,1)S(1)}, bf16[6,64,128]{2,1,0:T(8,128)(2,1)S(1)}, u32[]{:S(2)}, u32[]{:S(2)}) collective-permute-start(bf16[6,64,128]{2,1,0:T(8,128)(2,1)S(1)} %get-tuple-element.61), channel_id=1, source_target_pairs={{0,1},{1,0},{2,3},{3,2},{4,5},{5,4},{6,7},{7,6},{8,9},{9,8},{10,11... | collective-permute-start | bytes 294920 | tf_op jit(solution)/shard_map/ppermute | solution.py:588
  38.3 4.7 %collective-permute-start.11 = (bf16[6,64,128]{2,1,0:T(8,128)(2,1)S(1)}, bf16[6,64,128]{2,1,0:T(8,128)(2,1)S(1)}, u32[]{:S(2)}, u32[]{:S(2)}) collective-permute-start(bf16[6,64,128]{2,1,0:T(8,128)(2,1)S(1)} %get-tuple-element.62), channel_id=1, source_target_pairs={{0,8},{1,2},{2,1},{3,4},{4,3},{5,6},{6,5},{7,15},{8,0},{9,10},{10,... | collective-permute-start | bytes 294920 | tf_op jit(solution)/shard_map/ppermute | solution.py:588
  40.1 20.7 %copy-start.9 = (bf16[3,64,576]{2,1,0:T(8,128)(2,1)S(1)}, bf16[3,64,576]{2,1,0:T(8,128)(2,1)}, u32[]{:S(2)}) copy-start(bf16[3,64,576]{2,1,0:T(8,128)(2,1)} %param.17) | copy-start | bytes 663556
  45.0 6.3 %collective-permute-start.12 = (bf16[10,64,128]{2,1,0:T(8,128)(2,1)S(1)}, bf16[10,64,128]{2,1,0:T(8,128)(2,1)S(1)}, u32[]{:S(2)}, u32[]{:S(2)}) collective-permute-start(bf16[10,64,128]{2,1,0:T(8,128)(2,1)S(1)} %get-tuple-element.65), channel_id=1, source_target_pairs={{0,8},{1,9},{2,10},{3,11},{4,12},{5,13},{6,14},{7,15},{8,0},{9,1},... | collective-permute-start | bytes 491528 | tf_op jit(solution)/shard_map/ppermute | solution.py:588
  45.1 8.4 %collective-permute-start.13 = (bf16[10,64,128]{2,1,0:T(8,128)(2,1)S(1)}, bf16[10,64,128]{2,1,0:T(8,128)(2,1)S(1)}, u32[]{:S(2)}, u32[]{:S(2)}) collective-permute-start(bf16[10,64,128]{2,1,0:T(8,128)(2,1)S(1)} %get-tuple-element.66), channel_id=1, source_target_pairs={{0,1},{1,0},{2,3},{3,2},{4,5},{5,4},{6,7},{7,6},{8,16},{9,17},{10,... | collective-permute-start | bytes 491528 | tf_op jit(solution)/shard_map/ppermute | solution.py:588
  54.2 1.6 %collective-permute-start.14 = (bf16[15,64,128]{2,1,0:T(8,128)(2,1)S(1)}, bf16[15,64,128]{2,1,0:T(8,128)(2,1)S(1)}, u32[]{:S(2)}, u32[]{:S(2)}) collective-permute-start(bf16[15,64,128]{2,1,0:T(8,128)(2,1)S(1)} %get-tuple-element.71), channel_id=1, source_target_pairs={{0,1},{1,0},{2,3},{3,2},{4,5},{5,4},{6,7},{7,6},{8,9},{9,8},{10,11... | collective-permute-start | bytes 737288 | tf_op jit(solution)/shard_map/ppermute | solution.py:588
  54.3 6.5 %collective-permute-start.15 = (bf16[15,64,128]{2,1,0:T(8,128)(2,1)S(1)}, bf16[15,64,128]{2,1,0:T(8,128)(2,1)S(1)}, u32[]{:S(2)}, u32[]{:S(2)}) collective-permute-start(bf16[15,64,128]{2,1,0:T(8,128)(2,1)S(1)} %get-tuple-element.72), channel_id=1, source_target_pairs={{0,8},{1,2},{2,1},{3,4},{4,3},{5,6},{6,5},{7,15},{8,0},{9,10},{10,... | collective-permute-start | bytes 737288 | tf_op jit(solution)/shard_map/ppermute | solution.py:588
  60.8 15.6 %copy-start.1 = (bf16[32,128,128]{2,1,0:T(8,128)(2,1)S(1)}, bf16[32,128,128]{2,1,0:T(8,128)(2,1)}, u32[]{:S(2)}) copy-start(bf16[32,128,128]{2,1,0:T(8,128)(2,1)} %weight_ref.1) | copy-start | bytes 3145732
  60.8 15.6 %copy-start.3 = (s32[32,128]{1,0:T(8,128)S(1)}, s32[32,128]{1,0:T(8,128)}, u32[]{:S(2)}) copy-start(s32[32,128]{1,0:T(8,128)} %nodes_ref.3) | copy-start | bytes 49156
  60.8 15.6 %copy-start.6 = (s32[16]{0:T(128)S(1)}, s32[16]{0:T(128)}, u32[]{:S(2)}) copy-start(s32[16]{0:T(128)} %counts_ref.3) | copy-start | bytes 196
  60.8 15.6 %copy-start.7 = (s32[32]{0:T(128)S(1)}, s32[32]{0:T(128)}, u32[]{:S(2)}) copy-start(s32[32]{0:T(128)} %block_ref.3) | copy-start | bytes 388
  60.8 15.6 %copy-start.8 = (s32[32,1]{0,1:T(1,128)S(1)}, s32[32,1]{0,1:T(1,128)}, u32[]{:S(2)}) copy-start(s32[32,1]{0,1:T(1,128)} %param.13) | copy-start | bytes 388
  64.1 6.0 %collective-permute-start.17 = (bf16[3,32,128]{2,1,0:T(8,128)(2,1)S(1)}, bf16[3,32,128]{2,1,0:T(8,128)(2,1)S(1)}, u32[]{:S(2)}, u32[]{:S(2)}) collective-permute-start(bf16[3,32,128]{2,1,0:T(8,128)(2,1)S(1)} %get-tuple-element.74.own_ref), channel_id=1, source_target_pairs={{0,1},{1,0},{2,3},{3,2},{4,5},{5,4},{6,7},{7,6},{8,16},{9,17},{10,... | collective-permute-start | bytes 73736 | tf_op jit(solution)/shard_map/ppermute | solution.py:588
  67.5 3.8 %collective-permute-start.16 = (bf16[3,32,128]{2,1,0:T(8,128)(2,1)S(1)}, bf16[3,32,128]{2,1,0:T(8,128)(2,1)S(1)}, u32[]{:S(2)}, u32[]{:S(2)}) collective-permute-start(bf16[3,32,128]{2,1,0:T(8,128)(2,1)S(1)} %get-tuple-element.74.own_ref), channel_id=1, source_target_pairs={{0,8},{1,9},{2,10},{3,11},{4,12},{5,13},{6,14},{7,15},{8,0},{9,1},... | collective-permute-start | bytes 73736 | tf_op jit(solution)/shard_map/ppermute | solution.py:588
  71.9 4.4 %collective-permute-start.19 = (bf16[3,3,32,128]{3,2,1,0:T(8,128)(2,1)S(1)}, bf16[3,3,32,128]{3,2,1,0:T(8,128)(2,1)S(1)}, u32[]{:S(2)}, u32[]{:S(2)}) collective-permute-start(bf16[3,3,32,128]{3,2,1,0:T(8,128)(2,1)S(1)} %shard_map.109.row_ref), channel_id=1, source_target_pairs={{0,8},{1,2},{2,1},{3,4},{4,3},{5,6},{6,5},{7,15},{8,0},{9,10},{10,... | collective-permute-start | bytes 221192 | tf_op jit(solution)/shard_map/ppermute | solution.py:588
  72.0 4.3 %collective-permute-start.18 = (bf16[3,3,32,128]{3,2,1,0:T(8,128)(2,1)S(1)}, bf16[3,3,32,128]{3,2,1,0:T(8,128)(2,1)S(1)}, u32[]{:S(2)}, u32[]{:S(2)}) collective-permute-start(bf16[3,3,32,128]{3,2,1,0:T(8,128)(2,1)S(1)} %shard_map.109.row_ref), channel_id=1, source_target_pairs={{0,1},{1,0},{2,3},{3,2},{4,5},{5,4},{6,7},{7,6},{8,9},{9,8},{10,11... | collective-permute-start | bytes 221192 | tf_op jit(solution)/shard_map/ppermute | solution.py:588

commit v2 on v1

--- a/solution.py
+++ b/solution.py
@@ -39,7 +39,7 @@
 
 
 def partial_kernel(
-    where_ref, counts_ref, block_ref, dest_ref, feat_hbm, nodes_ref, weight_hbm, *rest
+    counts_ref, block_ref, dest_ref, feat_hbm, nodes_ref, weight_hbm, *rest
 ):
     outs = rest[:9]
     feat_ref, weight_ref, sem, part, hi_all, lo_all, index, taken, entry_of = rest[9:]
@@ -60,10 +60,10 @@
 
     def place(e, carry):
         tile = dest_ref[e]
-        step_x = tile // where_ref[2] - where_ref[0]
-        step_y = tile % where_ref[2] - where_ref[1]
-        odd_x = where_ref[0] % 2
-        odd_y = where_ref[1] % 2
+        step_x = tile // lax.axis_size("gy") - lax.axis_index("gx")
+        step_y = tile % lax.axis_size("gy") - lax.axis_index("gy")
+        odd_x = lax.axis_index("gx") % 2
+        odd_y = lax.axis_index("gy") % 2
         by_x = jnp.where(step_x > 0, odd_x, 1 - odd_x)
         by_y = jnp.where(step_y > 0, odd_y, 1 - odd_y)
         d = jnp.where(step_x == step_y, 5 + by_x, 7 + by_x)
@@ -97,9 +97,8 @@
 
 
 def scatter_kernel(parts, first, last, *refs):
-    where_ref = refs[0]
-    got = refs[1 : parts + 1]
-    refs = refs[parts + 1 :]
+    got = refs[:parts]
+    refs = refs[parts:]
     if not first:
         before = refs[0]
         refs = refs[1:]
@@ -155,7 +154,7 @@
             x = t // 4
             y = (t % 4) * 2 + half
             grid_ref[x, y] = column
-    odd = where_ref[0] % 2
+    odd = lax.axis_index("gx") % 2
 
     @pl.when(odd == 0)
     def _():
@@ -168,7 +167,7 @@
         two_ref[...] = grid_ref[TILE_X - 1]
 
 
-def scatter(where, parts, before, last):
+def scatter(parts, before, last):
     most = len(parts) * SLOTS + GROUP
     sums = ((16 * CHAN, 256), F32)
     first = before is None
@@ -179,7 +178,7 @@
     return call(
         functools.partial(scatter_kernel, len(parts), first, last),
         outs,
-        [SM] + [VM] * (len(parts) + (not first)),
+        [VM] * (len(parts) + (not first)),
         [
             pltpu.VMEM((most, CHAN, LANES), BF),
             pltpu.VMEM((len(parts) * 16, LANES), F32),
@@ -188,7 +187,7 @@
         ]
         + [pltpu.VMEM(*sums)] * last,
         800000000,
-    )(where, *parts, *([] if first else [before]))
+    )(*parts, *([] if first else [before]))
 
 
 def shifted(column):
@@ -224,11 +223,13 @@
     return v / (1.0 + jnp.exp(-v))
 
 
-def edges(where_ref):
-    x_lo = where_ref[0] > 0
-    x_hi = where_ref[0] < where_ref[3] - 1
-    y_lo = where_ref[1] > 0
-    y_hi = where_ref[1] < where_ref[2] - 1
+def edges():
+    index_x = lax.axis_index("gx")
+    index_y = lax.axis_index("gy")
+    x_lo = index_x > 0
+    x_hi = index_x < lax.axis_size("gx") - 1
+    y_lo = index_y > 0
+    y_hi = index_y < lax.axis_size("gy") - 1
     return x_lo, x_hi, y_lo, y_hi
 
 
@@ -244,9 +245,9 @@
         two_ref[...] = high_ref[...]
 
 
-def sorted_x(where_ref, one_ref, two_ref, xl_ref, xh_ref):
-    x_lo, x_hi, _, _ = edges(where_ref)
-    odd = where_ref[0] % 2 == 1
+def sorted_x(one_ref, two_ref, xl_ref, xh_ref):
+    x_lo, x_hi, _, _ = edges()
+    odd = lax.axis_index("gx") % 2 == 1
     for i in range(xl_ref.shape[0]):
         one = one_ref[i].astype(F32)
         two = two_ref[i].astype(F32)
@@ -254,9 +255,9 @@
         xh_ref[i] = jnp.where(x_hi, jnp.where(odd, two, one), 0.0).astype(BF)
 
 
-def sorted_y(where_ref, one_ref, two_ref, i):
-    _, _, y_lo, y_hi = edges(where_ref)
-    odd = where_ref[1] % 2 == 1
+def sorted_y(one_ref, two_ref, i):
+    _, _, y_lo, y_hi = edges()
+    odd = lax.axis_index("gy") % 2 == 1
     one = one_ref[i].astype(F32)
     two = two_ref[i].astype(F32)
     lower = jnp.where(y_lo, jnp.where(odd, one, two), 0.0).astype(BF)
@@ -265,37 +266,37 @@
 
 
 def grid_side_kernel(
-    where_ref, one_ref, two_ref, grid_ref, xl_ref, xh_ref, y_one_ref, y_two_ref, low, high
+    one_ref, two_ref, grid_ref, xl_ref, xh_ref, y_one_ref, y_two_ref, low, high
 ):
-    sorted_x(where_ref, one_ref, two_ref, xl_ref, xh_ref)
+    sorted_x(one_ref, two_ref, xl_ref, xh_ref)
     for ref, y in ((low, 0), (high, TILE_Y - 1)):
         ref[0] = xl_ref[y]
         for x in range(TILE_X):
             ref[x + 1] = grid_ref[x, y]
         ref[TILE_X + 1] = xh_ref[y]
-    in_order(where_ref[1] % 2, y_one_ref, y_two_ref, low, high)
+    in_order(lax.axis_index("gy") % 2, y_one_ref, y_two_ref, low, high)
 
 
 def coarse_side_kernel(
-    where_ref, one_ref, two_ref, coarse_ref, down_ref, up_ref,
+    one_ref, two_ref, coarse_ref, down_ref, up_ref,
     xl_ref, xh_ref, y_one_ref, y_two_ref, low, high,
 ):
-    sorted_x(where_ref, one_ref, two_ref, xl_ref, xh_ref)
+    sorted_x(one_ref, two_ref, xl_ref, xh_ref)
     half_y = TILE_Y // 2
-    for ref, y, own in ((low, 0, down_ref), (high, half_y - 2, up_ref)):
+    left = xl_ref[8].astype(F32)
+    right = xh_ref[8].astype(F32)
+    for ref, y, own, row in ((low, 0, down_ref, 48), (high, half_y - 2, up_ref, 54)):
         for x in range(2):
             for k in range(2):
                 ref[x * 2 + k] = xl_ref[x * half_y + y + k]
                 ref[4 + x * 2 + k] = coarse_ref[x, y + k]
                 ref[8 + x * 2 + k] = xh_ref[x * half_y + y + k]
-        ref[12] = own[0]
-        ref[13] = xl_ref[9]
-        ref[14] = xh_ref[9]
-    in_order(where_ref[1] % 2, y_one_ref, y_two_ref, low, high)
-
-
-def field_side_kernel(where_ref, one_ref, two_ref, own_ref, row_ref):
-    odd = where_ref[0] % 2
+        ref[12] = filled_up([own[...], left[row : row + 6], right[row : row + 6]])
+    in_order(lax.axis_index("gy") % 2, y_one_ref, y_two_ref, low, high)
+
+
+def field_side_kernel(one_ref, two_ref, own_ref, row_ref):
+    odd = lax.axis_index("gx") % 2
     row_ref[1] = own_ref[...]
 
     @pl.when(odd == 0)
@@ -343,20 +344,24 @@
 
 def two_parts(value):
     high = value.astype(BF).astype(F32)
-    return jnp.concatenate([high, value - high, jnp.zeros((2, LANES), F32)], axis=0)
-
-
-def one_part(column, row):
-    piece = column[row : row + 8]
-    return piece[0:3] + piece[3:6]
+    return jnp.concatenate([high, value - high], axis=0)
+
+
+def filled_up(pieces):
+    rest = CHAN - sum(piece.shape[0] for piece in pieces)
+    return jnp.concatenate(pieces + [jnp.zeros((rest, LANES), F32)], axis=0).astype(BF)
+
+
+def added(pieces):
+    return functools.reduce(lambda one, two: one + two, pieces)
 
 
 def outer_conv_kernel(
-    where_ref, grid_ref, stack, inner_ref, y_one_ref, y_two_ref, weight_ref, out_weight_ref,
-    act_ref, coarse_ref, one_ref, two_ref, down_ref, up_ref, edge, taps, low_ref, high_ref,
+    grid_ref, stack, inner_ref, y_one_ref, y_two_ref, weight_ref, out_weight_ref,
+    act_ref, coarse_ref, one_ref, two_ref, edge, taps, low_ref, high_ref,
 ):
     for x in range(TILE_X + 2):
-        lower, higher = sorted_y(where_ref, y_one_ref, y_two_ref, x)
+        lower, higher = sorted_y(y_one_ref, y_two_ref, x)
         edge[x, 0] = shifted(lower)
         edge[x, 1] = shifted(higher)
     last_y = TILE_Y - 1
@@ -389,133 +394,172 @@
             coarse_ref[x, y] = result
             low_ref[x * half_y + y] = result
             high_ref[x * half_y + y] = result
-    pairs = []
-    for x in (0, TILE_X - 1):
-        pairs += [((x, y), (x, y + 1)) for y in range(0, TILE_Y, 2)]
-    pairs += [((1, y), (2, y)) for y in (0, last_y)]
+    for side, ref, x, a in ((0, low_ref, 0, 2), (1, high_ref, TILE_X - 1, 0)):
+        weight = out_weight_ref[a * 72 : a * 72 + 72]
+        for y in range(0, TILE_Y, 2):
+            rhs = jnp.concatenate([act_ref[x, y], act_ref[x, y + 1]], axis=1)
+            prod = jnp.dot(weight, rhs, preferred_element_type=F32)
+            taps[side, y] = prod[:, :LANES]
+            taps[side, y + 1] = prod[:, LANES:]
+        cells = []
+        for y in [*range(TILE_Y), -1, TILE_Y]:
+            near = [(y + b - 1, b) for b in range(3) if 0 <= y + b - 1 < TILE_Y]
+            total = added([taps[side, v, b * 24 : b * 24 + 24, :] for v, b in near])
+            cells.append(two_parts(joined(total)))
+        ref[8] = filled_up(cells)
+    in_order(lax.axis_index("gx") % 2, one_ref, two_ref, low_ref, high_ref)
+
+
+def rim_kernel(act_ref, out_weight_ref, down_ref, up_ref, taps):
     weight = out_weight_ref[...]
-    for first, second in pairs:
-        rhs = jnp.concatenate([act_ref[first], act_ref[second]], axis=1)
-        prod = jnp.dot(weight, rhs, preferred_element_type=F32)
-        taps[first] = prod[:, :LANES]
-        taps[second] = prod[:, LANES:]
-
-    def outside(cells):
-        total = None
-        for x, y, a, b in cells:
-            if 0 <= x < TILE_X and 0 <= y < TILE_Y:
-                start = (a * 3 + b) * 24
-                piece = taps[x, y, start : start + 24, :]
-                total = piece if total is None else total + piece
-        return two_parts(joined(total))
-
-    def column(pieces):
-        rest = CHAN - 8 * len(pieces)
-        if rest:
-            pieces = pieces + [jnp.zeros((rest, LANES), F32)]
-        return jnp.concatenate(pieces, axis=0).astype(BF)
-
-    for ref, x, a in ((low_ref, 0, 2), (high_ref, TILE_X - 1, 0)):
-        cells = [
-            outside([(x, y + b - 1, a, b) for b in range(3)]) for y in range(-1, TILE_Y + 1)
-        ]
-        ref[8] = column(cells[1:-1])
-        ref[9] = column([cells[0], cells[-1]])
-    for ref, y, b in ((down_ref, 0, 2), (up_ref, last_y, 0)):
-        ref[0] = column(
-            [outside([(x + a - 1, y, a, b) for a in range(3)]) for x in range(TILE_X)]
-        )
-    in_order(where_ref[0] % 2, one_ref, two_ref, low_ref, high_ref)
-
-
-def second_conv_kernel(
-    where_ref, act_ref, coarse_ref, xl_ref, xh_ref, y_one_ref, y_two_ref,
-    mid_weight_ref, out_weight_ref,
-    field_ref, sent_ref, stack, merged, mid_ref, taps, yl_ref, yh_ref,
+    for ref, y, b in ((down_ref, 0, 2), (up_ref, TILE_Y - 1, 0)):
+        for x in range(0, TILE_X, 2):
+            rhs = jnp.concatenate([act_ref[x, y], act_ref[x + 1, y]], axis=1)
+            prod = jnp.dot(weight, rhs, preferred_element_type=F32)
+            taps[x] = prod[:, :LANES]
+            taps[x + 1] = prod[:, LANES:]
+        cells = []
+        for x in range(TILE_X):
+            near = [(x + a - 1, (a * 3 + b) * 24) for a in range(3) if 0 <= x + a - 1 < TILE_X]
+            total = added([taps[u, start : start + 24, :] for u, start in near])
+            cells.append(two_parts(joined(total)))
+        ref[...] = jnp.concatenate(cells, axis=0)
+
+
+def put_taps(weight, taps, places, columns):
+    for (one, two), pair in zip(zip(places[::2], places[1::2]), zip(columns[::2], columns[1::2])):
+        prod = jnp.dot(weight, jnp.concatenate(pair, axis=1), preferred_element_type=F32)
+        taps[one] = prod[:, :LANES]
+        taps[two] = prod[:, LANES:]
+
+
+def inner_mid_kernel(
+    coarse_ref, xl_ref, xh_ref, act_ref, mid_weight_ref, out_weight_ref, stack, taps, mid_ref
 ):
-    for i in range(15):
-        yl_ref[i], yh_ref[i] = sorted_y(where_ref, y_one_ref, y_two_ref, i)
-    x_lo, x_hi, y_lo, y_hi = edges(where_ref)
+    x_lo, x_hi, _, _ = edges()
     half_x = TILE_X // 2
     half_y = TILE_Y // 2
     for x in range(half_x):
         for y in range(half_y):
-            stack[x + 2, y + 2] = shifted(coarse_ref[x, y])
-            stack[x, y + 2] = shifted(xl_ref[x * half_y + y])
-            stack[x + 2 + half_x, y + 2] = shifted(xh_ref[x * half_y + y])
+            stack[x + 2, y] = shifted(coarse_ref[x, y])
+            stack[x, y] = shifted(xl_ref[x * half_y + y])
+            stack[x + 2 + half_x, y] = shifted(xh_ref[x * half_y + y])
+
+    def picks(x):
+        return [flat(stack[x, 0:3]), flat(stack[x, 1:4])]
+
+    def put(x, value):
+        result = silu(value).astype(BF)
+        mid_ref[x, 0] = result[:, :LANES]
+        mid_ref[x, 1] = result[:, LANES:]
+
+    conv_rows(picks, mid_weight_ref, half_x + 2, put)
+    weight = out_weight_ref[...]
+    for x in range(TILE_X + 2):
+        columns = []
+        for y in range(4):
+            value = mid_ref[(x + 1) // 2, y // 2]
+            if x == 0:
+                columns.append(masked(value, x_lo))
+            elif x == TILE_X + 1:
+                columns.append(masked(value, x_hi))
+            else:
+                fine = act_ref[x - 1, y + 2].astype(F32)
+                columns.append((fine + value.astype(F32)).astype(BF))
+        put_taps(weight, taps, [(x, y) for y in range(4)], columns)
+
+
+def outer_mid_kernel(
+    act_ref, stack, inner, xl_ref, xh_ref, y_one_ref, y_two_ref, mid_weight_ref, out_weight_ref,
+    field_ref, sent_ref, edge, mid_ref, taps, yl_ref, yh_ref,
+):
+    x_lo, x_hi, y_lo, y_hi = edges()
+    half_x = TILE_X // 2
+    for i in range(13):
+        yl_ref[i], yh_ref[i] = sorted_y(y_one_ref, y_two_ref, i)
     for x in range(half_x + 4):
-        for y in range(2):
-            stack[x, y] = shifted(yl_ref[x * 2 + y])
-            stack[x, half_y + 2 + y] = shifted(yh_ref[x * 2 + y])
-    for y in range(0, half_y + 2, 2):
-
-        def picks(x, y=y):
-            return [flat(stack[x, y : y + 3]), flat(stack[x, y + 1 : y + 4])]
-
-        def put(x, value, y=y):
+        for k in range(2):
+            edge[x, k] = shifted(yl_ref[x * 2 + k])
+            edge[x, 2 + k] = shifted(yh_ref[x * 2 + k])
+    for side in range(2):
+
+        def picks(x, side=side):
+            if side == 0:
+                near = [edge[x, 0], edge[x, 1], stack[x, 0], stack[x, 1]]
+            else:
+                near = [stack[x, 2], stack[x, 3], edge[x, 2], edge[x, 3]]
+            return [jnp.concatenate(near[:3], axis=0), jnp.concatenate(near[1:], axis=0)]
+
+        def put(x, value, side=side):
             result = silu(value).astype(BF)
-            mid_ref[x, y] = result[:, :LANES]
-            mid_ref[x, y + 1] = result[:, LANES:]
+            mid_ref[x, 2 * side] = result[:, :LANES]
+            mid_ref[x, 2 * side + 1] = result[:, LANES:]
 
         conv_rows(picks, mid_weight_ref, half_x + 2, put)
+    weight = out_weight_ref[...]
+    rows = (-1, 0, 1, TILE_Y - 2, TILE_Y - 1, TILE_Y)
     for x in range(TILE_X + 2):
-        for y in range(TILE_Y + 2):
+        columns = []
+        for y, k in zip(rows, (0, 1, 1, 2, 2, 3)):
+            value = mid_ref[(x + 1) // 2, k]
             more = ()
             if x == 0:
                 more += (x_lo,)
             if x == TILE_X + 1:
                 more += (x_hi,)
-            if y == 0:
+            if y < 0:
                 more += (y_lo,)
-            if y == TILE_Y + 1:
+            if y == TILE_Y:
                 more += (y_hi,)
-            value = mid_ref[(x + 1) // 2, (y + 1) // 2]
             if more:
-                merged[x, y] = masked(value, *more)
+                columns.append(masked(value, *more))
             else:
-                merged[x, y] = (act_ref[x - 1, y - 1].astype(F32) + value.astype(F32)).astype(BF)
-    weight = out_weight_ref[...]
-    for x in range(TILE_X + 2):
-        for y in range(0, TILE_Y + 2, 2):
-            pair = jnp.concatenate([merged[x, y], merged[x, y + 1]], axis=1)
-            prod = jnp.dot(weight, pair, preferred_element_type=F32)
-            taps[x, y] = prod[:, :LANES]
-            taps[x, y + 1] = prod[:, LANES:]
+                fine = act_ref[x - 1, y].astype(F32)
+                columns.append((fine + value.astype(F32)).astype(BF))
+        put_taps(weight, taps, [(x, k) for k in range(6)], columns)
+
+    def tap(x, y, start):
+        if y in rows:
+            return taps[x, rows.index(y), start : start + 24, :]
+        return inner[x, y - 2, start : start + 24, :]
 
     def received(ref, place, row):
-        return one_part(ref[place].astype(F32), row)
+        piece = ref[place].astype(F32)[row : row + 6]
+        return piece[0:3] + piece[3:6]
 
     for x in range(TILE_X):
         for y in range(TILE_Y):
-            total = None
-            for a in range(3):
-                for b in range(3):
-                    start = (a * 3 + b) * 24
-                    piece = taps[x + a, y + b, start : start + 24, :]
-                    total = piece if total is None else total + piece
-            value = joined(total)
+            value = joined(
+                added(
+                    [
+                        tap(x + a, y + b - 1, (a * 3 + b) * 24)
+                        for a in range(3)
+                        for b in range(3)
+                    ]
+                )
+            )
             x_ref = xl_ref if x == 0 else xh_ref
             y_ref = yl_ref if y == 0 else yh_ref
             on_x = x in (0, TILE_X - 1)
             on_y = y in (0, TILE_Y - 1)
             if on_x:
-                value += received(x_ref, 8, y * 8)
+                value += received(x_ref, 8, y * 6)
             if on_y:
-                value += received(y_ref, 12, x * 8)
+                value += received(y_ref, 12, x * 6)
             if on_x and on_y:
-                value += received(y_ref, 13 + (x > 0), 8 if y == 0 else 0)
+                value += received(y_ref, 12, 24 if x == 0 else 30)
             for d in range(3):
                 field_ref[d, x * TILE_Y + y : x * TILE_Y + y + 1, :] = value[d : d + 1]
     sent_ref[...] = field_ref[...].astype(BF)
 
 
 def gather_kernel(
-    where_ref, counts_ref, block_ref, dest_ref, own_ref, row_ref, y_one_ref, y_two_ref,
+    counts_ref, block_ref, dest_ref, own_ref, row_ref, y_one_ref, y_two_ref,
     nodes_ref, weight_ref, out_ref, frame, total,
 ):
     entries = weight_ref.shape[0]
     blocks = out_ref.shape[0]
-    odd = where_ref[1] % 2 == 1
+    odd = lax.axis_index("gy") % 2 == 1
     frame[5] = own_ref[...]
     for i in range(3):
         one = y_one_ref[i].astype(F32)
@@ -528,7 +572,7 @@
     sub = lax.broadcasted_iota(I32, (8, LANES), 0)
     for e in range(entries):
         tile = dest_ref[e]
-        d = (tile // where_ref[2] - where_ref[0] + 1) * 3 + (tile % where_ref[2] - where_ref[1] + 1)
+        d = (tile // lax.axis_size("gy") - lax.axis_index("gx") + 1) * 3 + (tile % lax.axis_size("gy") - lax.axis_index("gy") + 1)
         node = jnp.broadcast_to(nodes_ref[e : e + 1, :], (8, LANES))
         z = node & (LANES - 1)
         column = node >> 7
@@ -600,16 +644,6 @@
     particle_feat, block_counts, entry_block, entry_dest, entry_nodes, entry_weights,
     conv_in, conv_mid, conv_out, head_weight,
 ):
-    size_x = lax.axis_size("gx")
-    size_y = lax.axis_size("gy")
-    where = jnp.stack(
-        [
-            lax.axis_index("gx").astype(I32),
-            lax.axis_index("gy").astype(I32),
-            jnp.int32(size_y),
-            jnp.int32(size_x),
-        ]
-    )
     blocks = particle_feat.shape[0]
     entries = entry_weights.shape[0]
     dest = entry_dest.reshape(entries)
@@ -628,7 +662,7 @@
     sent = call(
         partial_kernel,
         [(packed, BF)] * 9,
-        [SM] * 4 + [HB, VM, HB],
+        [SM] * 3 + [HB, VM, HB],
         [
             pltpu.VMEM(particle_feat.shape, BF),
             pltpu.VMEM(entry_weights.shape, BF),
@@ -642,25 +676,25 @@
         ],
         70000000,
         limit=60 * 1024 * 1024,
-    )(where, block_counts, entry_block, dest, particle_feat, entry_nodes, entry_weights)
+    )(block_counts, entry_block, dest, particle_feat, entry_nodes, entry_weights)
     sides = [*across_x(sent[1], sent[2]), *across_y(sent[3], sent[4])]
-    sums = scatter(where, [sent[0]], None, False)[0]
-    *corners, sums = lax.optimization_barrier((*sent[5:], sums))
+    sums = scatter([sent[0]], None, False)[0]
+    corners = sent[5:]
     corners = [
         swapped(value, 1, 1 - 2 * (i // 2), i % 2) for i, value in enumerate(corners)
     ]
-    sums = scatter(where, sides, sums, False)[0]
-    grid, one, two = scatter(where, corners, sums, True)
+    sums = scatter(sides, sums, False)[0]
+    grid, one, two = scatter(corners, sums, True)
 
     column = (CHAN, LANES)
     one, two = across_x(one, two)
     xl, xh, one, two = call(
         grid_side_kernel,
         [((TILE_Y, *column), BF)] * 2 + [((TILE_X + 2, *column), BF)] * 2,
-        [SM] + [VM] * 3,
+        [VM] * 3,
         [pltpu.VMEM((TILE_X + 2, *column), BF)] * 2,
         1000000,
-    )(where, one, two, grid)
+    )(one, two, grid)
     one, two = across_y(one, two)
     stack, inner = call(
         inner_conv_kernel,
@@ -672,70 +706,84 @@
         [],
         1000000000,
     )(grid, xl, xh, in_weight)
-    act, coarse, one, two, down, up = call(
+    act, coarse, one, two = call(
         outer_conv_kernel,
         [
             ((TILE_X, TILE_Y, *column), BF),
             ((TILE_X // 2, TILE_Y // 2, *column), BF),
-            ((10, *column), BF),
-            ((10, *column), BF),
-            ((1, *column), BF),
-            ((1, *column), BF),
+            ((9, *column), BF),
+            ((9, *column), BF),
         ],
-        [SM] + [VM] * 7,
+        [VM] * 7,
         [
             pltpu.VMEM((TILE_X + 2, 2, 3 * CHAN, LANES), BF),
-            pltpu.VMEM((TILE_X, TILE_Y, 27 * 8, LANES), F32),
-            pltpu.VMEM((10, *column), BF),
-            pltpu.VMEM((10, *column), BF),
+            pltpu.VMEM((2, TILE_Y, 72, LANES), F32),
+            pltpu.VMEM((9, *column), BF),
+            pltpu.VMEM((9, *column), BF),
         ],
         600000000,
-    )(where, grid, stack, inner, one, two, in_weight, out_weight)
+    )(grid, stack, inner, one, two, in_weight, out_weight)
 
     one, two = across_x(one, two)
+    down, up = call(
+        rim_kernel,
+        [((24, LANES), F32)] * 2,
+        [VM] * 2,
+        [pltpu.VMEM((TILE_X, 27 * 8, LANES), F32)],
+        1000000000,
+    )(act, out_weight)
     xl, xh, one, two = call(
         coarse_side_kernel,
-        [((10, *column), BF)] * 2 + [((15, *column), BF)] * 2,
-        [SM] + [VM] * 5,
-        [pltpu.VMEM((15, *column), BF)] * 2,
+        [((9, *column), BF)] * 2 + [((13, *column), BF)] * 2,
+        [VM] * 5,
+        [pltpu.VMEM((13, *column), BF)] * 2,
         1000000,
-    )(where, one, two, coarse, down, up)
+    )(one, two, coarse, down, up)
     one, two = across_y(one, two)
+    stack, inner = call(
+        inner_mid_kernel,
+        [
+            ((6, TILE_Y // 2, 3 * CHAN, LANES), BF),
+            ((TILE_X + 2, 4, 27 * 8, LANES), F32),
+        ],
+        [VM] * 6,
+        [pltpu.VMEM((4, 2, *column), BF)],
+        1000000000,
+    )(coarse, xl, xh, act, mid_weight, out_weight)
     field, rounded = call(
-        second_conv_kernel,
+        outer_mid_kernel,
         [((3, TILE_X * TILE_Y, LANES), F32), ((3, TILE_X * TILE_Y, LANES), BF)],
-        [SM] + [VM] * 8,
+        [VM] * 9,
         [
-            pltpu.VMEM((6, 8, 3 * CHAN, LANES), BF),
-            pltpu.VMEM((TILE_X + 2, TILE_Y + 2, CHAN, LANES), BF),
-            pltpu.VMEM((4, 6, CHAN, LANES), BF),
-            pltpu.VMEM((TILE_X + 2, TILE_Y + 2, 27 * 8, LANES), F32),
-            pltpu.VMEM((15, *column), BF),
-            pltpu.VMEM((15, *column), BF),
+            pltpu.VMEM((6, 4, 3 * CHAN, LANES), BF),
+            pltpu.VMEM((4, 4, *column), BF),
+            pltpu.VMEM((TILE_X + 2, 6, 27 * 8, LANES), F32),
+            pltpu.VMEM((13, *column), BF),
+            pltpu.VMEM((13, *column), BF),
         ],
         1300000000,
-    )(where, act, coarse, xl, xh, one, two, mid_weight, out_weight)
+    )(act, stack, inner, xl, xh, one, two, mid_weight, out_weight)
 
     one, two = across_x(rounded, rounded)
     row = call(
         field_side_kernel,
         [((3, 3, TILE_X * TILE_Y, LANES), BF)],
-        [SM] + [VM] * 3,
+        [VM] * 3,
         [],
         1000000,
-    )(where, one, two, rounded)[0]
+    )(one, two, rounded)[0]
     one, two = across_y(row, row)
     return call(
         gather_kernel,
         [((blocks, 3, LANES), F32)],
-        [SM] * 4 + [VM] * 6,
+        [SM] * 3 + [VM] * 6,
         [
             pltpu.VMEM((10, 3, TILE_X * TILE_Y, LANES), F32),
             pltpu.VMEM((blocks, 24, LANES), F32),
         ],
         70000000,
     )(
-        where, block_counts, entry_block, dest, field, row, one, two, entry_nodes, entry_weights
+        block_counts, entry_block, dest, field, row, one, two, entry_nodes, entry_weights
     )[0]
 
 

time: 78.4 us -> 69.5 us (0.89)
  waiting for transfers between devices: 32.9 us -> 27.3 us
  Pallas kernels: 20 us -> 16.4 us
  starting transfers between devices: 22.1 us -> 22.9 us
    ppermute x20, waiting for transfers between devices: 32.9 us -> 27.3 us  [swapped(): return lax.ppermute(value, ('gx', 'gy'), pairs)]
    pallas_call x8 -> x10, Pallas kernels: 15.9 us -> 13.9 us  [the longest x3 4.68 us: scatter(): call(functools.partial(scatter_kernel, len(parts), first, last), outs, [V...]
    pallas_call x1, Pallas kernels: 2.03 us -> 1.01 us  [shards(): call(outer_conv_kernel, [((TILE_X, TILE_Y, *column), BF), ((TILE_X // 2,...]
    ppermute x20, starting transfers between devices: 22.1 us -> 22.9 us  [swapped(): return lax.ppermute(value, ('gx', 'gy'), pairs)]
  transfers between devices with their start and end apart: 20 -> 20, of which waited for: 13 -> 11; matrix products, arithmetic and copies ran while one was open for 1% -> 1% of each run, Pallas kernels for 7% -> 10%
where the time goes in v2:
time: 69.5 us; the launch traced here: 69 us
  waiting for transfers between devices  27.3 us (39%)
  starting transfers between devices  22.9 us (33%)
  Pallas kernels  16.4 us (24%)
  local copies, waits for them, and re-layouts  1.77 us (3%)
    ppermute x20, waiting for transfers between devices, swapped(): return lax.ppermute(value, ('gx', 'gy'), pairs)  27.3 us
    ppermute x20, starting transfers between devices, swapped(): return lax.ppermute(value, ('gx', 'gy'), pairs)  22.9 us
    pallas_call x3, Pallas kernels, scatter(): call(functools.partial(scatter_kernel, len(parts), first, last), outs, [V...  4.68 us
    pallas_call x1, Pallas kernels, shards(): call(partial_kernel, [(packed, BF)] * 9, [SM] * 3 + [HB, VM, HB], [pltpu....  4.08 us
    pallas_call x1, Pallas kernels, shards(): call(outer_mid_kernel, [((3, TILE_X * TILE_Y, LANES), F32), ((3, TILE_X *...  1.71 us
    pallas_call x1, Pallas kernels, shards(): call(inner_mid_kernel, [((6, TILE_Y // 2, 3 * CHAN, LANES), BF), ((TILE_X...  1.5 us
    pallas_call x1, Pallas kernels, shards(): call(inner_conv_kernel, [((TILE_X + 2, TILE_Y, 3 * CHAN, LANES), BF), ((T...  1.41 us
    pallas_call x1, Pallas kernels, shards(): call(gather_kernel, [((blocks, 3, LANES), F32)], [SM] * 3 + [VM] * 6, [pl...  1.41 us
  transfers between devices with their start and end apart: 20, of which 11 were waited for; matrix products, arithmetic and copies ran while one was open for 1% of the time, Pallas kernels for 10%

profile of v2, /device:TPU:16, one launch (start us, length us, event | category | flops | bytes accessed | tf_op | source)
XLA Modules:
  0.0 69.0 jit_solution(720400321413867149)
XLA Ops:
  0.0 4.1 %shard_map.100 = (bf16[528,128]{1,0:T(8,128)(2,1)}, bf16[528,128]{1,0:T(8,128)(2,1)}, bf16[528,128]{1,0:T(8,128)(2,1)}, bf16[528,128]{1,0:T(8,128)(2,1)}, bf16[5...) custom-call(s32[16]{0:T(128)} %counts_ref.3, ...), custom_call_target="tpu_custom_call" | custom-call | flops 70000000 | bytes 2000000 | tf_op jit(solution)/shard_map/pallas_call | solution.py:662
  4.1 2.0 %collective-permute-start.4 = (bf16[528,128]{1,0:T(8,128)(2,1)}, bf16[528,128]{1,0:T(8,128)(2,1)S(1)}, u32[]{:S(2)}, u32[]{:S(2)}) collective-permute-start(bf16[528,128]{1,0:T(8,128)(2,1)} %get-tuple-element.41), channel_id=1, source_target_pairs={{0,8},{1,9},{2,10},{3,11},{4,12},{5,13},{6,14},{7,15},{8,0},{9,1},... | collective-permute-start | bytes 405512 | tf_op jit(solution)/shard_map/ppermute | solution.py:632
  6.1 2.4 %collective-permute-start.5 = (bf16[528,128]{1,0:T(8,128)(2,1)}, bf16[528,128]{1,0:T(8,128)(2,1)S(1)}, u32[]{:S(2)}, u32[]{:S(2)}) collective-permute-start(bf16[528,128]{1,0:T(8,128)(2,1)} %get-tuple-element.42), channel_id=1, source_target_pairs={{0,1},{1,0},{2,3},{3,2},{4,5},{5,4},{6,7},{7,6},{8,16},{9,17},{10,... | collective-permute-start | bytes 405512 | tf_op jit(solution)/shard_map/ppermute | solution.py:632
  8.5 1.1 %collective-permute-start.7 = (bf16[528,128]{1,0:T(8,128)(2,1)}, bf16[528,128]{1,0:T(8,128)(2,1)S(1)}, u32[]{:S(2)}, u32[]{:S(2)}) collective-permute-start(bf16[528,128]{1,0:T(8,128)(2,1)} %get-tuple-element.44), channel_id=1, source_target_pairs={{0,8},{1,2},{2,1},{3,4},{4,3},{5,6},{6,5},{7,15},{8,0},{9,10},{10,... | collective-permute-start | bytes 405512 | tf_op jit(solution)/shard_map/ppermute | solution.py:632
  9.6 1.2 %collective-permute-start = (bf16[528,128]{1,0:T(8,128)(2,1)}, bf16[528,128]{1,0:T(8,128)(2,1)S(1)}, u32[]{:S(2)}, u32[]{:S(2)}) collective-permute-start(bf16[528,128]{1,0:T(8,128)(2,1)} %get-tuple-element.37), channel_id=1, source_target_pairs={{0,9},{1,10},{2,11},{3,12},{4,13},{5,14},{6,15},{7,23},{8,24},{9,0... | collective-permute-start | bytes 405512 | tf_op jit(solution)/shard_map/ppermute | solution.py:632
  10.8 0.1 pad.2.clone
  10.9 2.5 %collective-permute-start.1 = (bf16[528,128]{1,0:T(8,128)(2,1)}, bf16[528,128]{1,0:T(8,128)(2,1)S(1)}, u32[]{:S(2)}, u32[]{:S(2)}) collective-permute-start(bf16[528,128]{1,0:T(8,128)(2,1)} %get-tuple-element.38), channel_id=1, source_target_pairs={{0,1},{1,0},{2,3},{3,2},{4,5},{5,4},{6,7},{7,6},{8,17},{9,18},{10,... | collective-permute-start | bytes 405512 | tf_op jit(solution)/shard_map/ppermute | solution.py:632
  13.5 1.9 %collective-permute-start.2 = (bf16[528,128]{1,0:T(8,128)(2,1)}, bf16[528,128]{1,0:T(8,128)(2,1)S(1)}, u32[]{:S(2)}, u32[]{:S(2)}) collective-permute-start(bf16[528,128]{1,0:T(8,128)(2,1)} %get-tuple-element.39), channel_id=1, source_target_pairs={{0,15},{1,8},{2,9},{3,10},{4,11},{5,12},{6,13},{7,14},{8,1},{9,2},... | collective-permute-start | bytes 405512 | tf_op jit(solution)/shard_map/ppermute | solution.py:632
  15.4 0.6 collective-permute-start.3
  16.0 0.9 %copy-done.8 = bf16[528,128]{1,0:T(8,128)(2,1)S(1)} copy-done((bf16[528,128]{1,0:T(8,128)(2,1)S(1)}, bf16[528,128]{1,0:T(8,128)(2,1)}, u32[]{:S(2)}) %copy-start.8) | copy-done | bytes 135192
  16.9 1.2 %shard_map.101.refs_4_ = f32[1024,256]{1,0:T(8,128)S(1)} custom-call(bf16[528,128]{1,0:T(8,128)(2,1)S(1)} %copy-done.8), custom_call_target="tpu_custom_call" | custom-call | flops 800000000 | bytes 2000000 | tf_op jit(solution)/shard_map/pallas_call | solution.py:178
  18.1 0.0 copy-start.9
  18.2 2.2 %shard_map.102.refs_4_ = f32[1024,256]{1,0:T(8,128)S(1)} custom-call(bf16[528,128]{1,0:T(8,128)(2,1)S(1)} %collective-permute-done.4.refs_0_, bf16[528,128]{1,0:T(8,128)(2,1)S(1)} %collective-permute-done.5.refs_1_, bf16[528,128]{1,0:T(8,128)(2,1)S(1)} %collective-permute-done.6.refs_2_, bf16[528,128]{1,0:T(8,128)(2,1)S(1)} %collective-permute-done.7.refs_3_, ...), custom_call_target="tpu_custom_call" | custom-call | flops 800000000 | bytes 2000000 | tf_op jit(solution)/shard_map/pallas_call | solution.py:178
  20.4 0.0 copy-start.2
  20.4 2.6 %collective-permute-done.2.refs_2_ = bf16[528,128]{1,0:T(8,128)(2,1)S(1)} collective-permute-done((bf16[528,128]{1,0:T(8,128)(2,1)}, bf16[528,128]{1,0:T(8,128)(2,1)S(1)}, u32[]{:S(2)}, u32[]{:S(2)}) %collective-permute-start.2) | collective-permute-done | bytes 135200 | tf_op jit(solution)/shard_map/ppermute | solution.py:632
  23.0 1.3 %collective-permute-done.3.refs_3_ = bf16[528,128]{1,0:T(8,128)(2,1)S(1)} collective-permute-done((bf16[528,128]{1,0:T(8,128)(2,1)}, bf16[528,128]{1,0:T(8,128)(2,1)S(1)}, u32[]{:S(2)}, u32[]{:S(2)}) %collective-permute-start.3) | collective-permute-done | bytes 135200 | tf_op jit(solution)/shard_map/ppermute | solution.py:632
  24.3 1.3 %shard_map.103 = (bf16[4,8,64,128]{3,2,1,0:T(8,128)(2,1)S(1)}, bf16[8,64,128]{2,1,0:T(8,128)(2,1)S(1)}, bf16[8,64,128]{2,1,0:T(8,128)(2,1)S(1)}) custom-call(bf16[528,128]{1,0:T(8,128)(2,1)S(1)} %collective-permute-done.refs_0_, bf16[528,128]{1,0:T(8,128)(2,1)S(1)} %collective-permute-done.1.refs_1_, bf16[528,128]{1,0:T(8,128)(2,1)S(1)} %collective-permute-done.2.refs_2_, ...), custom_call_target="tpu_custom_call" | custom-call | flops 800000000 | bytes 2000000 | tf_op jit(solution)/shard_map/pallas_call | solution.py:178
  25.6 0.1 collective-permute-start.8
  25.7 3.1 %collective-permute-start.9 = (bf16[8,64,128]{2,1,0:T(8,128)(2,1)S(1)}, bf16[8,64,128]{2,1,0:T(8,128)(2,1)S(1)}, u32[]{:S(2)}, u32[]{:S(2)}) collective-permute-start(bf16[8,64,128]{2,1,0:T(8,128)(2,1)S(1)} %get-tuple-element.48), channel_id=1, source_target_pairs={{0,1},{1,0},{2,3},{3,2},{4,5},{5,4},{6,7},{7,6},{8,16},{9,17},{10,... | collective-permute-start | bytes 393224 | tf_op jit(solution)/shard_map/ppermute | solution.py:632
  28.8 0.2 reduce-precision_convert_fusion
  29.0 1.6 %collective-permute-done.8.one_ref = bf16[8,64,128]{2,1,0:T(8,128)(2,1)S(1)} collective-permute-done((bf16[8,64,128]{2,1,0:T(8,128)(2,1)S(1)}, bf16[8,64,128]{2,1,0:T(8,128)(2,1)S(1)}, u32[]{:S(2)}, u32[]{:S(2)}) %collective-permute-start.8) | collective-permute-done | bytes 131104 | tf_op jit(solution)/shard_map/ppermute | solution.py:632
  30.6 2.6 %collective-permute-done.9.two_ref = bf16[8,64,128]{2,1,0:T(8,128)(2,1)S(1)} collective-permute-done((bf16[8,64,128]{2,1,0:T(8,128)(2,1)S(1)}, bf16[8,64,128]{2,1,0:T(8,128)(2,1)S(1)}, u32[]{:S(2)}, u32[]{:S(2)}) %collective-permute-start.9) | collective-permute-done | bytes 131104 | tf_op jit(solution)/shard_map/ppermute | solution.py:632
  33.3 0.1 shard_map.104
  33.4 0.1 collective-permute-start.10
  33.5 0.6 collective-permute-start.11
  34.1 0.1 maximum_maximum_fusion
  34.1 0.1 convert_element_type.8
  34.3 1.4 %shard_map.105 = (bf16[6,8,192,128]{3,2,1,0:T(8,128)(2,1)S(1)}, bf16[4,6,64,128]{3,2,1,0:T(8,128)(2,1)S(1)}) custom-call(bf16[4,8,64,128]{3,2,1,0:T(8,128)(2,1)S(1)} %get-tuple-element.46.grid_ref, bf16[8,64,128]{2,1,0:T(8,128)(2,1)S(1)} %get-tuple-element.49.xl_ref, bf16[8,64,128]{2,1,0:T(8,128)(2,1)S(1)} %get-tuple-element.50.xh_ref, ...), custom_call_target="tpu_custom_call" | custom-call | flops 1000000000 | bytes 2000000 | tf_op jit(solution)/shard_map/pallas_call | solution.py:699
  35.7 2.5 %collective-permute-done.11.y_two_ref = bf16[6,64,128]{2,1,0:T(8,128)(2,1)S(1)} collective-permute-done((bf16[6,64,128]{2,1,0:T(8,128)(2,1)S(1)}, bf16[6,64,128]{2,1,0:T(8,128)(2,1)S(1)}, u32[]{:S(2)}, u32[]{:S(2)}) %collective-permute-start.11) | collective-permute-done | bytes 98336 | tf_op jit(solution)/shard_map/ppermute | solution.py:632
  38.2 1.0 %shard_map.106 = (bf16[4,8,64,128]{3,2,1,0:T(8,128)(2,1)S(1)}, bf16[2,4,64,128]{3,2,1,0:T(8,128)(2,1)S(1)}, bf16[9,64,128]{2,1,0:T(8,128)(2,1)S(1)}, bf16[9,64,128]{2,1,0:T(8,128)(2,1)S(1)}) custom-call(bf16[4,8,64,128]{3,2,1,0:T(8,128)(2,1)S(1)} %get-tuple-element.46.grid_ref, bf16[6,8,192,128]{3,2,1,0:T(8,128)(2,1)S(1)} %get-tuple-element.51.stack, ...), custom_call_target="tpu_custom_call" | custom-call | flops 600000000 | bytes 2000000 | tf_op jit(solution)/shard_map/pallas_call | solution.py:709
  39.2 0.6 collective-permute-start.12
  39.8 2.8 %collective-permute-start.13 = (bf16[9,64,128]{2,1,0:T(8,128)(2,1)S(1)}, bf16[9,64,128]{2,1,0:T(8,128)(2,1)S(1)}, u32[]{:S(2)}, u32[]{:S(2)}) collective-permute-start(bf16[9,64,128]{2,1,0:T(8,128)(2,1)S(1)} %get-tuple-element.58), channel_id=1, source_target_pairs={{0,1},{1,0},{2,3},{3,2},{4,5},{5,4},{6,7},{7,6},{8,16},{9,17},{10,... | collective-permute-start | bytes 442376 | tf_op jit(solution)/shard_map/ppermute | solution.py:632
  42.6 0.3 shard_map.107
  42.9 2.3 %collective-permute-done.12.one_ref = bf16[9,64,128]{2,1,0:T(8,128)(2,1)S(1)} collective-permute-done((bf16[9,64,128]{2,1,0:T(8,128)(2,1)S(1)}, bf16[9,64,128]{2,1,0:T(8,128)(2,1)S(1)}, u32[]{:S(2)}, u32[]{:S(2)}) %collective-permute-start.12) | collective-permute-done | bytes 147488 | tf_op jit(solution)/shard_map/ppermute | solution.py:632
  45.2 2.3 %collective-permute-done.13.two_ref = bf16[9,64,128]{2,1,0:T(8,128)(2,1)S(1)} collective-permute-done((bf16[9,64,128]{2,1,0:T(8,128)(2,1)S(1)}, bf16[9,64,128]{2,1,0:T(8,128)(2,1)S(1)}, u32[]{:S(2)}, u32[]{:S(2)}) %collective-permute-start.13) | collective-permute-done | bytes 147488 | tf_op jit(solution)/shard_map/ppermute | solution.py:632
  47.5 0.2 shard_map.108
  47.7 0.1 collective-permute-start.14
  47.8 0.6 collective-permute-start.15
  48.4 1.5 %shard_map.109 = (bf16[6,4,192,128]{3,2,1,0:T(8,128)(2,1)S(1)}, f32[6,4,216,128]{3,2,1,0:T(8,128)S(1)}) custom-call(bf16[2,4,64,128]{3,2,1,0:T(8,128)(2,1)S(1)} %get-tuple-element.56.coarse_ref, bf16[9,64,128]{2,1,0:T(8,128)(2,1)S(1)} %get-tuple-element.61.xl_ref, bf16[9,64,128]{2,1,0:T(8,128)(2,1)S(1)} %get-tuple-element.62.xh_ref, ...), custom_call_target="tpu_custom_call" | custom-call | flops 1000000000 | bytes 2000000 | tf_op jit(solution)/shard_map/pallas_call | solution.py:743
  49.9 3.9 %collective-permute-done.15.y_two_ref = bf16[13,64,128]{2,1,0:T(8,128)(2,1)S(1)} collective-permute-done((bf16[13,64,128]{2,1,0:T(8,128)(2,1)S(1)}, bf16[13,64,128]{2,1,0:T(8,128)(2,1)S(1)}, u32[]{:S(2)}, u32[]{:S(2)}) %collective-permute-start.15) | collective-permute-done | bytes 213024 | tf_op jit(solution)/shard_map/ppermute | solution.py:632
  53.9 1.7 %shard_map.110 = (f32[3,32,128]{2,1,0:T(8,128)S(1)}, bf16[3,32,128]{2,1,0:T(8,128)(2,1)S(1)}) custom-call(bf16[4,8,64,128]{3,2,1,0:T(8,128)(2,1)S(1)} %get-tuple-element.55.act_ref, bf16[6,4,192,128]{3,2,1,0:T(8,128)(2,1)S(1)} %get-tuple-element.63.stack, f32[6,4,216,128]{3,2,1,0:T(8,128)S(1)} %get-tuple-element.64.inner, ...), custom_call_target="tpu_custom_call" | custom-call | flops 1300000000 | bytes 2000000 | tf_op jit(solution)/shard_map/pallas_call | solution.py:753
  55.6 3.1 %collective-permute-start.17 = (bf16[3,32,128]{2,1,0:T(8,128)(2,1)S(1)}, bf16[3,32,128]{2,1,0:T(8,128)(2,1)S(1)}, u32[]{:S(2)}, u32[]{:S(2)}) collective-permute-start(bf16[3,32,128]{2,1,0:T(8,128)(2,1)S(1)} %get-tuple-element.68.own_ref), channel_id=1, source_target_pairs={{0,1},{1,0},{2,3},{3,2},{4,5},{5,4},{6,7},{7,6},{8,16},{9,17},{10,... | collective-permute-start | bytes 73736 | tf_op jit(solution)/shard_map/ppermute | solution.py:632
  58.7 2.9 %collective-permute-done.17.two_ref = bf16[3,32,128]{2,1,0:T(8,128)(2,1)S(1)} collective-permute-done((bf16[3,32,128]{2,1,0:T(8,128)(2,1)S(1)}, bf16[3,32,128]{2,1,0:T(8,128)(2,1)S(1)}, u32[]{:S(2)}, u32[]{:S(2)}) %collective-permute-start.17) | collective-permute-done | bytes 24608 | tf_op jit(solution)/shard_map/ppermute | solution.py:632
  61.6 0.9 %collective-permute-done.16.one_ref = bf16[3,32,128]{2,1,0:T(8,128)(2,1)S(1)} collective-permute-done((bf16[3,32,128]{2,1,0:T(8,128)(2,1)S(1)}, bf16[3,32,128]{2,1,0:T(8,128)(2,1)S(1)}, u32[]{:S(2)}, u32[]{:S(2)}) %collective-permute-start.16) | collective-permute-done | bytes 24608 | tf_op jit(solution)/shard_map/ppermute | solution.py:632
  62.6 0.1 collective-permute-start.18
  62.7 4.3 %collective-permute-done.19.y_two_ref = bf16[3,3,32,128]{3,2,1,0:T(8,128)(2,1)S(1)} collective-permute-done((bf16[3,3,32,128]{3,2,1,0:T(8,128)(2,1)S(1)}, bf16[3,3,32,128]{3,2,1,0:T(8,128)(2,1)S(1)}, u32[]{:S(2)}, u32[]{:S(2)}) %collective-permute-start.19) | collective-permute-done | bytes 73760 | tf_op jit(solution)/shard_map/ppermute | solution.py:632
  67.0 1.4 %shard_map.112 = f32[16,3,128]{2,1,0:T(4,128)S(1)} custom-call(s32[16]{0:T(128)S(1)} %copy-done.5, s32[32]{0:T(128)S(1)} %copy-done.6, s32[32]{0:T(128)S(1)} %bitcast.22, f32[3,32,128]{2,1,0:T(8,128)S(1)} %get-tuple-element.67.own_ref, bf16[3,3,32,128]{3,2,1,0:T(8,128)(2,1)S(1)} %shard_map.111.row_ref, ...), custom_call_target="tpu_custom_call" | custom-call | flops 70000000 | bytes 2000000 | tf_op jit(solution)/shard_map/pallas_call | solution.py:776
  68.4 0.6 copy.14
  (32 shorter events, 0.1 us)
Async XLA Ops:
  0.0 28.8 %copy-start = (bf16[3,64,576]{2,1,0:T(8,128)(2,1)S(1)}, bf16[3,64,576]{2,1,0:T(8,128)(2,1)}, u32[]{:S(2)}) copy-start(bf16[3,64,576]{2,1,0:T(8,128)(2,1)} %param.18) | copy-start | bytes 663556
  4.1 6.8 %collective-permute-start.4 = (bf16[528,128]{1,0:T(8,128)(2,1)}, bf16[528,128]{1,0:T(8,128)(2,1)S(1)}, u32[]{:S(2)}, u32[]{:S(2)}) collective-permute-start(bf16[528,128]{1,0:T(8,128)(2,1)} %get-tuple-element.41), channel_id=1, source_target_pairs={{0,8},{1,9},{2,10},{3,11},{4,12},{5,13},{6,14},{7,15},{8,0},{9,1},... | collective-permute-start | bytes 405512 | tf_op jit(solution)/shard_map/ppermute | solution.py:632
  6.1 7.4 %collective-permute-start.5 = (bf16[528,128]{1,0:T(8,128)(2,1)}, bf16[528,128]{1,0:T(8,128)(2,1)S(1)}, u32[]{:S(2)}, u32[]{:S(2)}) collective-permute-start(bf16[528,128]{1,0:T(8,128)(2,1)} %get-tuple-element.42), channel_id=1, source_target_pairs={{0,1},{1,0},{2,3},{3,2},{4,5},{5,4},{6,7},{7,6},{8,16},{9,17},{10,... | collective-permute-start | bytes 405512 | tf_op jit(solution)/shard_map/ppermute | solution.py:632
  8.5 6.9 %collective-permute-start.6 = (bf16[528,128]{1,0:T(8,128)(2,1)}, bf16[528,128]{1,0:T(8,128)(2,1)S(1)}, u32[]{:S(2)}, u32[]{:S(2)}) collective-permute-start(bf16[528,128]{1,0:T(8,128)(2,1)} %get-tuple-element.43), channel_id=1, source_target_pairs={{0,1},{1,0},{2,3},{3,2},{4,5},{5,4},{6,7},{7,6},{8,9},{9,8},{10,11... | collective-permute-start | bytes 405512 | tf_op jit(solution)/shard_map/ppermute | solution.py:632
  8.5 9.7 %collective-permute-start.7 = (bf16[528,128]{1,0:T(8,128)(2,1)}, bf16[528,128]{1,0:T(8,128)(2,1)S(1)}, u32[]{:S(2)}, u32[]{:S(2)}) collective-permute-start(bf16[528,128]{1,0:T(8,128)(2,1)} %get-tuple-element.44), channel_id=1, source_target_pairs={{0,8},{1,2},{2,1},{3,4},{4,3},{5,6},{6,5},{7,15},{8,0},{9,10},{10,... | collective-permute-start | bytes 405512 | tf_op jit(solution)/shard_map/ppermute | solution.py:632
  9.6 10.8 %collective-permute-start = (bf16[528,128]{1,0:T(8,128)(2,1)}, bf16[528,128]{1,0:T(8,128)(2,1)S(1)}, u32[]{:S(2)}, u32[]{:S(2)}) collective-permute-start(bf16[528,128]{1,0:T(8,128)(2,1)} %get-tuple-element.37), channel_id=1, source_target_pairs={{0,9},{1,10},{2,11},{3,12},{4,13},{5,14},{6,15},{7,23},{8,24},{9,0... | collective-permute-start | bytes 405512 | tf_op jit(solution)/shard_map/ppermute | solution.py:632
  10.9 9.5 %collective-permute-start.1 = (bf16[528,128]{1,0:T(8,128)(2,1)}, bf16[528,128]{1,0:T(8,128)(2,1)S(1)}, u32[]{:S(2)}, u32[]{:S(2)}) collective-permute-start(bf16[528,128]{1,0:T(8,128)(2,1)} %get-tuple-element.38), channel_id=1, source_target_pairs={{0,1},{1,0},{2,3},{3,2},{4,5},{5,4},{6,7},{7,6},{8,17},{9,18},{10,... | collective-permute-start | bytes 405512 | tf_op jit(solution)/shard_map/ppermute | solution.py:632
  13.5 9.5 %collective-permute-start.2 = (bf16[528,128]{1,0:T(8,128)(2,1)}, bf16[528,128]{1,0:T(8,128)(2,1)S(1)}, u32[]{:S(2)}, u32[]{:S(2)}) collective-permute-start(bf16[528,128]{1,0:T(8,128)(2,1)} %get-tuple-element.39), channel_id=1, source_target_pairs={{0,15},{1,8},{2,9},{3,10},{4,11},{5,12},{6,13},{7,14},{8,1},{9,2},... | collective-permute-start | bytes 405512 | tf_op jit(solution)/shard_map/ppermute | solution.py:632
  15.4 8.9 %collective-permute-start.3 = (bf16[528,128]{1,0:T(8,128)(2,1)}, bf16[528,128]{1,0:T(8,128)(2,1)S(1)}, u32[]{:S(2)}, u32[]{:S(2)}) collective-permute-start(bf16[528,128]{1,0:T(8,128)(2,1)} %get-tuple-element.40), channel_id=1, source_target_pairs={{0,1},{1,0},{2,3},{3,2},{4,5},{5,4},{6,7},{7,6},{8,24},{9,16},{10,... | collective-permute-start | bytes 405512 | tf_op jit(solution)/shard_map/ppermute | solution.py:632
  16.0 0.9 %copy-start.8 = (bf16[528,128]{1,0:T(8,128)(2,1)S(1)}, bf16[528,128]{1,0:T(8,128)(2,1)}, u32[]{:S(2)}) copy-start(bf16[528,128]{1,0:T(8,128)(2,1)} %get-tuple-element.45.refs_0_) | copy-start | bytes 405508
  18.1 10.7 %copy-start.9 = (f32[3,64]{1,0:T(4,128)S(1)}, f32[3,64]{1,0:T(4,128)}, u32[]{:S(2)}) copy-start(f32[3,64]{1,0:T(4,128)} %param.19) | copy-start | bytes 2308
  20.4 13.9 %copy-start.2 = (bf16[3,64,576]{2,1,0:T(8,128)(2,1)S(1)}, bf16[3,64,576]{2,1,0:T(8,128)(2,1)}, u32[]{:S(2)}) copy-start(bf16[3,64,576]{2,1,0:T(8,128)(2,1)} %param.16) | copy-start | bytes 663556
  25.6 5.0 %collective-permute-start.8 = (bf16[8,64,128]{2,1,0:T(8,128)(2,1)S(1)}, bf16[8,64,128]{2,1,0:T(8,128)(2,1)S(1)}, u32[]{:S(2)}, u32[]{:S(2)}) collective-permute-start(bf16[8,64,128]{2,1,0:T(8,128)(2,1)S(1)} %get-tuple-element.47), channel_id=1, source_target_pairs={{0,8},{1,9},{2,10},{3,11},{4,12},{5,13},{6,14},{7,15},{8,0},{9,1},... | collective-permute-start | bytes 393224 | tf_op jit(solution)/shard_map/ppermute | solution.py:632
  25.7 7.6 %collective-permute-start.9 = (bf16[8,64,128]{2,1,0:T(8,128)(2,1)S(1)}, bf16[8,64,128]{2,1,0:T(8,128)(2,1)S(1)}, u32[]{:S(2)}, u32[]{:S(2)}) collective-permute-start(bf16[8,64,128]{2,1,0:T(8,128)(2,1)S(1)} %get-tuple-element.48), channel_id=1, source_target_pairs={{0,1},{1,0},{2,3},{3,2},{4,5},{5,4},{6,7},{7,6},{8,16},{9,17},{10,... | collective-permute-start | bytes 393224 | tf_op jit(solution)/shard_map/ppermute | solution.py:632
  33.4 2.3 %collective-permute-start.10 = (bf16[6,64,128]{2,1,0:T(8,128)(2,1)S(1)}, bf16[6,64,128]{2,1,0:T(8,128)(2,1)S(1)}, u32[]{:S(2)}, u32[]{:S(2)}) collective-permute-start(bf16[6,64,128]{2,1,0:T(8,128)(2,1)S(1)} %get-tuple-element.53), channel_id=1, source_target_pairs={{0,1},{1,0},{2,3},{3,2},{4,5},{5,4},{6,7},{7,6},{8,9},{9,8},{10,11... | collective-permute-start | bytes 294920 | tf_op jit(solution)/shard_map/ppermute | solution.py:632
  33.5 4.7 %collective-permute-start.11 = (bf16[6,64,128]{2,1,0:T(8,128)(2,1)S(1)}, bf16[6,64,128]{2,1,0:T(8,128)(2,1)S(1)}, u32[]{:S(2)}, u32[]{:S(2)}) collective-permute-start(bf16[6,64,128]{2,1,0:T(8,128)(2,1)S(1)} %get-tuple-element.54), channel_id=1, source_target_pairs={{0,8},{1,2},{2,1},{3,4},{4,3},{5,6},{6,5},{7,15},{8,0},{9,10},{10,... | collective-permute-start | bytes 294920 | tf_op jit(solution)/shard_map/ppermute | solution.py:632
  39.2 9.2 %copy-start.3 = (bf16[3,64,576]{2,1,0:T(8,128)(2,1)S(1)}, bf16[3,64,576]{2,1,0:T(8,128)(2,1)}, u32[]{:S(2)}) copy-start(bf16[3,64,576]{2,1,0:T(8,128)(2,1)} %param.17) | copy-start | bytes 663556
  39.2 5.9 %collective-permute-start.12 = (bf16[9,64,128]{2,1,0:T(8,128)(2,1)S(1)}, bf16[9,64,128]{2,1,0:T(8,128)(2,1)S(1)}, u32[]{:S(2)}, u32[]{:S(2)}) collective-permute-start(bf16[9,64,128]{2,1,0:T(8,128)(2,1)S(1)} %get-tuple-element.57), channel_id=1, source_target_pairs={{0,8},{1,9},{2,10},{3,11},{4,12},{5,13},{6,14},{7,15},{8,0},{9,1},... | collective-permute-start | bytes 442376 | tf_op jit(solution)/shard_map/ppermute | solution.py:632
  39.8 7.7 %collective-permute-start.13 = (bf16[9,64,128]{2,1,0:T(8,128)(2,1)S(1)}, bf16[9,64,128]{2,1,0:T(8,128)(2,1)S(1)}, u32[]{:S(2)}, u32[]{:S(2)}) collective-permute-start(bf16[9,64,128]{2,1,0:T(8,128)(2,1)S(1)} %get-tuple-element.58), channel_id=1, source_target_pairs={{0,1},{1,0},{2,3},{3,2},{4,5},{5,4},{6,7},{7,6},{8,16},{9,17},{10,... | collective-permute-start | bytes 442376 | tf_op jit(solution)/shard_map/ppermute | solution.py:632
  47.7 2.2 %collective-permute-start.14 = (bf16[13,64,128]{2,1,0:T(8,128)(2,1)S(1)}, bf16[13,64,128]{2,1,0:T(8,128)(2,1)S(1)}, u32[]{:S(2)}, u32[]{:S(2)}) collective-permute-start(bf16[13,64,128]{2,1,0:T(8,128)(2,1)S(1)} %get-tuple-element.65), channel_id=1, source_target_pairs={{0,1},{1,0},{2,3},{3,2},{4,5},{5,4},{6,7},{7,6},{8,9},{9,8},{10,11... | collective-permute-start | bytes 638984 | tf_op jit(solution)/shard_map/ppermute | solution.py:632
  47.8 6.1 %collective-permute-start.15 = (bf16[13,64,128]{2,1,0:T(8,128)(2,1)S(1)}, bf16[13,64,128]{2,1,0:T(8,128)(2,1)S(1)}, u32[]{:S(2)}, u32[]{:S(2)}) collective-permute-start(bf16[13,64,128]{2,1,0:T(8,128)(2,1)S(1)} %get-tuple-element.66), channel_id=1, source_target_pairs={{0,8},{1,2},{2,1},{3,4},{4,3},{5,6},{6,5},{7,15},{8,0},{9,10},{10,... | collective-permute-start | bytes 638984 | tf_op jit(solution)/shard_map/ppermute | solution.py:632
  53.9 13.1 %copy-start.1 = (bf16[32,128,128]{2,1,0:T(8,128)(2,1)S(1)}, bf16[32,128,128]{2,1,0:T(8,128)(2,1)}, u32[]{:S(2)}) copy-start(bf16[32,128,128]{2,1,0:T(8,128)(2,1)} %weight_ref.1) | copy-start | bytes 3145732
  53.9 13.1 %copy-start.4 = (s32[32,128]{1,0:T(8,128)S(1)}, s32[32,128]{1,0:T(8,128)}, u32[]{:S(2)}) copy-start(s32[32,128]{1,0:T(8,128)} %nodes_ref.3) | copy-start | bytes 49156
  53.9 13.1 %copy-start.5 = (s32[16]{0:T(128)S(1)}, s32[16]{0:T(128)}, u32[]{:S(2)}) copy-start(s32[16]{0:T(128)} %counts_ref.3) | copy-start | bytes 196
  53.9 13.1 %copy-start.6 = (s32[32]{0:T(128)S(1)}, s32[32]{0:T(128)}, u32[]{:S(2)}) copy-start(s32[32]{0:T(128)} %block_ref.3) | copy-start | bytes 388
  53.9 13.1 %copy-start.7 = (s32[32,1]{0,1:T(1,128)S(1)}, s32[32,1]{0,1:T(1,128)}, u32[]{:S(2)}) copy-start(s32[32,1]{0,1:T(1,128)} %param.13) | copy-start | bytes 388
  55.6 6.0 %collective-permute-start.17 = (bf16[3,32,128]{2,1,0:T(8,128)(2,1)S(1)}, bf16[3,32,128]{2,1,0:T(8,128)(2,1)S(1)}, u32[]{:S(2)}, u32[]{:S(2)}) collective-permute-start(bf16[3,32,128]{2,1,0:T(8,128)(2,1)S(1)} %get-tuple-element.68.own_ref), channel_id=1, source_target_pairs={{0,1},{1,0},{2,3},{3,2},{4,5},{5,4},{6,7},{7,6},{8,16},{9,17},{10,... | collective-permute-start | bytes 73736 | tf_op jit(solution)/shard_map/ppermute | solution.py:632
  58.7 3.8 %collective-permute-start.16 = (bf16[3,32,128]{2,1,0:T(8,128)(2,1)S(1)}, bf16[3,32,128]{2,1,0:T(8,128)(2,1)S(1)}, u32[]{:S(2)}, u32[]{:S(2)}) collective-permute-start(bf16[3,32,128]{2,1,0:T(8,128)(2,1)S(1)} %get-tuple-element.68.own_ref), channel_id=1, source_target_pairs={{0,8},{1,9},{2,10},{3,11},{4,12},{5,13},{6,14},{7,15},{8,0},{9,1},... | collective-permute-start | bytes 73736 | tf_op jit(solution)/shard_map/ppermute | solution.py:632
  62.6 4.4 %collective-permute-start.19 = (bf16[3,3,32,128]{3,2,1,0:T(8,128)(2,1)S(1)}, bf16[3,3,32,128]{3,2,1,0:T(8,128)(2,1)S(1)}, u32[]{:S(2)}, u32[]{:S(2)}) collective-permute-start(bf16[3,3,32,128]{3,2,1,0:T(8,128)(2,1)S(1)} %shard_map.111.row_ref), channel_id=1, source_target_pairs={{0,8},{1,2},{2,1},{3,4},{4,3},{5,6},{6,5},{7,15},{8,0},{9,10},{10,... | collective-permute-start | bytes 221192 | tf_op jit(solution)/shard_map/ppermute | solution.py:632
  62.6 4.3 %collective-permute-start.18 = (bf16[3,3,32,128]{3,2,1,0:T(8,128)(2,1)S(1)}, bf16[3,3,32,128]{3,2,1,0:T(8,128)(2,1)S(1)}, u32[]{:S(2)}, u32[]{:S(2)}) collective-permute-start(bf16[3,3,32,128]{3,2,1,0:T(8,128)(2,1)S(1)} %shard_map.111.row_ref), channel_id=1, source_target_pairs={{0,1},{1,0},{2,3},{3,2},{4,5},{5,4},{6,7},{7,6},{8,9},{9,8},{10,11... | collective-permute-start | bytes 221192 | tf_op jit(solution)/shard_map/ppermute | solution.py:632

commit v3 on v2

--- a/solution.py
+++ b/solution.py
@@ -18,6 +18,8 @@
 SLOTS = 8
 GROUP = 4
 CHUNKS = 4
+OUTER = (0, TILE_X - 1)
+MIDDLE = tuple(range(1, TILE_X - 1))
 VMEM_LIMIT = 40 * 1024 * 1024
 
 VM = pl.BlockSpec(memory_space=pltpu.VMEM)
@@ -26,12 +28,12 @@
 NT = (((1,), (1,)), ((), ()))
 
 
-def call(kernel, outs, ins, scratch, flops, limit=VMEM_LIMIT):
+def call(kernel, outs, ins, scratch, flops, limit=VMEM_LIMIT, to=VM):
     return pl.pallas_call(
         kernel,
         out_shape=[jax.ShapeDtypeStruct(s, d) for s, d in outs],
         in_specs=ins,
-        out_specs=[VM] * len(outs),
+        out_specs=[to] * len(outs),
         scratch_shapes=scratch,
         compiler_params=pltpu.CompilerParams(vmem_limit_bytes=limit),
         cost_estimate=pl.CostEstimate(flops=flops, bytes_accessed=2000000, transcendentals=0),
@@ -42,7 +44,7 @@
     counts_ref, block_ref, dest_ref, feat_hbm, nodes_ref, weight_hbm, *rest
 ):
     outs = rest[:9]
-    feat_ref, weight_ref, sem, part, hi_all, lo_all, index, taken, entry_of = rest[9:]
+    feat_ref, weight_ref, sem, packed, hi_all, lo_all, index, taken = rest[9:]
     entries = weight_ref.shape[0]
     size = entries // CHUNKS
     copies = [pltpu.make_async_copy(feat_hbm, feat_ref, sem.at[CHUNKS])]
@@ -57,13 +59,18 @@
     index[...] = jnp.full(index.shape, -1.0, F32)
     for d in range(9):
         taken[d] = 0
-
-    def place(e, carry):
+    index_x = lax.axis_index("gx")
+    index_y = lax.axis_index("gy")
+    odd_x = (index_x + 1) % 2
+    odd_y = (index_y + 1) % 2
+    lane = lax.broadcasted_iota(I32, (CHAN, LANES), 1)
+    copies[0].wait()
+    for e in range(entries):
+        if e % size == 0:
+            copies[1 + e // size].wait()
         tile = dest_ref[e]
-        step_x = tile // lax.axis_size("gy") - lax.axis_index("gx")
-        step_y = tile % lax.axis_size("gy") - lax.axis_index("gy")
-        odd_x = lax.axis_index("gx") % 2
-        odd_y = lax.axis_index("gy") % 2
+        step_x = tile // lax.axis_size("gy") - index_x
+        step_y = tile % lax.axis_size("gy") - index_y
         by_x = jnp.where(step_x > 0, odd_x, 1 - odd_x)
         by_y = jnp.where(step_y > 0, odd_y, 1 - odd_y)
         d = jnp.where(step_x == step_y, 5 + by_x, 7 + by_x)
@@ -71,48 +78,43 @@
         d = jnp.where(step_x == 0, jnp.where(step_y == 0, 0, 3 + by_y), d)
         s = taken[d]
         taken[d] = s + 1
-        entry_of[d * SLOTS + s] = e
-        index[pl.ds(d * 16 + s, 1), :] = hi_all[pl.ds(e, 1), :]
-        index[pl.ds(d * 16 + 8 + s, 1), :] = lo_all[pl.ds(e, 1), :]
-        return carry
-
-    lax.fori_loop(0, entries, place, 0)
-    copies[0].wait()
-    lane = lax.broadcasted_iota(I32, (CHAN, LANES), 1)
-    for e in range(entries):
-        if e % size == 0:
-            copies[1 + e // size].wait()
+        index[pl.ds(d * 16 + s, 1), :] = hi_all[e : e + 1, :]
+        index[pl.ds(d * 16 + 8 + s, 1), :] = lo_all[e : e + 1, :]
         block = block_ref[e]
         feat = jnp.where(lane < counts_ref[block], feat_ref[block].astype(F32), 0.0).astype(BF)
         value = jnp.dot(feat, weight_ref[e], preferred_element_type=F32)
-        part[e] = value.astype(BF)
-    for d in range(9):
-
-        def copy(s, carry, d=d):
-            outs[d][pl.ds(pl.multiple_of(s * CHAN, CHAN), CHAN), :] = part[entry_of[d * SLOTS + s]]
-            return carry
-
-        lax.fori_loop(0, taken[d], copy, 0)
-        outs[d][SLOTS * CHAN :, :] = index[d * 16 : d * 16 + 16, :].astype(BF)
-
-
-def scatter_kernel(parts, first, last, *refs):
+        start = pl.multiple_of(s * CHAN, CHAN)
+        packed[d, pl.ds(start, CHAN), :] = value.astype(BF)
+    copies = []
+    for d in (1, 2, 3, 4, 5, 6, 7, 8, 0):
+        packed[d, SLOTS * CHAN :, :] = index[d * 16 : d * 16 + 16, :].astype(BF)
+        copies.append(pltpu.make_async_copy(packed.at[d], outs[d], sem.at[CHUNKS + 1 + d]))
+        copies[-1].start()
+    for c in copies:
+        c.wait()
+
+
+def scatter_kernel(parts, first, rows, *refs):
     got = refs[:parts]
     refs = refs[parts:]
     if not first:
         before = refs[0]
         refs = refs[1:]
-    if last:
-        grid_ref, one_ref, two_ref, values, index, hi_all, lo_all, acc = refs
+    if rows is None:
+        acc, values, index, hi_all, lo_all = refs
+        groups = list(range(16))
     else:
-        acc, values, index, hi_all, lo_all = refs
+        grid_ref = refs[0]
+        sides = refs[1:-5]
+        values, index, hi_all, lo_all, acc = refs[-5:]
+        groups = [4 * x + k for x in rows for k in range(4)]
     hi_all[...] = jnp.full(hi_all.shape, -1.0, F32)
     lo_all[...] = jnp.full(lo_all.shape, -1.0, F32)
     counts = []
     for d in range(parts):
-        rows = got[d][SLOTS * CHAN :, :].astype(F32)
-        index[d * 16 : d * 16 + 16, :] = rows
-        counts.append(jnp.sum(jnp.where(rows[0:8, 0:1] >= 0.0, 1.0, 0.0)).astype(I32))
+        marks = got[d][SLOTS * CHAN :, :].astype(F32)
+        index[d * 16 : d * 16 + 16, :] = marks
+        counts.append(jnp.sum(jnp.where(marks[0:8, 0:1] >= 0.0, 1.0, 0.0)).astype(I32))
     filled = jnp.int32(0)
     for d in range(parts):
 
@@ -124,13 +126,15 @@
 
         filled = lax.fori_loop(0, counts[d], copy, filled)
     row = lax.broadcasted_iota(I32, (256, LANES), 0).astype(F32)
-    if first:
-        acc[...] = jnp.zeros(acc.shape, F32)
-    else:
-        acc[...] = before[...]
+    for i, t in enumerate(groups):
+        piece = slice(i * CHAN, (i + 1) * CHAN)
+        if first:
+            acc[piece, :] = jnp.zeros((CHAN, 256), F32)
+        else:
+            acc[piece, :] = before[t * CHAN : (t + 1) * CHAN, :]
 
     def step(g, carry):
-        left = [[] for _ in range(16)]
+        left = [[] for _ in groups]
         right = []
         for j in range(GROUP):
             e = g * GROUP + j
@@ -138,45 +142,38 @@
             hi = jnp.broadcast_to(hi_all[pl.ds(e, 1), :], (CHAN, LANES)).astype(BF)
             lo = lo_all[pl.ds(e, 1), :]
             right.append(jnp.where(row == lo, 1.0, 0.0).astype(BF))
-            for t in range(16):
-                left[t].append(jnp.where(hi == jnp.array(t, BF), value, jnp.array(0, BF)))
-        a = jnp.concatenate([jnp.concatenate(rows, axis=1) for rows in left], axis=0)
+            for kept, t in zip(left, groups):
+                kept.append(jnp.where(hi == jnp.array(t, BF), value, jnp.array(0, BF)))
+        a = jnp.concatenate([jnp.concatenate(kept, axis=1) for kept in left], axis=0)
         b = jnp.concatenate(right, axis=1)
         acc[...] += lax.dot_general(a, b, NT, preferred_element_type=F32)
         return carry
 
     lax.fori_loop(0, (filled + GROUP - 1) // GROUP, step, 0)
-    if not last:
+    if rows is None:
         return
-    for t in range(16):
+    for i in range(len(groups)):
         for half in range(2):
-            column = acc[t * CHAN : (t + 1) * CHAN, half * LANES : (half + 1) * LANES].astype(BF)
-            x = t // 4
-            y = (t % 4) * 2 + half
-            grid_ref[x, y] = column
-    odd = lax.axis_index("gx") % 2
-
-    @pl.when(odd == 0)
-    def _():
-        one_ref[...] = grid_ref[TILE_X - 1]
-        two_ref[...] = grid_ref[0]
-
-    @pl.when(odd == 1)
-    def _():
-        one_ref[...] = grid_ref[0]
-        two_ref[...] = grid_ref[TILE_X - 1]
-
-
-def scatter(parts, before, last):
+            column = acc[i * CHAN : (i + 1) * CHAN, half * LANES : (half + 1) * LANES].astype(BF)
+            grid_ref[i // 4, (i % 4) * 2 + half] = column
+    if sides:
+        in_order((lax.axis_index("gx") + 1) % 2, *sides, grid_ref.at[0], grid_ref.at[1])
+
+
+def scatter(parts, before, rows=None):
     most = len(parts) * SLOTS + GROUP
     sums = ((16 * CHAN, 256), F32)
     first = before is None
-    if last:
-        outs = [((TILE_X, TILE_Y, CHAN, LANES), BF)] + [((TILE_Y, CHAN, LANES), BF)] * 2
+    if rows is None:
+        outs = [sums]
+        scratch = []
     else:
-        outs = [sums]
+        outs = [((len(rows), TILE_Y, CHAN, LANES), BF)]
+        if rows == OUTER:
+            outs += [((TILE_Y, CHAN, LANES), BF)] * 2
+        scratch = [pltpu.VMEM((len(rows) * 4 * CHAN, 256), F32)]
     return call(
-        functools.partial(scatter_kernel, len(parts), first, last),
+        functools.partial(scatter_kernel, len(parts), first, rows),
         outs,
         [VM] * (len(parts) + (not first)),
         [
@@ -185,9 +182,13 @@
             pltpu.VMEM((most, LANES), F32),
             pltpu.VMEM((most, LANES), F32),
         ]
-        + [pltpu.VMEM(*sums)] * last,
+        + scratch,
         800000000,
     )(*parts, *([] if first else [before]))
+
+
+def cell(outer_ref, middle_ref, x, y):
+    return outer_ref[x // (TILE_X - 1), y] if x in OUTER else middle_ref[x - 1, y]
 
 
 def shifted(column):
@@ -247,7 +248,7 @@
 
 def sorted_x(one_ref, two_ref, xl_ref, xh_ref):
     x_lo, x_hi, _, _ = edges()
-    odd = lax.axis_index("gx") % 2 == 1
+    odd = (lax.axis_index("gx") + 1) % 2 == 1
     for i in range(xl_ref.shape[0]):
         one = one_ref[i].astype(F32)
         two = two_ref[i].astype(F32)
@@ -257,7 +258,7 @@
 
 def sorted_y(one_ref, two_ref, i):
     _, _, y_lo, y_hi = edges()
-    odd = lax.axis_index("gy") % 2 == 1
+    odd = (lax.axis_index("gy") + 1) % 2 == 1
     one = one_ref[i].astype(F32)
     two = two_ref[i].astype(F32)
     lower = jnp.where(y_lo, jnp.where(odd, one, two), 0.0).astype(BF)
@@ -266,15 +267,15 @@
 
 
 def grid_side_kernel(
-    one_ref, two_ref, grid_ref, xl_ref, xh_ref, y_one_ref, y_two_ref, low, high
+    one_ref, two_ref, outer_ref, middle_ref, xl_ref, xh_ref, y_one_ref, y_two_ref, low, high
 ):
     sorted_x(one_ref, two_ref, xl_ref, xh_ref)
     for ref, y in ((low, 0), (high, TILE_Y - 1)):
         ref[0] = xl_ref[y]
         for x in range(TILE_X):
-            ref[x + 1] = grid_ref[x, y]
+            ref[x + 1] = cell(outer_ref, middle_ref, x, y)
         ref[TILE_X + 1] = xh_ref[y]
-    in_order(lax.axis_index("gy") % 2, y_one_ref, y_two_ref, low, high)
+    in_order((lax.axis_index("gy") + 1) % 2, y_one_ref, y_two_ref, low, high)
 
 
 def coarse_side_kernel(
@@ -292,11 +293,11 @@
                 ref[4 + x * 2 + k] = coarse_ref[x, y + k]
                 ref[8 + x * 2 + k] = xh_ref[x * half_y + y + k]
         ref[12] = filled_up([own[...], left[row : row + 6], right[row : row + 6]])
-    in_order(lax.axis_index("gy") % 2, y_one_ref, y_two_ref, low, high)
+    in_order((lax.axis_index("gy") + 1) % 2, y_one_ref, y_two_ref, low, high)
 
 
 def field_side_kernel(one_ref, two_ref, own_ref, row_ref):
-    odd = lax.axis_index("gx") % 2
+    odd = (lax.axis_index("gx") + 1) % 2
     row_ref[1] = own_ref[...]
 
     @pl.when(odd == 0)
@@ -315,10 +316,10 @@
     return jnp.where(keep, column.astype(F32), 0.0).astype(BF)
 
 
-def inner_conv_kernel(grid_ref, xl_ref, xh_ref, weight_ref, stack, act_ref):
+def inner_conv_kernel(outer_ref, middle_ref, xl_ref, xh_ref, weight_ref, stack, act_ref):
     for y in range(TILE_Y):
         for x in range(TILE_X):
-            stack[x + 1, y] = shifted(grid_ref[x, y])
+            stack[x + 1, y] = shifted(cell(outer_ref, middle_ref, x, y))
         stack[0, y] = shifted(xl_ref[y])
         stack[TILE_X + 1, y] = shifted(xh_ref[y])
     for y in range(1, TILE_Y - 1, 2):
@@ -329,7 +330,8 @@
         def put(x, value, y=y):
             for k in range(2):
                 part = value[:, k * LANES : (k + 1) * LANES]
-                act_ref[x, y - 1 + k] = (silu(part) + grid_ref[x, y + k].astype(F32)).astype(BF)
+                own = cell(outer_ref, middle_ref, x, y + k).astype(F32)
+                act_ref[x, y - 1 + k] = (silu(part) + own).astype(BF)
 
         conv_rows(picks, weight_ref, TILE_X, put)
 
@@ -357,7 +359,7 @@
 
 
 def outer_conv_kernel(
-    grid_ref, stack, inner_ref, y_one_ref, y_two_ref, weight_ref, out_weight_ref,
+    outer_ref, middle_ref, stack, inner_ref, y_one_ref, y_two_ref, weight_ref, out_weight_ref,
     act_ref, coarse_ref, one_ref, two_ref, edge, taps, low_ref, high_ref,
 ):
     for x in range(TILE_X + 2):
@@ -375,7 +377,8 @@
     def put(x, value):
         for k, y in enumerate((0, last_y)):
             part = value[:, k * LANES : (k + 1) * LANES]
-            act_ref[x, y] = (silu(part) + grid_ref[x, y].astype(F32)).astype(BF)
+            own = cell(outer_ref, middle_ref, x, y).astype(F32)
+            act_ref[x, y] = (silu(part) + own).astype(BF)
 
     conv_rows(picks, weight_ref, TILE_X, put)
     for x in range(TILE_X):
@@ -407,7 +410,7 @@
             total = added([taps[side, v, b * 24 : b * 24 + 24, :] for v, b in near])
             cells.append(two_parts(joined(total)))
         ref[8] = filled_up(cells)
-    in_order(lax.axis_index("gx") % 2, one_ref, two_ref, low_ref, high_ref)
+    in_order((lax.axis_index("gx") + 1) % 2, one_ref, two_ref, low_ref, high_ref)
 
 
 def rim_kernel(act_ref, out_weight_ref, down_ref, up_ref, taps):
@@ -559,7 +562,7 @@
 ):
     entries = weight_ref.shape[0]
     blocks = out_ref.shape[0]
-    odd = lax.axis_index("gy") % 2 == 1
+    odd = (lax.axis_index("gy") + 1) % 2 == 1
     frame[5] = own_ref[...]
     for i in range(3):
         one = y_one_ref[i].astype(F32)
@@ -633,11 +636,11 @@
 
 
 def across_x(one, two):
-    return swapped(one, 1, 0, 0), swapped(two, 1, 0, 1)
+    return swapped(one, 1, 0, 1), swapped(two, 1, 0, 0)
 
 
 def across_y(one, two):
-    return swapped(one, 0, 1, 0), swapped(two, 0, 1, 1)
+    return swapped(one, 0, 1, 1), swapped(two, 0, 1, 0)
 
 
 def shards(
@@ -666,35 +669,36 @@
         [
             pltpu.VMEM(particle_feat.shape, BF),
             pltpu.VMEM(entry_weights.shape, BF),
-            pltpu.SemaphoreType.DMA((CHUNKS + 1,)),
-            pltpu.VMEM((entries, CHAN, LANES), BF),
+            pltpu.SemaphoreType.DMA((CHUNKS + 10,)),
+            pltpu.VMEM((9, *packed), BF),
             pltpu.VMEM((entries, LANES), F32),
             pltpu.VMEM((entries, LANES), F32),
             pltpu.VMEM((9 * 16, LANES), F32),
             pltpu.SMEM((9,), I32),
-            pltpu.SMEM((9 * SLOTS,), I32),
         ],
         70000000,
         limit=60 * 1024 * 1024,
+        to=HB,
     )(block_counts, entry_block, dest, particle_feat, entry_nodes, entry_weights)
     sides = [*across_x(sent[1], sent[2]), *across_y(sent[3], sent[4])]
-    sums = scatter([sent[0]], None, False)[0]
+    sums = scatter([sent[0]], None)[0]
     corners = sent[5:]
     corners = [
-        swapped(value, 1, 1 - 2 * (i // 2), i % 2) for i, value in enumerate(corners)
+        swapped(value, 1, 1 - 2 * (i // 2), 1 - i % 2) for i, value in enumerate(corners)
     ]
-    sums = scatter(sides, sums, False)[0]
-    grid, one, two = scatter(corners, sums, True)
+    sums = scatter([*sides, *corners[:2]], sums)[0]
+    outer, one, two = scatter(corners[2:], sums, OUTER)
+    middle = scatter(corners[2:], sums, MIDDLE)[0]
 
     column = (CHAN, LANES)
     one, two = across_x(one, two)
     xl, xh, one, two = call(
         grid_side_kernel,
         [((TILE_Y, *column), BF)] * 2 + [((TILE_X + 2, *column), BF)] * 2,
-        [VM] * 3,
+        [VM] * 4,
         [pltpu.VMEM((TILE_X + 2, *column), BF)] * 2,
         1000000,
-    )(one, two, grid)
+    )(one, two, outer, middle)
     one, two = across_y(one, two)
     stack, inner = call(
         inner_conv_kernel,
@@ -702,10 +706,10 @@
             ((TILE_X + 2, TILE_Y, 3 * CHAN, LANES), BF),
             ((TILE_X, TILE_Y - 2, CHAN, LANES), BF),
         ],
-        [VM] * 4,
+        [VM] * 5,
         [],
         1000000000,
-    )(grid, xl, xh, in_weight)
+    )(outer, middle, xl, xh, in_weight)
     act, coarse, one, two = call(
         outer_conv_kernel,
         [
@@ -714,7 +718,7 @@
             ((9, *column), BF),
             ((9, *column), BF),
         ],
-        [VM] * 7,
+        [VM] * 8,
         [
             pltpu.VMEM((TILE_X + 2, 2, 3 * CHAN, LANES), BF),
             pltpu.VMEM((2, TILE_Y, 72, LANES), F32),
@@ -722,7 +726,7 @@
             pltpu.VMEM((9, *column), BF),
         ],
         600000000,
-    )(grid, stack, inner, one, two, in_weight, out_weight)
+    )(outer, middle, stack, inner, one, two, in_weight, out_weight)
 
     one, two = across_x(one, two)
     down, up = call(

time: 69.5 us -> 66.5 us (0.957)
  starting transfers between devices: 22.9 us -> 17.5 us
  waiting for transfers between devices: 27.3 us -> 29.8 us
    ppermute x20, starting transfers between devices: 22.9 us -> 17.5 us  [swapped(): return lax.ppermute(value, ('gx', 'gy'), pairs)]
    ppermute x20, waiting for transfers between devices: 27.3 us -> 29.8 us  [swapped(): return lax.ppermute(value, ('gx', 'gy'), pairs)]
    pallas_call x3 -> x4, Pallas kernels: 4.68 us -> 4.52 us  [scatter(): call(functools.partial(scatter_kernel, len(parts), first, rows), outs, [V...]
  transfers between devices with their start and end apart: 20 -> 20, of which waited for: 11 -> 13; matrix products, arithmetic and copies ran while one was open for 1% -> 1% of each run, Pallas kernels for 10% -> 11%
where the time goes in v3:
time: 66.5 us; the launch traced here: 65.7 us
  waiting for transfers between devices  29.8 us (45%)
  starting transfers between devices  17.5 us (26%)
  Pallas kernels  16.1 us (24%)
  local copies, waits for them, and re-layouts  1.77 us (3%)
    ppermute x20, waiting for transfers between devices, swapped(): return lax.ppermute(value, ('gx', 'gy'), pairs)  29.8 us
    ppermute x20, starting transfers between devices, swapped(): return lax.ppermute(value, ('gx', 'gy'), pairs)  17.5 us
    pallas_call x4, Pallas kernels, scatter(): call(functools.partial(scatter_kernel, len(parts), first, rows), outs, [V...  4.52 us
    pallas_call x1, Pallas kernels, shards(): call(partial_kernel, [(packed, BF)] * 9, [SM] * 3 + [HB, VM, HB], [pltpu....  3.86 us
    pallas_call x1, Pallas kernels, shards(): call(outer_mid_kernel, [((3, TILE_X * TILE_Y, LANES), F32), ((3, TILE_X *...  1.71 us
    pallas_call x1, Pallas kernels, shards(): call(inner_mid_kernel, [((6, TILE_Y // 2, 3 * CHAN, LANES), BF), ((TILE_X...  1.51 us
    pallas_call x1, Pallas kernels, shards(): call(gather_kernel, [((blocks, 3, LANES), F32)], [SM] * 3 + [VM] * 6, [pl...  1.42 us
    pallas_call x1, Pallas kernels, shards(): call(inner_conv_kernel, [((TILE_X + 2, TILE_Y, 3 * CHAN, LANES), BF), ((T...  1.41 us
  transfers between devices with their start and end apart: 20, of which 13 were waited for; matrix products, arithmetic and copies ran while one was open for 1% of the time, Pallas kernels for 11%

profile of v3, /device:TPU:16, one launch (start us, length us, event | category | flops | bytes accessed | tf_op | source)
XLA Modules:
  0.0 65.7 jit_solution(8546472319762023857)
XLA Ops:
  0.0 3.9 %shard_map.100 = (bf16[528,128]{1,0:T(8,128)(2,1)}, bf16[528,128]{1,0:T(8,128)(2,1)}, bf16[528,128]{1,0:T(8,128)(2,1)}, bf16[528,128]{1,0:T(8,128)(2,1)}, bf16[5...) custom-call(s32[16]{0:T(128)} %counts_ref.3, ...), custom_call_target="tpu_custom_call" | custom-call | flops 70000000 | bytes 2000000 | tf_op jit(solution)/shard_map/pallas_call | solution.py:665
  3.9 4.0 %collective-permute-start.2 = (bf16[528,128]{1,0:T(8,128)(2,1)}, bf16[528,128]{1,0:T(8,128)(2,1)S(1)}, u32[]{:S(2)}, u32[]{:S(2)}) collective-permute-start(bf16[528,128]{1,0:T(8,128)(2,1)} %get-tuple-element.39), channel_id=1, source_target_pairs={{0,1},{1,0},{2,3},{3,2},{4,5},{5,4},{6,7},{7,6},{8,16},{9,17},{10,... | collective-permute-start | bytes 405512 | tf_op jit(solution)/shard_map/ppermute | solution.py:635
  7.9 2.0 %collective-permute-start.4 = (bf16[528,128]{1,0:T(8,128)(2,1)}, bf16[528,128]{1,0:T(8,128)(2,1)S(1)}, u32[]{:S(2)}, u32[]{:S(2)}) collective-permute-start(bf16[528,128]{1,0:T(8,128)(2,1)} %get-tuple-element.41), channel_id=1, source_target_pairs={{0,8},{1,2},{2,1},{3,4},{4,3},{5,6},{6,5},{7,15},{8,0},{9,10},{10,... | collective-permute-start | bytes 405512 | tf_op jit(solution)/shard_map/ppermute | solution.py:635
  9.9 1.3 %collective-permute-start.6 = (bf16[528,128]{1,0:T(8,128)(2,1)}, bf16[528,128]{1,0:T(8,128)(2,1)S(1)}, u32[]{:S(2)}, u32[]{:S(2)}) collective-permute-start(bf16[528,128]{1,0:T(8,128)(2,1)} %get-tuple-element.43), channel_id=1, source_target_pairs={{0,1},{1,0},{2,3},{3,2},{4,5},{5,4},{6,7},{7,6},{8,17},{9,18},{10,... | collective-permute-start | bytes 405512 | tf_op jit(solution)/shard_map/ppermute | solution.py:635
  11.2 0.5 collective-permute-done.2.refs_0_
  11.7 0.1 collective-permute-start.7
  11.8 1.4 %collective-permute-done.3.refs_1_ = bf16[528,128]{1,0:T(8,128)(2,1)S(1)} collective-permute-done((bf16[528,128]{1,0:T(8,128)(2,1)}, bf16[528,128]{1,0:T(8,128)(2,1)S(1)}, u32[]{:S(2)}, u32[]{:S(2)}) %collective-permute-start.3) | collective-permute-done | bytes 135200 | tf_op jit(solution)/shard_map/ppermute | solution.py:635
  13.1 1.5 %collective-permute-start = (bf16[528,128]{1,0:T(8,128)(2,1)}, bf16[528,128]{1,0:T(8,128)(2,1)S(1)}, u32[]{:S(2)}, u32[]{:S(2)}) collective-permute-start(bf16[528,128]{1,0:T(8,128)(2,1)} %get-tuple-element.37), channel_id=1, source_target_pairs={{0,1},{1,0},{2,3},{3,2},{4,5},{5,4},{6,7},{7,6},{8,24},{9,16},{10,... | collective-permute-start | bytes 405512 | tf_op jit(solution)/shard_map/ppermute | solution.py:635
  14.6 1.2 %collective-permute-start.1 = (bf16[528,128]{1,0:T(8,128)(2,1)}, bf16[528,128]{1,0:T(8,128)(2,1)S(1)}, u32[]{:S(2)}, u32[]{:S(2)}) collective-permute-start(bf16[528,128]{1,0:T(8,128)(2,1)} %get-tuple-element.38), channel_id=1, source_target_pairs={{0,15},{1,8},{2,9},{3,10},{4,11},{5,12},{6,13},{7,14},{8,1},{9,2},... | collective-permute-start | bytes 405512 | tf_op jit(solution)/shard_map/ppermute | solution.py:635
  15.8 0.9 %copy-done.8 = bf16[528,128]{1,0:T(8,128)(2,1)S(1)} copy-done((bf16[528,128]{1,0:T(8,128)(2,1)S(1)}, bf16[528,128]{1,0:T(8,128)(2,1)}, u32[]{:S(2)}) %copy-start.8) | copy-done | bytes 135192
  16.7 1.2 %shard_map.101.refs_6_ = f32[1024,256]{1,0:T(8,128)S(1)} custom-call(bf16[528,128]{1,0:T(8,128)(2,1)S(1)} %copy-done.8), custom_call_target="tpu_custom_call" | custom-call | flops 800000000 | bytes 2000000 | tf_op jit(solution)/shard_map/pallas_call | solution.py:175
  18.0 0.8 %collective-permute-done.6.refs_4_ = bf16[528,128]{1,0:T(8,128)(2,1)S(1)} collective-permute-done((bf16[528,128]{1,0:T(8,128)(2,1)}, bf16[528,128]{1,0:T(8,128)(2,1)S(1)}, u32[]{:S(2)}, u32[]{:S(2)}) %collective-permute-start.6) | collective-permute-done | bytes 135200 | tf_op jit(solution)/shard_map/ppermute | solution.py:635
  18.8 2.2 %shard_map.102.refs_2_ = f32[1024,256]{1,0:T(8,128)S(1)} custom-call(bf16[528,128]{1,0:T(8,128)(2,1)S(1)} %collective-permute-done.2.refs_0_, bf16[528,128]{1,0:T(8,128)(2,1)S(1)} %collective-permute-done.3.refs_1_, bf16[528,128]{1,0:T(8,128)(2,1)S(1)} %collective-permute-done.4.refs_2_, bf16[528,128]{1,0:T(8,128)(2,1)S(1)} %collective-permute-done.5.refs_3_, ...), custom_call_target="tpu_custom_call" | custom-call | flops 800000000 | bytes 2000000 | tf_op jit(solution)/shard_map/pallas_call | solution.py:175
  21.0 1.4 %collective-permute-done.refs_0_ = bf16[528,128]{1,0:T(8,128)(2,1)S(1)} collective-permute-done((bf16[528,128]{1,0:T(8,128)(2,1)}, bf16[528,128]{1,0:T(8,128)(2,1)S(1)}, u32[]{:S(2)}, u32[]{:S(2)}) %collective-permute-start) | collective-permute-done | bytes 135200 | tf_op jit(solution)/shard_map/ppermute | solution.py:635
  22.4 1.0 %collective-permute-done.1.refs_1_ = bf16[528,128]{1,0:T(8,128)(2,1)S(1)} collective-permute-done((bf16[528,128]{1,0:T(8,128)(2,1)}, bf16[528,128]{1,0:T(8,128)(2,1)S(1)}, u32[]{:S(2)}, u32[]{:S(2)}) %collective-permute-start.1) | collective-permute-done | bytes 135200 | tf_op jit(solution)/shard_map/ppermute | solution.py:635
  23.4 0.6 shard_map.103
  24.0 0.0 copy-start.2
  24.0 2.4 %collective-permute-start.8 = (bf16[8,64,128]{2,1,0:T(8,128)(2,1)S(1)}, bf16[8,64,128]{2,1,0:T(8,128)(2,1)S(1)}, u32[]{:S(2)}, u32[]{:S(2)}) collective-permute-start(bf16[8,64,128]{2,1,0:T(8,128)(2,1)S(1)} %get-tuple-element.47), channel_id=1, source_target_pairs={{0,1},{1,0},{2,3},{3,2},{4,5},{5,4},{6,7},{7,6},{8,16},{9,17},{10,... | collective-permute-start | bytes 393224 | tf_op jit(solution)/shard_map/ppermute | solution.py:635
  26.3 0.2 reduce-precision_convert_fusion
  26.6 0.1 pad.2.clone
  26.7 0.5 shard_map.104.middle_ref
  27.2 4.8 %collective-permute-done.8.one_ref = bf16[8,64,128]{2,1,0:T(8,128)(2,1)S(1)} collective-permute-done((bf16[8,64,128]{2,1,0:T(8,128)(2,1)S(1)}, bf16[8,64,128]{2,1,0:T(8,128)(2,1)S(1)}, u32[]{:S(2)}, u32[]{:S(2)}) %collective-permute-start.8) | collective-permute-done | bytes 131104 | tf_op jit(solution)/shard_map/ppermute | solution.py:635
  32.0 0.1 shard_map.105
  32.2 0.6 collective-permute-start.10
  32.8 0.1 maximum_maximum_fusion
  32.9 0.1 convert_element_type.8
  33.0 1.4 %shard_map.106 = (bf16[6,8,192,128]{3,2,1,0:T(8,128)(2,1)S(1)}, bf16[4,6,64,128]{3,2,1,0:T(8,128)(2,1)S(1)}) custom-call(bf16[2,8,64,128]{3,2,1,0:T(8,128)(2,1)S(1)} %get-tuple-element.46.outer_ref, bf16[2,8,64,128]{3,2,1,0:T(8,128)(2,1)S(1)} %shard_map.104.middle_ref, bf16[8,64,128]{2,1,0:T(8,128)(2,1)S(1)} %get-tuple-element.49.xl_ref, ...), custom_call_target="tpu_custom_call" | custom-call | flops 1000000000 | bytes 2000000 | tf_op jit(solution)/shard_map/pallas_call | solution.py:703
  34.5 2.4 %collective-permute-done.10.y_one_ref = bf16[6,64,128]{2,1,0:T(8,128)(2,1)S(1)} collective-permute-done((bf16[6,64,128]{2,1,0:T(8,128)(2,1)S(1)}, bf16[6,64,128]{2,1,0:T(8,128)(2,1)S(1)}, u32[]{:S(2)}, u32[]{:S(2)}) %collective-permute-start.10) | collective-permute-done | bytes 98336 | tf_op jit(solution)/shard_map/ppermute | solution.py:635
  36.9 1.0 %shard_map.107 = (bf16[4,8,64,128]{3,2,1,0:T(8,128)(2,1)S(1)}, bf16[2,4,64,128]{3,2,1,0:T(8,128)(2,1)S(1)}, bf16[9,64,128]{2,1,0:T(8,128)(2,1)S(1)}, bf16[9,64,128]{2,1,0:T(8,128)(2,1)S(1)}) custom-call(bf16[2,8,64,128]{3,2,1,0:T(8,128)(2,1)S(1)} %get-tuple-element.46.outer_ref, bf16[2,8,64,128]{3,2,1,0:T(8,128)(2,1)S(1)} %shard_map.104.middle_ref, ...), custom_call_target="tpu_custom_call" | custom-call | flops 600000000 | bytes 2000000 | tf_op jit(solution)/shard_map/pallas_call | solution.py:713
  37.9 1.8 %collective-permute-start.12 = (bf16[9,64,128]{2,1,0:T(8,128)(2,1)S(1)}, bf16[9,64,128]{2,1,0:T(8,128)(2,1)S(1)}, u32[]{:S(2)}, u32[]{:S(2)}) collective-permute-start(bf16[9,64,128]{2,1,0:T(8,128)(2,1)S(1)} %get-tuple-element.57), channel_id=1, source_target_pairs={{0,1},{1,0},{2,3},{3,2},{4,5},{5,4},{6,7},{7,6},{8,16},{9,17},{10,... | collective-permute-start | bytes 442376 | tf_op jit(solution)/shard_map/ppermute | solution.py:635
  39.7 0.3 shard_map.108
  40.0 5.2 %collective-permute-done.12.one_ref = bf16[9,64,128]{2,1,0:T(8,128)(2,1)S(1)} collective-permute-done((bf16[9,64,128]{2,1,0:T(8,128)(2,1)S(1)}, bf16[9,64,128]{2,1,0:T(8,128)(2,1)S(1)}, u32[]{:S(2)}, u32[]{:S(2)}) %collective-permute-start.12) | collective-permute-done | bytes 147488 | tf_op jit(solution)/shard_map/ppermute | solution.py:635
  45.2 0.2 shard_map.109
  45.4 0.1 collective-permute-start.14
  45.5 0.3 collective-permute-start.15
  45.8 1.5 %shard_map.110 = (bf16[6,4,192,128]{3,2,1,0:T(8,128)(2,1)S(1)}, f32[6,4,216,128]{3,2,1,0:T(8,128)S(1)}) custom-call(bf16[2,4,64,128]{3,2,1,0:T(8,128)(2,1)S(1)} %get-tuple-element.56.coarse_ref, bf16[9,64,128]{2,1,0:T(8,128)(2,1)S(1)} %get-tuple-element.61.xl_ref, bf16[9,64,128]{2,1,0:T(8,128)(2,1)S(1)} %get-tuple-element.62.xh_ref, ...), custom_call_target="tpu_custom_call" | custom-call | flops 1000000000 | bytes 2000000 | tf_op jit(solution)/shard_map/pallas_call | solution.py:747
  47.3 4.0 %collective-permute-done.14.y_one_ref = bf16[13,64,128]{2,1,0:T(8,128)(2,1)S(1)} collective-permute-done((bf16[13,64,128]{2,1,0:T(8,128)(2,1)S(1)}, bf16[13,64,128]{2,1,0:T(8,128)(2,1)S(1)}, u32[]{:S(2)}, u32[]{:S(2)}) %collective-permute-start.14) | collective-permute-done | bytes 213024 | tf_op jit(solution)/shard_map/ppermute | solution.py:635
  51.4 0.0 copy-start.6
  51.4 1.7 %shard_map.111 = (f32[3,32,128]{2,1,0:T(8,128)S(1)}, bf16[3,32,128]{2,1,0:T(8,128)(2,1)S(1)}) custom-call(bf16[4,8,64,128]{3,2,1,0:T(8,128)(2,1)S(1)} %get-tuple-element.55.act_ref, bf16[6,4,192,128]{3,2,1,0:T(8,128)(2,1)S(1)} %get-tuple-element.63.stack, f32[6,4,216,128]{3,2,1,0:T(8,128)S(1)} %get-tuple-element.64.inner, ...), custom_call_target="tpu_custom_call" | custom-call | flops 1300000000 | bytes 2000000 | tf_op jit(solution)/shard_map/pallas_call | solution.py:757
  53.1 0.1 collective-permute-start.17
  53.2 2.1 %collective-permute-start.16 = (bf16[3,32,128]{2,1,0:T(8,128)(2,1)S(1)}, bf16[3,32,128]{2,1,0:T(8,128)(2,1)S(1)}, u32[]{:S(2)}, u32[]{:S(2)}) collective-permute-start(bf16[3,32,128]{2,1,0:T(8,128)(2,1)S(1)} %get-tuple-element.68.own_ref), channel_id=1, source_target_pairs={{0,1},{1,0},{2,3},{3,2},{4,5},{5,4},{6,7},{7,6},{8,16},{9,17},{10,... | collective-permute-start | bytes 73736 | tf_op jit(solution)/shard_map/ppermute | solution.py:635
  55.3 1.7 %collective-permute-done.17.two_ref = bf16[3,32,128]{2,1,0:T(8,128)(2,1)S(1)} collective-permute-done((bf16[3,32,128]{2,1,0:T(8,128)(2,1)S(1)}, bf16[3,32,128]{2,1,0:T(8,128)(2,1)S(1)}, u32[]{:S(2)}, u32[]{:S(2)}) %collective-permute-start.17) | collective-permute-done | bytes 24608 | tf_op jit(solution)/shard_map/ppermute | solution.py:635
  57.0 2.2 %collective-permute-done.16.one_ref = bf16[3,32,128]{2,1,0:T(8,128)(2,1)S(1)} collective-permute-done((bf16[3,32,128]{2,1,0:T(8,128)(2,1)S(1)}, bf16[3,32,128]{2,1,0:T(8,128)(2,1)S(1)}, u32[]{:S(2)}, u32[]{:S(2)}) %collective-permute-start.16) | collective-permute-done | bytes 24608 | tf_op jit(solution)/shard_map/ppermute | solution.py:635
  59.2 0.1 collective-permute-start.18
  59.3 1.2 %collective-permute-done.19.y_two_ref = bf16[3,3,32,128]{3,2,1,0:T(8,128)(2,1)S(1)} collective-permute-done((bf16[3,3,32,128]{3,2,1,0:T(8,128)(2,1)S(1)}, bf16[3,3,32,128]{3,2,1,0:T(8,128)(2,1)S(1)}, u32[]{:S(2)}, u32[]{:S(2)}) %collective-permute-start.19) | collective-permute-done | bytes 73760 | tf_op jit(solution)/shard_map/ppermute | solution.py:635
  60.5 3.2 %collective-permute-done.18.y_one_ref = bf16[3,3,32,128]{3,2,1,0:T(8,128)(2,1)S(1)} collective-permute-done((bf16[3,3,32,128]{3,2,1,0:T(8,128)(2,1)S(1)}, bf16[3,3,32,128]{3,2,1,0:T(8,128)(2,1)S(1)}, u32[]{:S(2)}, u32[]{:S(2)}) %collective-permute-start.18) | collective-permute-done | bytes 73760 | tf_op jit(solution)/shard_map/ppermute | solution.py:635
  63.7 1.4 %shard_map.113 = f32[16,3,128]{2,1,0:T(4,128)S(1)} custom-call(s32[16]{0:T(128)S(1)} %copy-done.5, s32[32]{0:T(128)S(1)} %copy-done.6, s32[32]{0:T(128)S(1)} %bitcast.22, f32[3,32,128]{2,1,0:T(8,128)S(1)} %get-tuple-element.67.own_ref, bf16[3,3,32,128]{3,2,1,0:T(8,128)(2,1)S(1)} %shard_map.112.row_ref, ...), custom_call_target="tpu_custom_call" | custom-call | flops 70000000 | bytes 2000000 | tf_op jit(solution)/shard_map/pallas_call | solution.py:780
  65.1 0.6 copy.14
  (33 shorter events, 0.1 us)
Async XLA Ops:
  0.0 26.3 %copy-start = (bf16[3,64,576]{2,1,0:T(8,128)(2,1)S(1)}, bf16[3,64,576]{2,1,0:T(8,128)(2,1)}, u32[]{:S(2)}) copy-start(bf16[3,64,576]{2,1,0:T(8,128)(2,1)} %param.18) | copy-start | bytes 663556
  3.9 7.8 %collective-permute-start.2 = (bf16[528,128]{1,0:T(8,128)(2,1)}, bf16[528,128]{1,0:T(8,128)(2,1)S(1)}, u32[]{:S(2)}, u32[]{:S(2)}) collective-permute-start(bf16[528,128]{1,0:T(8,128)(2,1)} %get-tuple-element.39), channel_id=1, source_target_pairs={{0,1},{1,0},{2,3},{3,2},{4,5},{5,4},{6,7},{7,6},{8,16},{9,17},{10,... | collective-permute-start | bytes 405512 | tf_op jit(solution)/shard_map/ppermute | solution.py:635
  7.9 5.3 %collective-permute-start.3 = (bf16[528,128]{1,0:T(8,128)(2,1)}, bf16[528,128]{1,0:T(8,128)(2,1)S(1)}, u32[]{:S(2)}, u32[]{:S(2)}) collective-permute-start(bf16[528,128]{1,0:T(8,128)(2,1)} %get-tuple-element.40), channel_id=1, source_target_pairs={{0,8},{1,9},{2,10},{3,11},{4,12},{5,13},{6,14},{7,15},{8,0},{9,1},... | collective-permute-start | bytes 405512 | tf_op jit(solution)/shard_map/ppermute | solution.py:635
  7.9 6.8 %collective-permute-start.4 = (bf16[528,128]{1,0:T(8,128)(2,1)}, bf16[528,128]{1,0:T(8,128)(2,1)S(1)}, u32[]{:S(2)}, u32[]{:S(2)}) collective-permute-start(bf16[528,128]{1,0:T(8,128)(2,1)} %get-tuple-element.41), channel_id=1, source_target_pairs={{0,8},{1,2},{2,1},{3,4},{4,3},{5,6},{6,5},{7,15},{8,0},{9,10},{10,... | collective-permute-start | bytes 405512 | tf_op jit(solution)/shard_map/ppermute | solution.py:635
  9.9 8.1 %collective-permute-start.5 = (bf16[528,128]{1,0:T(8,128)(2,1)}, bf16[528,128]{1,0:T(8,128)(2,1)S(1)}, u32[]{:S(2)}, u32[]{:S(2)}) collective-permute-start(bf16[528,128]{1,0:T(8,128)(2,1)} %get-tuple-element.42), channel_id=1, source_target_pairs={{0,1},{1,0},{2,3},{3,2},{4,5},{5,4},{6,7},{7,6},{8,9},{9,8},{10,11... | collective-permute-start | bytes 405512 | tf_op jit(solution)/shard_map/ppermute | solution.py:635
  9.9 8.9 %collective-permute-start.6 = (bf16[528,128]{1,0:T(8,128)(2,1)}, bf16[528,128]{1,0:T(8,128)(2,1)S(1)}, u32[]{:S(2)}, u32[]{:S(2)}) collective-permute-start(bf16[528,128]{1,0:T(8,128)(2,1)} %get-tuple-element.43), channel_id=1, source_target_pairs={{0,1},{1,0},{2,3},{3,2},{4,5},{5,4},{6,7},{7,6},{8,17},{9,18},{10,... | collective-permute-start | bytes 405512 | tf_op jit(solution)/shard_map/ppermute | solution.py:635
  11.7 7.1 %collective-permute-start.7 = (bf16[528,128]{1,0:T(8,128)(2,1)}, bf16[528,128]{1,0:T(8,128)(2,1)S(1)}, u32[]{:S(2)}, u32[]{:S(2)}) collective-permute-start(bf16[528,128]{1,0:T(8,128)(2,1)} %get-tuple-element.44), channel_id=1, source_target_pairs={{0,9},{1,10},{2,11},{3,12},{4,13},{5,14},{6,15},{7,23},{8,24},{9,0... | collective-permute-start | bytes 405512 | tf_op jit(solution)/shard_map/ppermute | solution.py:635
  13.1 9.3 %collective-permute-start = (bf16[528,128]{1,0:T(8,128)(2,1)}, bf16[528,128]{1,0:T(8,128)(2,1)S(1)}, u32[]{:S(2)}, u32[]{:S(2)}) collective-permute-start(bf16[528,128]{1,0:T(8,128)(2,1)} %get-tuple-element.37), channel_id=1, source_target_pairs={{0,1},{1,0},{2,3},{3,2},{4,5},{5,4},{6,7},{7,6},{8,24},{9,16},{10,... | collective-permute-start | bytes 405512 | tf_op jit(solution)/shard_map/ppermute | solution.py:635
  14.6 8.8 %collective-permute-start.1 = (bf16[528,128]{1,0:T(8,128)(2,1)}, bf16[528,128]{1,0:T(8,128)(2,1)S(1)}, u32[]{:S(2)}, u32[]{:S(2)}) collective-permute-start(bf16[528,128]{1,0:T(8,128)(2,1)} %get-tuple-element.38), channel_id=1, source_target_pairs={{0,15},{1,8},{2,9},{3,10},{4,11},{5,12},{6,13},{7,14},{8,1},{9,2},... | collective-permute-start | bytes 405512 | tf_op jit(solution)/shard_map/ppermute | solution.py:635
  15.8 0.9 %copy-start.8 = (bf16[528,128]{1,0:T(8,128)(2,1)S(1)}, bf16[528,128]{1,0:T(8,128)(2,1)}, u32[]{:S(2)}) copy-start(bf16[528,128]{1,0:T(8,128)(2,1)} %get-tuple-element.45.refs_0_) | copy-start | bytes 405508
  17.9 8.4 %copy-start.9 = (f32[3,64]{1,0:T(4,128)S(1)}, f32[3,64]{1,0:T(4,128)}, u32[]{:S(2)}) copy-start(f32[3,64]{1,0:T(4,128)} %param.19) | copy-start | bytes 2308
  24.0 9.1 %copy-start.2 = (bf16[3,64,576]{2,1,0:T(8,128)(2,1)S(1)}, bf16[3,64,576]{2,1,0:T(8,128)(2,1)}, u32[]{:S(2)}) copy-start(bf16[3,64,576]{2,1,0:T(8,128)(2,1)} %param.16) | copy-start | bytes 663556
  24.0 8.1 %collective-permute-start.8 = (bf16[8,64,128]{2,1,0:T(8,128)(2,1)S(1)}, bf16[8,64,128]{2,1,0:T(8,128)(2,1)S(1)}, u32[]{:S(2)}, u32[]{:S(2)}) collective-permute-start(bf16[8,64,128]{2,1,0:T(8,128)(2,1)S(1)} %get-tuple-element.47), channel_id=1, source_target_pairs={{0,1},{1,0},{2,3},{3,2},{4,5},{5,4},{6,7},{7,6},{8,16},{9,17},{10,... | collective-permute-start | bytes 393224 | tf_op jit(solution)/shard_map/ppermute | solution.py:635
  26.3 5.7 %collective-permute-start.9 = (bf16[8,64,128]{2,1,0:T(8,128)(2,1)S(1)}, bf16[8,64,128]{2,1,0:T(8,128)(2,1)S(1)}, u32[]{:S(2)}, u32[]{:S(2)}) collective-permute-start(bf16[8,64,128]{2,1,0:T(8,128)(2,1)S(1)} %get-tuple-element.48), channel_id=1, source_target_pairs={{0,8},{1,9},{2,10},{3,11},{4,12},{5,13},{6,14},{7,15},{8,0},{9,1},... | collective-permute-start | bytes 393224 | tf_op jit(solution)/shard_map/ppermute | solution.py:635
  32.2 4.7 %collective-permute-start.10 = (bf16[6,64,128]{2,1,0:T(8,128)(2,1)S(1)}, bf16[6,64,128]{2,1,0:T(8,128)(2,1)S(1)}, u32[]{:S(2)}, u32[]{:S(2)}) collective-permute-start(bf16[6,64,128]{2,1,0:T(8,128)(2,1)S(1)} %get-tuple-element.53), channel_id=1, source_target_pairs={{0,8},{1,2},{2,1},{3,4},{4,3},{5,6},{6,5},{7,15},{8,0},{9,10},{10,... | collective-permute-start | bytes 294920 | tf_op jit(solution)/shard_map/ppermute | solution.py:635
  32.8 4.1 %collective-permute-start.11 = (bf16[6,64,128]{2,1,0:T(8,128)(2,1)S(1)}, bf16[6,64,128]{2,1,0:T(8,128)(2,1)S(1)}, u32[]{:S(2)}, u32[]{:S(2)}) collective-permute-start(bf16[6,64,128]{2,1,0:T(8,128)(2,1)S(1)} %get-tuple-element.54), channel_id=1, source_target_pairs={{0,1},{1,0},{2,3},{3,2},{4,5},{5,4},{6,7},{7,6},{8,9},{9,8},{10,11... | collective-permute-start | bytes 294920 | tf_op jit(solution)/shard_map/ppermute | solution.py:635
  37.9 7.9 %copy-start.3 = (bf16[3,64,576]{2,1,0:T(8,128)(2,1)S(1)}, bf16[3,64,576]{2,1,0:T(8,128)(2,1)}, u32[]{:S(2)}) copy-start(bf16[3,64,576]{2,1,0:T(8,128)(2,1)} %param.17) | copy-start | bytes 663556
  37.9 7.3 %collective-permute-start.12 = (bf16[9,64,128]{2,1,0:T(8,128)(2,1)S(1)}, bf16[9,64,128]{2,1,0:T(8,128)(2,1)S(1)}, u32[]{:S(2)}, u32[]{:S(2)}) collective-permute-start(bf16[9,64,128]{2,1,0:T(8,128)(2,1)S(1)} %get-tuple-element.57), channel_id=1, source_target_pairs={{0,1},{1,0},{2,3},{3,2},{4,5},{5,4},{6,7},{7,6},{8,16},{9,17},{10,... | collective-permute-start | bytes 442376 | tf_op jit(solution)/shard_map/ppermute | solution.py:635
  39.7 5.5 %collective-permute-start.13 = (bf16[9,64,128]{2,1,0:T(8,128)(2,1)S(1)}, bf16[9,64,128]{2,1,0:T(8,128)(2,1)S(1)}, u32[]{:S(2)}, u32[]{:S(2)}) collective-permute-start(bf16[9,64,128]{2,1,0:T(8,128)(2,1)S(1)} %get-tuple-element.58), channel_id=1, source_target_pairs={{0,8},{1,9},{2,10},{3,11},{4,12},{5,13},{6,14},{7,15},{8,0},{9,1},... | collective-permute-start | bytes 442376 | tf_op jit(solution)/shard_map/ppermute | solution.py:635
  45.4 5.9 %collective-permute-start.14 = (bf16[13,64,128]{2,1,0:T(8,128)(2,1)S(1)}, bf16[13,64,128]{2,1,0:T(8,128)(2,1)S(1)}, u32[]{:S(2)}, u32[]{:S(2)}) collective-permute-start(bf16[13,64,128]{2,1,0:T(8,128)(2,1)S(1)} %get-tuple-element.65), channel_id=1, source_target_pairs={{0,8},{1,2},{2,1},{3,4},{4,3},{5,6},{6,5},{7,15},{8,0},{9,10},{10,... | collective-permute-start | bytes 638984 | tf_op jit(solution)/shard_map/ppermute | solution.py:635
  45.5 5.8 %collective-permute-start.15 = (bf16[13,64,128]{2,1,0:T(8,128)(2,1)S(1)}, bf16[13,64,128]{2,1,0:T(8,128)(2,1)S(1)}, u32[]{:S(2)}, u32[]{:S(2)}) collective-permute-start(bf16[13,64,128]{2,1,0:T(8,128)(2,1)S(1)} %get-tuple-element.66), channel_id=1, source_target_pairs={{0,1},{1,0},{2,3},{3,2},{4,5},{5,4},{6,7},{7,6},{8,9},{9,8},{10,11... | collective-permute-start | bytes 638984 | tf_op jit(solution)/shard_map/ppermute | solution.py:635
  51.3 12.3 %copy-start.1 = (bf16[32,128,128]{2,1,0:T(8,128)(2,1)S(1)}, bf16[32,128,128]{2,1,0:T(8,128)(2,1)}, u32[]{:S(2)}) copy-start(bf16[32,128,128]{2,1,0:T(8,128)(2,1)} %weight_ref.1) | copy-start | bytes 3145732
  51.3 12.3 %copy-start.4 = (s32[32,128]{1,0:T(8,128)S(1)}, s32[32,128]{1,0:T(8,128)}, u32[]{:S(2)}) copy-start(s32[32,128]{1,0:T(8,128)} %nodes_ref.3) | copy-start | bytes 49156
  51.3 12.3 %copy-start.5 = (s32[16]{0:T(128)S(1)}, s32[16]{0:T(128)}, u32[]{:S(2)}) copy-start(s32[16]{0:T(128)} %counts_ref.3) | copy-start | bytes 196
  51.4 12.3 %copy-start.6 = (s32[32]{0:T(128)S(1)}, s32[32]{0:T(128)}, u32[]{:S(2)}) copy-start(s32[32]{0:T(128)} %block_ref.3) | copy-start | bytes 388
  51.4 12.3 %copy-start.7 = (s32[32,1]{0,1:T(1,128)S(1)}, s32[32,1]{0,1:T(1,128)}, u32[]{:S(2)}) copy-start(s32[32,1]{0,1:T(1,128)} %param.13) | copy-start | bytes 388
  53.1 3.9 %collective-permute-start.17 = (bf16[3,32,128]{2,1,0:T(8,128)(2,1)S(1)}, bf16[3,32,128]{2,1,0:T(8,128)(2,1)S(1)}, u32[]{:S(2)}, u32[]{:S(2)}) collective-permute-start(bf16[3,32,128]{2,1,0:T(8,128)(2,1)S(1)} %get-tuple-element.68.own_ref), channel_id=1, source_target_pairs={{0,8},{1,9},{2,10},{3,11},{4,12},{5,13},{6,14},{7,15},{8,0},{9,1},... | collective-permute-start | bytes 73736 | tf_op jit(solution)/shard_map/ppermute | solution.py:635
  53.2 6.0 %collective-permute-start.16 = (bf16[3,32,128]{2,1,0:T(8,128)(2,1)S(1)}, bf16[3,32,128]{2,1,0:T(8,128)(2,1)S(1)}, u32[]{:S(2)}, u32[]{:S(2)}) collective-permute-start(bf16[3,32,128]{2,1,0:T(8,128)(2,1)S(1)} %get-tuple-element.68.own_ref), channel_id=1, source_target_pairs={{0,1},{1,0},{2,3},{3,2},{4,5},{5,4},{6,7},{7,6},{8,16},{9,17},{10,... | collective-permute-start | bytes 73736 | tf_op jit(solution)/shard_map/ppermute | solution.py:635
  59.2 1.3 %collective-permute-start.19 = (bf16[3,3,32,128]{3,2,1,0:T(8,128)(2,1)S(1)}, bf16[3,3,32,128]{3,2,1,0:T(8,128)(2,1)S(1)}, u32[]{:S(2)}, u32[]{:S(2)}) collective-permute-start(bf16[3,3,32,128]{3,2,1,0:T(8,128)(2,1)S(1)} %shard_map.112.row_ref), channel_id=1, source_target_pairs={{0,1},{1,0},{2,3},{3,2},{4,5},{5,4},{6,7},{7,6},{8,9},{9,8},{10,11... | collective-permute-start | bytes 221192 | tf_op jit(solution)/shard_map/ppermute | solution.py:635
  59.2 4.4 %collective-permute-start.18 = (bf16[3,3,32,128]{3,2,1,0:T(8,128)(2,1)S(1)}, bf16[3,3,32,128]{3,2,1,0:T(8,128)(2,1)S(1)}, u32[]{:S(2)}, u32[]{:S(2)}) collective-permute-start(bf16[3,3,32,128]{3,2,1,0:T(8,128)(2,1)S(1)} %shard_map.112.row_ref), channel_id=1, source_target_pairs={{0,8},{1,2},{2,1},{3,4},{4,3},{5,6},{6,5},{7,15},{8,0},{9,10},{10,... | collective-permute-start | bytes 221192 | tf_op jit(solution)/shard_map/ppermute | solution.py:635

commit v4 on v3

--- a/solution.py
+++ b/solution.py
@@ -16,8 +16,8 @@
 TILE_X = 4
 TILE_Y = 8
 SLOTS = 8
-GROUP = 4
 CHUNKS = 4
+PADDED = 224
 OUTER = (0, TILE_X - 1)
 MIDDLE = tuple(range(1, TILE_X - 1))
 VMEM_LIMIT = 40 * 1024 * 1024
@@ -94,6 +94,10 @@
         c.wait()
 
 
+def group_size(rows):
+    return 8 if rows is None else 4
+
+
 def scatter_kernel(parts, first, rows, *refs):
     got = refs[:parts]
     refs = refs[parts:]
@@ -133,11 +137,13 @@
         else:
             acc[piece, :] = before[t * CHAN : (t + 1) * CHAN, :]
 
+    size = group_size(rows)
+
     def step(g, carry):
         left = [[] for _ in groups]
         right = []
-        for j in range(GROUP):
-            e = g * GROUP + j
+        for j in range(size):
+            e = g * size + j
             value = values[e]
             hi = jnp.broadcast_to(hi_all[pl.ds(e, 1), :], (CHAN, LANES)).astype(BF)
             lo = lo_all[pl.ds(e, 1), :]
@@ -149,7 +155,7 @@
         acc[...] += lax.dot_general(a, b, NT, preferred_element_type=F32)
         return carry
 
-    lax.fori_loop(0, (filled + GROUP - 1) // GROUP, step, 0)
+    lax.fori_loop(0, (filled + size - 1) // size, step, 0)
     if rows is None:
         return
     for i in range(len(groups)):
@@ -161,7 +167,7 @@
 
 
 def scatter(parts, before, rows=None):
-    most = len(parts) * SLOTS + GROUP
+    most = len(parts) * SLOTS + group_size(rows)
     sums = ((16 * CHAN, 256), F32)
     first = before is None
     if rows is None:
@@ -398,7 +404,7 @@
             low_ref[x * half_y + y] = result
             high_ref[x * half_y + y] = result
     for side, ref, x, a in ((0, low_ref, 0, 2), (1, high_ref, TILE_X - 1, 0)):
-        weight = out_weight_ref[a * 72 : a * 72 + 72]
+        weight = out_weight_ref[a * 72 : a * 72 + 80]
         for y in range(0, TILE_Y, 2):
             rhs = jnp.concatenate([act_ref[x, y], act_ref[x, y + 1]], axis=1)
             prod = jnp.dot(weight, rhs, preferred_element_type=F32)
@@ -557,7 +563,7 @@
 
 
 def gather_kernel(
-    counts_ref, block_ref, dest_ref, own_ref, row_ref, y_one_ref, y_two_ref,
+    counts_ref, block_ref, dest_ref, own_ref, row_ref, y_two_ref, y_one_ref,
     nodes_ref, weight_ref, out_ref, frame, total,
 ):
     entries = weight_ref.shape[0]
@@ -660,6 +666,7 @@
     out_weight = (
         both.reshape(3, 8, 9, CHAN).transpose(0, 2, 1, 3).reshape(27 * 8, CHAN).astype(BF)
     )
+    out_weight = jnp.pad(out_weight, ((0, PADDED - 27 * 8), (0, 0)))
 
     packed = (SLOTS * CHAN + 16, LANES)
     sent = call(
@@ -721,7 +728,7 @@
         [VM] * 8,
         [
             pltpu.VMEM((TILE_X + 2, 2, 3 * CHAN, LANES), BF),
-            pltpu.VMEM((2, TILE_Y, 72, LANES), F32),
+            pltpu.VMEM((2, TILE_Y, 80, LANES), F32),
             pltpu.VMEM((9, *column), BF),
             pltpu.VMEM((9, *column), BF),
         ],
@@ -733,7 +740,7 @@
         rim_kernel,
         [((24, LANES), F32)] * 2,
         [VM] * 2,
-        [pltpu.VMEM((TILE_X, 27 * 8, LANES), F32)],
+        [pltpu.VMEM((TILE_X, PADDED, LANES), F32)],
         1000000000,
     )(act, out_weight)
     xl, xh, one, two = call(
@@ -748,7 +755,7 @@
         inner_mid_kernel,
         [
             ((6, TILE_Y // 2, 3 * CHAN, LANES), BF),
-            ((TILE_X + 2, 4, 27 * 8, LANES), F32),
+            ((TILE_X + 2, 4, PADDED, LANES), F32),
         ],
         [VM] * 6,
         [pltpu.VMEM((4, 2, *column), BF)],
@@ -761,7 +768,7 @@
         [
             pltpu.VMEM((6, 4, 3 * CHAN, LANES), BF),
             pltpu.VMEM((4, 4, *column), BF),
-            pltpu.VMEM((TILE_X + 2, 6, 27 * 8, LANES), F32),
+            pltpu.VMEM((TILE_X + 2, 6, PADDED, LANES), F32),
             pltpu.VMEM((13, *column), BF),
             pltpu.VMEM((13, *column), BF),
         ],
@@ -787,7 +794,7 @@
         ],
         70000000,
     )(
-        block_counts, entry_block, dest, field, row, one, two, entry_nodes, entry_weights
+        block_counts, entry_block, dest, field, row, two, one, entry_nodes, entry_weights
     )[0]
 
 

time: 66.5 us -> 65.8 us (0.989)
  waiting for transfers between devices: 29.8 us -> 30.7 us
    ppermute x20, waiting for transfers between devices: 29.8 us -> 30.7 us  [swapped(): return lax.ppermute(value, ('gx', 'gy'), pairs)]
  transfers between devices with their start and end apart: 20 -> 20, of which waited for: 13 -> 12; matrix products, arithmetic and copies ran while one was open for 1% -> 1% of each run, Pallas kernels for 11% -> 10%
where the time goes in v4:
time: 65.8 us; the launch traced here: 65.7 us
  waiting for transfers between devices  30.7 us (47%)
  starting transfers between devices  17.1 us (26%)
  Pallas kernels  15.5 us (24%)
  local copies, waits for them, and re-layouts  1.79 us (3%)
    ppermute x20, waiting for transfers between devices, swapped(): return lax.ppermute(value, ('gx', 'gy'), pairs)  30.7 us
    ppermute x20, starting transfers between devices, swapped(): return lax.ppermute(value, ('gx', 'gy'), pairs)  17.1 us
    pallas_call x4, Pallas kernels, scatter(): call(functools.partial(scatter_kernel, len(parts), first, rows), outs, [V...  3.93 us
    pallas_call x1, Pallas kernels, shards(): call(partial_kernel, [(packed, BF)] * 9, [SM] * 3 + [HB, VM, HB], [pltpu....  3.86 us
    pallas_call x1, Pallas kernels, shards(): call(outer_mid_kernel, [((3, TILE_X * TILE_Y, LANES), F32), ((3, TILE_X *...  1.71 us
    pallas_call x1, Pallas kernels, shards(): call(inner_mid_kernel, [((6, TILE_Y // 2, 3 * CHAN, LANES), BF), ((TILE_X...  1.51 us
    pallas_call x1, Pallas kernels, shards(): call(gather_kernel, [((blocks, 3, LANES), F32)], [SM] * 3 + [VM] * 6, [pl...  1.42 us
    pallas_call x1, Pallas kernels, shards(): call(inner_conv_kernel, [((TILE_X + 2, TILE_Y, 3 * CHAN, LANES), BF), ((T...  1.41 us
  transfers between devices with their start and end apart: 20, of which 12 were waited for; matrix products, arithmetic and copies ran while one was open for 1% of the time, Pallas kernels for 10%

profile of v4, /device:TPU:16, one launch (start us, length us, event | category | flops | bytes accessed | tf_op | source)
XLA Modules:
  0.0 65.7 jit_solution(16254645970299946567)
XLA Ops:
  0.0 3.9 %shard_map.100 = (bf16[528,128]{1,0:T(8,128)(2,1)}, bf16[528,128]{1,0:T(8,128)(2,1)}, bf16[528,128]{1,0:T(8,128)(2,1)}, bf16[528,128]{1,0:T(8,128)(2,1)}, bf16[5...) custom-call(s32[16]{0:T(128)} %counts_ref.3, ...), custom_call_target="tpu_custom_call" | custom-call | flops 70000000 | bytes 2000000 | tf_op jit(solution)/shard_map/pallas_call | solution.py:672
  3.9 4.0 %collective-permute-start.2 = (bf16[528,128]{1,0:T(8,128)(2,1)}, bf16[528,128]{1,0:T(8,128)(2,1)S(1)}, u32[]{:S(2)}, u32[]{:S(2)}) collective-permute-start(bf16[528,128]{1,0:T(8,128)(2,1)} %get-tuple-element.39), channel_id=1, source_target_pairs={{0,1},{1,0},{2,3},{3,2},{4,5},{5,4},{6,7},{7,6},{8,16},{9,17},{10,... | collective-permute-start | bytes 405512 | tf_op jit(solution)/shard_map/ppermute | solution.py:641
  7.9 2.0 %collective-permute-start.4 = (bf16[528,128]{1,0:T(8,128)(2,1)}, bf16[528,128]{1,0:T(8,128)(2,1)S(1)}, u32[]{:S(2)}, u32[]{:S(2)}) collective-permute-start(bf16[528,128]{1,0:T(8,128)(2,1)} %get-tuple-element.41), channel_id=1, source_target_pairs={{0,8},{1,2},{2,1},{3,4},{4,3},{5,6},{6,5},{7,15},{8,0},{9,10},{10,... | collective-permute-start | bytes 405512 | tf_op jit(solution)/shard_map/ppermute | solution.py:641
  9.9 1.3 %collective-permute-start.6 = (bf16[528,128]{1,0:T(8,128)(2,1)}, bf16[528,128]{1,0:T(8,128)(2,1)S(1)}, u32[]{:S(2)}, u32[]{:S(2)}) collective-permute-start(bf16[528,128]{1,0:T(8,128)(2,1)} %get-tuple-element.43), channel_id=1, source_target_pairs={{0,1},{1,0},{2,3},{3,2},{4,5},{5,4},{6,7},{7,6},{8,17},{9,18},{10,... | collective-permute-start | bytes 405512 | tf_op jit(solution)/shard_map/ppermute | solution.py:641
  11.2 0.5 collective-permute-done.2.refs_0_
  11.7 0.1 collective-permute-start.7
  11.8 1.4 %collective-permute-done.3.refs_1_ = bf16[528,128]{1,0:T(8,128)(2,1)S(1)} collective-permute-done((bf16[528,128]{1,0:T(8,128)(2,1)}, bf16[528,128]{1,0:T(8,128)(2,1)S(1)}, u32[]{:S(2)}, u32[]{:S(2)}) %collective-permute-start.3) | collective-permute-done | bytes 135200 | tf_op jit(solution)/shard_map/ppermute | solution.py:641
  13.1 1.5 %collective-permute-start = (bf16[528,128]{1,0:T(8,128)(2,1)}, bf16[528,128]{1,0:T(8,128)(2,1)S(1)}, u32[]{:S(2)}, u32[]{:S(2)}) collective-permute-start(bf16[528,128]{1,0:T(8,128)(2,1)} %get-tuple-element.37), channel_id=1, source_target_pairs={{0,1},{1,0},{2,3},{3,2},{4,5},{5,4},{6,7},{7,6},{8,24},{9,16},{10,... | collective-permute-start | bytes 405512 | tf_op jit(solution)/shard_map/ppermute | solution.py:641
  14.6 1.2 %collective-permute-start.1 = (bf16[528,128]{1,0:T(8,128)(2,1)}, bf16[528,128]{1,0:T(8,128)(2,1)S(1)}, u32[]{:S(2)}, u32[]{:S(2)}) collective-permute-start(bf16[528,128]{1,0:T(8,128)(2,1)} %get-tuple-element.38), channel_id=1, source_target_pairs={{0,15},{1,8},{2,9},{3,10},{4,11},{5,12},{6,13},{7,14},{8,1},{9,2},... | collective-permute-start | bytes 405512 | tf_op jit(solution)/shard_map/ppermute | solution.py:641
  15.8 0.9 %copy-done.8 = bf16[528,128]{1,0:T(8,128)(2,1)S(1)} copy-done((bf16[528,128]{1,0:T(8,128)(2,1)S(1)}, bf16[528,128]{1,0:T(8,128)(2,1)}, u32[]{:S(2)}) %copy-start.8) | copy-done | bytes 135192
  16.7 1.0 %shard_map.101.refs_6_ = f32[1024,256]{1,0:T(8,128)S(1)} custom-call(bf16[528,128]{1,0:T(8,128)(2,1)S(1)} %copy-done.8), custom_call_target="tpu_custom_call" | custom-call | flops 800000000 | bytes 2000000 | tf_op jit(solution)/shard_map/pallas_call | solution.py:181
  17.8 1.0 %collective-permute-done.6.refs_4_ = bf16[528,128]{1,0:T(8,128)(2,1)S(1)} collective-permute-done((bf16[528,128]{1,0:T(8,128)(2,1)}, bf16[528,128]{1,0:T(8,128)(2,1)S(1)}, u32[]{:S(2)}, u32[]{:S(2)}) %collective-permute-start.6) | collective-permute-done | bytes 135200 | tf_op jit(solution)/shard_map/ppermute | solution.py:641
  18.8 1.8 %shard_map.102.refs_2_ = f32[1024,256]{1,0:T(8,128)S(1)} custom-call(bf16[528,128]{1,0:T(8,128)(2,1)S(1)} %collective-permute-done.2.refs_0_, bf16[528,128]{1,0:T(8,128)(2,1)S(1)} %collective-permute-done.3.refs_1_, bf16[528,128]{1,0:T(8,128)(2,1)S(1)} %collective-permute-done.4.refs_2_, bf16[528,128]{1,0:T(8,128)(2,1)S(1)} %collective-permute-done.5.refs_3_, ...), custom_call_target="tpu_custom_call" | custom-call | flops 800000000 | bytes 2000000 | tf_op jit(solution)/shard_map/pallas_call | solution.py:181
  20.6 1.7 %collective-permute-done.refs_0_ = bf16[528,128]{1,0:T(8,128)(2,1)S(1)} collective-permute-done((bf16[528,128]{1,0:T(8,128)(2,1)}, bf16[528,128]{1,0:T(8,128)(2,1)S(1)}, u32[]{:S(2)}, u32[]{:S(2)}) %collective-permute-start) | collective-permute-done | bytes 135200 | tf_op jit(solution)/shard_map/ppermute | solution.py:641
  22.4 1.0 %collective-permute-done.1.refs_1_ = bf16[528,128]{1,0:T(8,128)(2,1)S(1)} collective-permute-done((bf16[528,128]{1,0:T(8,128)(2,1)}, bf16[528,128]{1,0:T(8,128)(2,1)S(1)}, u32[]{:S(2)}, u32[]{:S(2)}) %collective-permute-start.1) | collective-permute-done | bytes 135200 | tf_op jit(solution)/shard_map/ppermute | solution.py:641
  23.4 0.6 shard_map.103
  24.0 0.0 copy-start.2
  24.0 2.3 %collective-permute-start.8 = (bf16[8,64,128]{2,1,0:T(8,128)(2,1)S(1)}, bf16[8,64,128]{2,1,0:T(8,128)(2,1)S(1)}, u32[]{:S(2)}, u32[]{:S(2)}) collective-permute-start(bf16[8,64,128]{2,1,0:T(8,128)(2,1)S(1)} %get-tuple-element.47), channel_id=1, source_target_pairs={{0,1},{1,0},{2,3},{3,2},{4,5},{5,4},{6,7},{7,6},{8,16},{9,17},{10,... | collective-permute-start | bytes 393224 | tf_op jit(solution)/shard_map/ppermute | solution.py:641
  26.3 0.2 collective-permute-start.9
  26.4 0.2 reduce-precision_convert_fusion
  26.7 0.1 pad.7.clone
  26.8 0.5 shard_map.104.middle_ref
  27.3 4.7 %collective-permute-done.8.one_ref = bf16[8,64,128]{2,1,0:T(8,128)(2,1)S(1)} collective-permute-done((bf16[8,64,128]{2,1,0:T(8,128)(2,1)S(1)}, bf16[8,64,128]{2,1,0:T(8,128)(2,1)S(1)}, u32[]{:S(2)}, u32[]{:S(2)}) %collective-permute-start.8) | collective-permute-done | bytes 131104 | tf_op jit(solution)/shard_map/ppermute | solution.py:641
  32.0 0.1 shard_map.105
  32.2 0.1 collective-permute-start.10
  32.3 0.1 collective-permute-start.11
  32.4 0.1 maximum_maximum_fusion
  32.4 0.1 convert_element_type.13
  32.6 1.4 %shard_map.106 = (bf16[6,8,192,128]{3,2,1,0:T(8,128)(2,1)S(1)}, bf16[4,6,64,128]{3,2,1,0:T(8,128)(2,1)S(1)}) custom-call(bf16[2,8,64,128]{3,2,1,0:T(8,128)(2,1)S(1)} %get-tuple-element.46.outer_ref, bf16[2,8,64,128]{3,2,1,0:T(8,128)(2,1)S(1)} %shard_map.104.middle_ref, bf16[8,64,128]{2,1,0:T(8,128)(2,1)S(1)} %get-tuple-element.49.xl_ref, ...), custom_call_target="tpu_custom_call" | custom-call | flops 1000000000 | bytes 2000000 | tf_op jit(solution)/shard_map/pallas_call | solution.py:710
  34.0 2.8 %collective-permute-done.10.y_one_ref = bf16[6,64,128]{2,1,0:T(8,128)(2,1)S(1)} collective-permute-done((bf16[6,64,128]{2,1,0:T(8,128)(2,1)S(1)}, bf16[6,64,128]{2,1,0:T(8,128)(2,1)S(1)}, u32[]{:S(2)}, u32[]{:S(2)}) %collective-permute-start.10) | collective-permute-done | bytes 98336 | tf_op jit(solution)/shard_map/ppermute | solution.py:641
  36.9 1.0 %shard_map.107 = (bf16[4,8,64,128]{3,2,1,0:T(8,128)(2,1)S(1)}, bf16[2,4,64,128]{3,2,1,0:T(8,128)(2,1)S(1)}, bf16[9,64,128]{2,1,0:T(8,128)(2,1)S(1)}, bf16[9,64,128]{2,1,0:T(8,128)(2,1)S(1)}) custom-call(bf16[2,8,64,128]{3,2,1,0:T(8,128)(2,1)S(1)} %get-tuple-element.46.outer_ref, bf16[2,8,64,128]{3,2,1,0:T(8,128)(2,1)S(1)} %shard_map.104.middle_ref, ...), custom_call_target="tpu_custom_call" | custom-call | flops 600000000 | bytes 2000000 | tf_op jit(solution)/shard_map/pallas_call | solution.py:720
  37.9 1.8 %collective-permute-start.12 = (bf16[9,64,128]{2,1,0:T(8,128)(2,1)S(1)}, bf16[9,64,128]{2,1,0:T(8,128)(2,1)S(1)}, u32[]{:S(2)}, u32[]{:S(2)}) collective-permute-start(bf16[9,64,128]{2,1,0:T(8,128)(2,1)S(1)} %get-tuple-element.57), channel_id=1, source_target_pairs={{0,1},{1,0},{2,3},{3,2},{4,5},{5,4},{6,7},{7,6},{8,16},{9,17},{10,... | collective-permute-start | bytes 442376 | tf_op jit(solution)/shard_map/ppermute | solution.py:641
  39.7 0.3 shard_map.108
  40.0 5.2 %collective-permute-done.12.one_ref = bf16[9,64,128]{2,1,0:T(8,128)(2,1)S(1)} collective-permute-done((bf16[9,64,128]{2,1,0:T(8,128)(2,1)S(1)}, bf16[9,64,128]{2,1,0:T(8,128)(2,1)S(1)}, u32[]{:S(2)}, u32[]{:S(2)}) %collective-permute-start.12) | collective-permute-done | bytes 147488 | tf_op jit(solution)/shard_map/ppermute | solution.py:641
  45.3 0.2 shard_map.109
  45.4 0.1 collective-permute-start.14
  45.5 0.3 collective-permute-start.15
  45.8 1.5 %shard_map.110 = (bf16[6,4,192,128]{3,2,1,0:T(8,128)(2,1)S(1)}, f32[6,4,224,128]{3,2,1,0:T(8,128)S(1)}) custom-call(bf16[2,4,64,128]{3,2,1,0:T(8,128)(2,1)S(1)} %get-tuple-element.56.coarse_ref, bf16[9,64,128]{2,1,0:T(8,128)(2,1)S(1)} %get-tuple-element.61.xl_ref, bf16[9,64,128]{2,1,0:T(8,128)(2,1)S(1)} %get-tuple-element.62.xh_ref, ...), custom_call_target="tpu_custom_call" | custom-call | flops 1000000000 | bytes 2000000 | tf_op jit(solution)/shard_map/pallas_call | solution.py:754
  47.3 4.0 %collective-permute-done.14.y_one_ref = bf16[13,64,128]{2,1,0:T(8,128)(2,1)S(1)} collective-permute-done((bf16[13,64,128]{2,1,0:T(8,128)(2,1)S(1)}, bf16[13,64,128]{2,1,0:T(8,128)(2,1)S(1)}, u32[]{:S(2)}, u32[]{:S(2)}) %collective-permute-start.14) | collective-permute-done | bytes 213024 | tf_op jit(solution)/shard_map/ppermute | solution.py:641
  51.4 1.7 %shard_map.111 = (f32[3,32,128]{2,1,0:T(8,128)S(1)}, bf16[3,32,128]{2,1,0:T(8,128)(2,1)S(1)}) custom-call(bf16[4,8,64,128]{3,2,1,0:T(8,128)(2,1)S(1)} %get-tuple-element.55.act_ref, bf16[6,4,192,128]{3,2,1,0:T(8,128)(2,1)S(1)} %get-tuple-element.63.stack, f32[6,4,224,128]{3,2,1,0:T(8,128)S(1)} %get-tuple-element.64.inner, ...), custom_call_target="tpu_custom_call" | custom-call | flops 1300000000 | bytes 2000000 | tf_op jit(solution)/shard_map/pallas_call | solution.py:764
  53.1 0.1 collective-permute-start.17
  53.2 2.1 %collective-permute-start.16 = (bf16[3,32,128]{2,1,0:T(8,128)(2,1)S(1)}, bf16[3,32,128]{2,1,0:T(8,128)(2,1)S(1)}, u32[]{:S(2)}, u32[]{:S(2)}) collective-permute-start(bf16[3,32,128]{2,1,0:T(8,128)(2,1)S(1)} %get-tuple-element.68.own_ref), channel_id=1, source_target_pairs={{0,1},{1,0},{2,3},{3,2},{4,5},{5,4},{6,7},{7,6},{8,16},{9,17},{10,... | collective-permute-start | bytes 73736 | tf_op jit(solution)/shard_map/ppermute | solution.py:641
  55.3 1.7 %collective-permute-done.17.two_ref = bf16[3,32,128]{2,1,0:T(8,128)(2,1)S(1)} collective-permute-done((bf16[3,32,128]{2,1,0:T(8,128)(2,1)S(1)}, bf16[3,32,128]{2,1,0:T(8,128)(2,1)S(1)}, u32[]{:S(2)}, u32[]{:S(2)}) %collective-permute-start.17) | collective-permute-done | bytes 24608 | tf_op jit(solution)/shard_map/ppermute | solution.py:641
  57.0 2.2 %collective-permute-done.16.one_ref = bf16[3,32,128]{2,1,0:T(8,128)(2,1)S(1)} collective-permute-done((bf16[3,32,128]{2,1,0:T(8,128)(2,1)S(1)}, bf16[3,32,128]{2,1,0:T(8,128)(2,1)S(1)}, u32[]{:S(2)}, u32[]{:S(2)}) %collective-permute-start.16) | collective-permute-done | bytes 24608 | tf_op jit(solution)/shard_map/ppermute | solution.py:641
  59.3 0.1 collective-permute-start.18
  59.4 4.3 %collective-permute-done.19.y_one_ref = bf16[3,3,32,128]{3,2,1,0:T(8,128)(2,1)S(1)} collective-permute-done((bf16[3,3,32,128]{3,2,1,0:T(8,128)(2,1)S(1)}, bf16[3,3,32,128]{3,2,1,0:T(8,128)(2,1)S(1)}, u32[]{:S(2)}, u32[]{:S(2)}) %collective-permute-start.19) | collective-permute-done | bytes 73760 | tf_op jit(solution)/shard_map/ppermute | solution.py:641
  63.6 1.4 %shard_map.113 = f32[16,3,128]{2,1,0:T(4,128)S(1)} custom-call(s32[16]{0:T(128)S(1)} %copy-done.5, s32[32]{0:T(128)S(1)} %copy-done.6, s32[32]{0:T(128)S(1)} %bitcast.18, f32[3,32,128]{2,1,0:T(8,128)S(1)} %get-tuple-element.67.own_ref, bf16[3,3,32,128]{3,2,1,0:T(8,128)(2,1)S(1)} %shard_map.112.row_ref, ...), custom_call_target="tpu_custom_call" | custom-call | flops 70000000 | bytes 2000000 | tf_op jit(solution)/shard_map/pallas_call | solution.py:787
  65.1 0.6 copy.14
  (34 shorter events, 0.1 us)
Async XLA Ops:
  0.0 26.4 %copy-start = (bf16[3,64,576]{2,1,0:T(8,128)(2,1)S(1)}, bf16[3,64,576]{2,1,0:T(8,128)(2,1)}, u32[]{:S(2)}) copy-start(bf16[3,64,576]{2,1,0:T(8,128)(2,1)} %param.18) | copy-start | bytes 663556
  3.9 7.8 %collective-permute-start.2 = (bf16[528,128]{1,0:T(8,128)(2,1)}, bf16[528,128]{1,0:T(8,128)(2,1)S(1)}, u32[]{:S(2)}, u32[]{:S(2)}) collective-permute-start(bf16[528,128]{1,0:T(8,128)(2,1)} %get-tuple-element.39), channel_id=1, source_target_pairs={{0,1},{1,0},{2,3},{3,2},{4,5},{5,4},{6,7},{7,6},{8,16},{9,17},{10,... | collective-permute-start | bytes 405512 | tf_op jit(solution)/shard_map/ppermute | solution.py:641
  7.9 5.3 %collective-permute-start.3 = (bf16[528,128]{1,0:T(8,128)(2,1)}, bf16[528,128]{1,0:T(8,128)(2,1)S(1)}, u32[]{:S(2)}, u32[]{:S(2)}) collective-permute-start(bf16[528,128]{1,0:T(8,128)(2,1)} %get-tuple-element.40), channel_id=1, source_target_pairs={{0,8},{1,9},{2,10},{3,11},{4,12},{5,13},{6,14},{7,15},{8,0},{9,1},... | collective-permute-start | bytes 405512 | tf_op jit(solution)/shard_map/ppermute | solution.py:641
  7.9 6.8 %collective-permute-start.4 = (bf16[528,128]{1,0:T(8,128)(2,1)}, bf16[528,128]{1,0:T(8,128)(2,1)S(1)}, u32[]{:S(2)}, u32[]{:S(2)}) collective-permute-start(bf16[528,128]{1,0:T(8,128)(2,1)} %get-tuple-element.41), channel_id=1, source_target_pairs={{0,8},{1,2},{2,1},{3,4},{4,3},{5,6},{6,5},{7,15},{8,0},{9,10},{10,... | collective-permute-start | bytes 405512 | tf_op jit(solution)/shard_map/ppermute | solution.py:641
  9.9 7.9 %collective-permute-start.5 = (bf16[528,128]{1,0:T(8,128)(2,1)}, bf16[528,128]{1,0:T(8,128)(2,1)S(1)}, u32[]{:S(2)}, u32[]{:S(2)}) collective-permute-start(bf16[528,128]{1,0:T(8,128)(2,1)} %get-tuple-element.42), channel_id=1, source_target_pairs={{0,1},{1,0},{2,3},{3,2},{4,5},{5,4},{6,7},{7,6},{8,9},{9,8},{10,11... | collective-permute-start | bytes 405512 | tf_op jit(solution)/shard_map/ppermute | solution.py:641
  9.9 8.9 %collective-permute-start.6 = (bf16[528,128]{1,0:T(8,128)(2,1)}, bf16[528,128]{1,0:T(8,128)(2,1)S(1)}, u32[]{:S(2)}, u32[]{:S(2)}) collective-permute-start(bf16[528,128]{1,0:T(8,128)(2,1)} %get-tuple-element.43), channel_id=1, source_target_pairs={{0,1},{1,0},{2,3},{3,2},{4,5},{5,4},{6,7},{7,6},{8,17},{9,18},{10,... | collective-permute-start | bytes 405512 | tf_op jit(solution)/shard_map/ppermute | solution.py:641
  11.7 7.1 %collective-permute-start.7 = (bf16[528,128]{1,0:T(8,128)(2,1)}, bf16[528,128]{1,0:T(8,128)(2,1)S(1)}, u32[]{:S(2)}, u32[]{:S(2)}) collective-permute-start(bf16[528,128]{1,0:T(8,128)(2,1)} %get-tuple-element.44), channel_id=1, source_target_pairs={{0,9},{1,10},{2,11},{3,12},{4,13},{5,14},{6,15},{7,23},{8,24},{9,0... | collective-permute-start | bytes 405512 | tf_op jit(solution)/shard_map/ppermute | solution.py:641
  13.1 9.3 %collective-permute-start = (bf16[528,128]{1,0:T(8,128)(2,1)}, bf16[528,128]{1,0:T(8,128)(2,1)S(1)}, u32[]{:S(2)}, u32[]{:S(2)}) collective-permute-start(bf16[528,128]{1,0:T(8,128)(2,1)} %get-tuple-element.37), channel_id=1, source_target_pairs={{0,1},{1,0},{2,3},{3,2},{4,5},{5,4},{6,7},{7,6},{8,24},{9,16},{10,... | collective-permute-start | bytes 405512 | tf_op jit(solution)/shard_map/ppermute | solution.py:641
  14.6 8.8 %collective-permute-start.1 = (bf16[528,128]{1,0:T(8,128)(2,1)}, bf16[528,128]{1,0:T(8,128)(2,1)S(1)}, u32[]{:S(2)}, u32[]{:S(2)}) collective-permute-start(bf16[528,128]{1,0:T(8,128)(2,1)} %get-tuple-element.38), channel_id=1, source_target_pairs={{0,15},{1,8},{2,9},{3,10},{4,11},{5,12},{6,13},{7,14},{8,1},{9,2},... | collective-permute-start | bytes 405512 | tf_op jit(solution)/shard_map/ppermute | solution.py:641
  15.8 0.9 %copy-start.8 = (bf16[528,128]{1,0:T(8,128)(2,1)S(1)}, bf16[528,128]{1,0:T(8,128)(2,1)}, u32[]{:S(2)}) copy-start(bf16[528,128]{1,0:T(8,128)(2,1)} %get-tuple-element.45.refs_0_) | copy-start | bytes 405508
  17.7 8.7 %copy-start.9 = (f32[3,64]{1,0:T(4,128)S(1)}, f32[3,64]{1,0:T(4,128)}, u32[]{:S(2)}) copy-start(f32[3,64]{1,0:T(4,128)} %param.19) | copy-start | bytes 2308
  24.0 8.6 %copy-start.2 = (bf16[3,64,576]{2,1,0:T(8,128)(2,1)S(1)}, bf16[3,64,576]{2,1,0:T(8,128)(2,1)}, u32[]{:S(2)}) copy-start(bf16[3,64,576]{2,1,0:T(8,128)(2,1)} %param.16) | copy-start | bytes 663556
  24.0 8.1 %collective-permute-start.8 = (bf16[8,64,128]{2,1,0:T(8,128)(2,1)S(1)}, bf16[8,64,128]{2,1,0:T(8,128)(2,1)S(1)}, u32[]{:S(2)}, u32[]{:S(2)}) collective-permute-start(bf16[8,64,128]{2,1,0:T(8,128)(2,1)S(1)} %get-tuple-element.47), channel_id=1, source_target_pairs={{0,1},{1,0},{2,3},{3,2},{4,5},{5,4},{6,7},{7,6},{8,16},{9,17},{10,... | collective-permute-start | bytes 393224 | tf_op jit(solution)/shard_map/ppermute | solution.py:641
  26.3 5.8 %collective-permute-start.9 = (bf16[8,64,128]{2,1,0:T(8,128)(2,1)S(1)}, bf16[8,64,128]{2,1,0:T(8,128)(2,1)S(1)}, u32[]{:S(2)}, u32[]{:S(2)}) collective-permute-start(bf16[8,64,128]{2,1,0:T(8,128)(2,1)S(1)} %get-tuple-element.48), channel_id=1, source_target_pairs={{0,8},{1,9},{2,10},{3,11},{4,12},{5,13},{6,14},{7,15},{8,0},{9,1},... | collective-permute-start | bytes 393224 | tf_op jit(solution)/shard_map/ppermute | solution.py:641
  32.2 4.7 %collective-permute-start.10 = (bf16[6,64,128]{2,1,0:T(8,128)(2,1)S(1)}, bf16[6,64,128]{2,1,0:T(8,128)(2,1)S(1)}, u32[]{:S(2)}, u32[]{:S(2)}) collective-permute-start(bf16[6,64,128]{2,1,0:T(8,128)(2,1)S(1)} %get-tuple-element.53), channel_id=1, source_target_pairs={{0,8},{1,2},{2,1},{3,4},{4,3},{5,6},{6,5},{7,15},{8,0},{9,10},{10,... | collective-permute-start | bytes 294920 | tf_op jit(solution)/shard_map/ppermute | solution.py:641
  32.3 4.6 %collective-permute-start.11 = (bf16[6,64,128]{2,1,0:T(8,128)(2,1)S(1)}, bf16[6,64,128]{2,1,0:T(8,128)(2,1)S(1)}, u32[]{:S(2)}, u32[]{:S(2)}) collective-permute-start(bf16[6,64,128]{2,1,0:T(8,128)(2,1)S(1)} %get-tuple-element.54), channel_id=1, source_target_pairs={{0,1},{1,0},{2,3},{3,2},{4,5},{5,4},{6,7},{7,6},{8,9},{9,8},{10,11... | collective-permute-start | bytes 294920 | tf_op jit(solution)/shard_map/ppermute | solution.py:641
  37.9 7.9 %copy-start.3 = (bf16[3,64,576]{2,1,0:T(8,128)(2,1)S(1)}, bf16[3,64,576]{2,1,0:T(8,128)(2,1)}, u32[]{:S(2)}) copy-start(bf16[3,64,576]{2,1,0:T(8,128)(2,1)} %param.17) | copy-start | bytes 663556
  37.9 7.4 %collective-permute-start.12 = (bf16[9,64,128]{2,1,0:T(8,128)(2,1)S(1)}, bf16[9,64,128]{2,1,0:T(8,128)(2,1)S(1)}, u32[]{:S(2)}, u32[]{:S(2)}) collective-permute-start(bf16[9,64,128]{2,1,0:T(8,128)(2,1)S(1)} %get-tuple-element.57), channel_id=1, source_target_pairs={{0,1},{1,0},{2,3},{3,2},{4,5},{5,4},{6,7},{7,6},{8,16},{9,17},{10,... | collective-permute-start | bytes 442376 | tf_op jit(solution)/shard_map/ppermute | solution.py:641
  39.7 5.6 %collective-permute-start.13 = (bf16[9,64,128]{2,1,0:T(8,128)(2,1)S(1)}, bf16[9,64,128]{2,1,0:T(8,128)(2,1)S(1)}, u32[]{:S(2)}, u32[]{:S(2)}) collective-permute-start(bf16[9,64,128]{2,1,0:T(8,128)(2,1)S(1)} %get-tuple-element.58), channel_id=1, source_target_pairs={{0,8},{1,9},{2,10},{3,11},{4,12},{5,13},{6,14},{7,15},{8,0},{9,1},... | collective-permute-start | bytes 442376 | tf_op jit(solution)/shard_map/ppermute | solution.py:641
  45.4 5.9 %collective-permute-start.14 = (bf16[13,64,128]{2,1,0:T(8,128)(2,1)S(1)}, bf16[13,64,128]{2,1,0:T(8,128)(2,1)S(1)}, u32[]{:S(2)}, u32[]{:S(2)}) collective-permute-start(bf16[13,64,128]{2,1,0:T(8,128)(2,1)S(1)} %get-tuple-element.65), channel_id=1, source_target_pairs={{0,8},{1,2},{2,1},{3,4},{4,3},{5,6},{6,5},{7,15},{8,0},{9,10},{10,... | collective-permute-start | bytes 638984 | tf_op jit(solution)/shard_map/ppermute | solution.py:641
  45.5 5.8 %collective-permute-start.15 = (bf16[13,64,128]{2,1,0:T(8,128)(2,1)S(1)}, bf16[13,64,128]{2,1,0:T(8,128)(2,1)S(1)}, u32[]{:S(2)}, u32[]{:S(2)}) collective-permute-start(bf16[13,64,128]{2,1,0:T(8,128)(2,1)S(1)} %get-tuple-element.66), channel_id=1, source_target_pairs={{0,1},{1,0},{2,3},{3,2},{4,5},{5,4},{6,7},{7,6},{8,9},{9,8},{10,11... | collective-permute-start | bytes 638984 | tf_op jit(solution)/shard_map/ppermute | solution.py:641
  51.4 12.2 %copy-start.1 = (bf16[32,128,128]{2,1,0:T(8,128)(2,1)S(1)}, bf16[32,128,128]{2,1,0:T(8,128)(2,1)}, u32[]{:S(2)}) copy-start(bf16[32,128,128]{2,1,0:T(8,128)(2,1)} %weight_ref.1) | copy-start | bytes 3145732
  51.4 12.2 %copy-start.4 = (s32[32,128]{1,0:T(8,128)S(1)}, s32[32,128]{1,0:T(8,128)}, u32[]{:S(2)}) copy-start(s32[32,128]{1,0:T(8,128)} %nodes_ref.3) | copy-start | bytes 49156
  51.4 12.2 %copy-start.5 = (s32[16]{0:T(128)S(1)}, s32[16]{0:T(128)}, u32[]{:S(2)}) copy-start(s32[16]{0:T(128)} %counts_ref.3) | copy-start | bytes 196
  51.4 12.2 %copy-start.6 = (s32[32]{0:T(128)S(1)}, s32[32]{0:T(128)}, u32[]{:S(2)}) copy-start(s32[32]{0:T(128)} %block_ref.3) | copy-start | bytes 388
  51.4 12.2 %copy-start.7 = (s32[32,1]{0,1:T(1,128)S(1)}, s32[32,1]{0,1:T(1,128)}, u32[]{:S(2)}) copy-start(s32[32,1]{0,1:T(1,128)} %param.13) | copy-start | bytes 388
  53.1 3.9 %collective-permute-start.17 = (bf16[3,32,128]{2,1,0:T(8,128)(2,1)S(1)}, bf16[3,32,128]{2,1,0:T(8,128)(2,1)S(1)}, u32[]{:S(2)}, u32[]{:S(2)}) collective-permute-start(bf16[3,32,128]{2,1,0:T(8,128)(2,1)S(1)} %get-tuple-element.68.own_ref), channel_id=1, source_target_pairs={{0,8},{1,9},{2,10},{3,11},{4,12},{5,13},{6,14},{7,15},{8,0},{9,1},... | collective-permute-start | bytes 73736 | tf_op jit(solution)/shard_map/ppermute | solution.py:641
  53.2 6.0 %collective-permute-start.16 = (bf16[3,32,128]{2,1,0:T(8,128)(2,1)S(1)}, bf16[3,32,128]{2,1,0:T(8,128)(2,1)S(1)}, u32[]{:S(2)}, u32[]{:S(2)}) collective-permute-start(bf16[3,32,128]{2,1,0:T(8,128)(2,1)S(1)} %get-tuple-element.68.own_ref), channel_id=1, source_target_pairs={{0,1},{1,0},{2,3},{3,2},{4,5},{5,4},{6,7},{7,6},{8,16},{9,17},{10,... | collective-permute-start | bytes 73736 | tf_op jit(solution)/shard_map/ppermute | solution.py:641
  59.2 4.4 %collective-permute-start.19 = (bf16[3,3,32,128]{3,2,1,0:T(8,128)(2,1)S(1)}, bf16[3,3,32,128]{3,2,1,0:T(8,128)(2,1)S(1)}, u32[]{:S(2)}, u32[]{:S(2)}) collective-permute-start(bf16[3,3,32,128]{3,2,1,0:T(8,128)(2,1)S(1)} %shard_map.112.row_ref), channel_id=1, source_target_pairs={{0,8},{1,2},{2,1},{3,4},{4,3},{5,6},{6,5},{7,15},{8,0},{9,10},{10,... | collective-permute-start | bytes 221192 | tf_op jit(solution)/shard_map/ppermute | solution.py:641
  59.3 4.3 %collective-permute-start.18 = (bf16[3,3,32,128]{3,2,1,0:T(8,128)(2,1)S(1)}, bf16[3,3,32,128]{3,2,1,0:T(8,128)(2,1)S(1)}, u32[]{:S(2)}, u32[]{:S(2)}) collective-permute-start(bf16[3,3,32,128]{3,2,1,0:T(8,128)(2,1)S(1)} %shard_map.112.row_ref), channel_id=1, source_target_pairs={{0,1},{1,0},{2,3},{3,2},{4,5},{5,4},{6,7},{7,6},{8,9},{9,8},{10,11... | collective-permute-start | bytes 221192 | tf_op jit(solution)/shard_map/ppermute | solution.py:641

commit v5 on v4

--- a/solution.py
+++ b/solution.py
@@ -255,20 +255,22 @@
 def sorted_x(one_ref, two_ref, xl_ref, xh_ref):
     x_lo, x_hi, _, _ = edges()
     odd = (lax.axis_index("gx") + 1) % 2 == 1
+    zero = jnp.zeros((CHAN, LANES), BF)
     for i in range(xl_ref.shape[0]):
-        one = one_ref[i].astype(F32)
-        two = two_ref[i].astype(F32)
-        xl_ref[i] = jnp.where(x_lo, jnp.where(odd, one, two), 0.0).astype(BF)
-        xh_ref[i] = jnp.where(x_hi, jnp.where(odd, two, one), 0.0).astype(BF)
+        one = one_ref[i]
+        two = two_ref[i]
+        xl_ref[i] = jnp.where(x_lo, jnp.where(odd, one, two), zero)
+        xh_ref[i] = jnp.where(x_hi, jnp.where(odd, two, one), zero)
 
 
 def sorted_y(one_ref, two_ref, i):
     _, _, y_lo, y_hi = edges()
     odd = (lax.axis_index("gy") + 1) % 2 == 1
-    one = one_ref[i].astype(F32)
-    two = two_ref[i].astype(F32)
-    lower = jnp.where(y_lo, jnp.where(odd, one, two), 0.0).astype(BF)
-    higher = jnp.where(y_hi, jnp.where(odd, two, one), 0.0).astype(BF)
+    zero = jnp.zeros((CHAN, LANES), BF)
+    one = one_ref[i]
+    two = two_ref[i]
+    lower = jnp.where(y_lo, jnp.where(odd, one, two), zero)
+    higher = jnp.where(y_hi, jnp.where(odd, two, one), zero)
     return lower, higher
 
 
@@ -443,7 +445,7 @@
 
 
 def inner_mid_kernel(
-    coarse_ref, xl_ref, xh_ref, act_ref, mid_weight_ref, out_weight_ref, stack, taps, mid_ref
+    coarse_ref, xl_ref, xh_ref, act_ref, mid_weight_ref, out_weight_ref, stack, share, taps, mid_ref
 ):
     x_lo, x_hi, _, _ = edges()
     half_x = TILE_X // 2
@@ -476,10 +478,15 @@
                 fine = act_ref[x - 1, y + 2].astype(F32)
                 columns.append((fine + value.astype(F32)).astype(BF))
         put_taps(weight, taps, [(x, y) for y in range(4)], columns)
+    for x in range(TILE_X):
+        for y in range(1, TILE_Y - 1):
+            near = [(a, b) for a in range(3) for b in range(3) if 2 <= y + b - 1 < 6]
+            starts = [(x + a, y + b - 3, (a * 3 + b) * 24) for a, b in near]
+            share[x, y - 1] = added([taps[u, v, i : i + 24, :] for u, v, i in starts])
 
 
 def outer_mid_kernel(
-    act_ref, stack, inner, xl_ref, xh_ref, y_one_ref, y_two_ref, mid_weight_ref, out_weight_ref,
+    act_ref, stack, share_ref, xl_ref, xh_ref, y_one_ref, y_two_ref, mid_weight_ref, out_weight_ref,
     field_ref, sent_ref, edge, mid_ref, taps, yl_ref, yh_ref,
 ):
     x_lo, x_hi, y_lo, y_hi = edges()
@@ -527,26 +534,18 @@
                 columns.append((fine + value.astype(F32)).astype(BF))
         put_taps(weight, taps, [(x, k) for k in range(6)], columns)
 
-    def tap(x, y, start):
-        if y in rows:
-            return taps[x, rows.index(y), start : start + 24, :]
-        return inner[x, y - 2, start : start + 24, :]
-
     def received(ref, place, row):
         piece = ref[place].astype(F32)[row : row + 6]
         return piece[0:3] + piece[3:6]
 
     for x in range(TILE_X):
         for y in range(TILE_Y):
-            value = joined(
-                added(
-                    [
-                        tap(x + a, y + b - 1, (a * 3 + b) * 24)
-                        for a in range(3)
-                        for b in range(3)
-                    ]
-                )
-            )
+            near = [(a, b) for a in range(3) for b in range(3) if y + b - 1 in rows]
+            starts = [(x + a, rows.index(y + b - 1), (a * 3 + b) * 24) for a, b in near]
+            pieces = [taps[u, v, i : i + 24, :] for u, v, i in starts]
+            if 0 < y < TILE_Y - 1:
+                pieces.append(share_ref[x, y - 1])
+            value = joined(added(pieces))
             x_ref = xl_ref if x == 0 else xh_ref
             y_ref = yl_ref if y == 0 else yh_ref
             on_x = x in (0, TILE_X - 1)
@@ -755,10 +754,10 @@
         inner_mid_kernel,
         [
             ((6, TILE_Y // 2, 3 * CHAN, LANES), BF),
-            ((TILE_X + 2, 4, PADDED, LANES), F32),
+            ((TILE_X, TILE_Y - 2, 24, LANES), F32),
         ],
         [VM] * 6,
-        [pltpu.VMEM((4, 2, *column), BF)],
+        [pltpu.VMEM((TILE_X + 2, 4, PADDED, LANES), F32), pltpu.VMEM((4, 2, *column), BF)],
         1000000000,
     )(coarse, xl, xh, act, mid_weight, out_weight)
     field, rounded = call(

time: 65.8 us -> 66.1 us (level)
  starting transfers between devices: 17.1 us -> 17.8 us
where the time goes in v5:
time: 66.1 us; the launch traced here: 65.6 us
  waiting for transfers between devices  30.1 us (46%)
  starting transfers between devices  17.8 us (27%)
  Pallas kernels  15.4 us (23%)
  local copies, waits for them, and re-layouts  1.79 us (3%)
    ppermute x20, waiting for transfers between devices, swapped(): return lax.ppermute(value, ('gx', 'gy'), pairs)  30.1 us
    ppermute x20, starting transfers between devices, swapped(): return lax.ppermute(value, ('gx', 'gy'), pairs)  17.8 us
    pallas_call x4, Pallas kernels, scatter(): call(functools.partial(scatter_kernel, len(parts), first, rows), outs, [V...  3.93 us
    pallas_call x1, Pallas kernels, shards(): call(partial_kernel, [(packed, BF)] * 9, [SM] * 3 + [HB, VM, HB], [pltpu....  3.86 us
    pallas_call x1, Pallas kernels, shards(): call(outer_mid_kernel, [((3, TILE_X * TILE_Y, LANES), F32), ((3, TILE_X *...  1.71 us
    pallas_call x1, Pallas kernels, shards(): call(inner_mid_kernel, [((6, TILE_Y // 2, 3 * CHAN, LANES), BF), ((TILE_X...  1.51 us
    pallas_call x1, Pallas kernels, shards(): call(gather_kernel, [((blocks, 3, LANES), F32)], [SM] * 3 + [VM] * 6, [pl...  1.42 us
    pallas_call x1, Pallas kernels, shards(): call(inner_conv_kernel, [((TILE_X + 2, TILE_Y, 3 * CHAN, LANES), BF), ((T...  1.41 us
  transfers between devices with their start and end apart: 20, of which 12 were waited for; matrix products, arithmetic and copies ran while one was open for 1% of the time, Pallas kernels for 10%

profile of v5, /device:TPU:16, one launch (start us, length us, event | category | flops | bytes accessed | tf_op | source)
XLA Modules:
  0.0 65.6 jit_solution(16820147388316732134)
XLA Ops:
  0.0 3.9 %shard_map.100 = (bf16[528,128]{1,0:T(8,128)(2,1)}, bf16[528,128]{1,0:T(8,128)(2,1)}, bf16[528,128]{1,0:T(8,128)(2,1)}, bf16[528,128]{1,0:T(8,128)(2,1)}, bf16[5...) custom-call(s32[16]{0:T(128)} %counts_ref.3, ...), custom_call_target="tpu_custom_call" | custom-call | flops 70000000 | bytes 2000000 | tf_op jit(solution)/shard_map/pallas_call | solution.py:671
  3.9 4.0 %collective-permute-start.2 = (bf16[528,128]{1,0:T(8,128)(2,1)}, bf16[528,128]{1,0:T(8,128)(2,1)S(1)}, u32[]{:S(2)}, u32[]{:S(2)}) collective-permute-start(bf16[528,128]{1,0:T(8,128)(2,1)} %get-tuple-element.39), channel_id=1, source_target_pairs={{0,1},{1,0},{2,3},{3,2},{4,5},{5,4},{6,7},{7,6},{8,16},{9,17},{10,... | collective-permute-start | bytes 405512 | tf_op jit(solution)/shard_map/ppermute | solution.py:640
  7.9 2.0 %collective-permute-start.4 = (bf16[528,128]{1,0:T(8,128)(2,1)}, bf16[528,128]{1,0:T(8,128)(2,1)S(1)}, u32[]{:S(2)}, u32[]{:S(2)}) collective-permute-start(bf16[528,128]{1,0:T(8,128)(2,1)} %get-tuple-element.41), channel_id=1, source_target_pairs={{0,8},{1,2},{2,1},{3,4},{4,3},{5,6},{6,5},{7,15},{8,0},{9,10},{10,... | collective-permute-start | bytes 405512 | tf_op jit(solution)/shard_map/ppermute | solution.py:640
  9.9 1.3 %collective-permute-start.6 = (bf16[528,128]{1,0:T(8,128)(2,1)}, bf16[528,128]{1,0:T(8,128)(2,1)S(1)}, u32[]{:S(2)}, u32[]{:S(2)}) collective-permute-start(bf16[528,128]{1,0:T(8,128)(2,1)} %get-tuple-element.43), channel_id=1, source_target_pairs={{0,1},{1,0},{2,3},{3,2},{4,5},{5,4},{6,7},{7,6},{8,17},{9,18},{10,... | collective-permute-start | bytes 405512 | tf_op jit(solution)/shard_map/ppermute | solution.py:640
  11.2 0.5 collective-permute-done.2.refs_0_
  11.7 0.1 collective-permute-start.7
  11.8 1.4 %collective-permute-done.3.refs_1_ = bf16[528,128]{1,0:T(8,128)(2,1)S(1)} collective-permute-done((bf16[528,128]{1,0:T(8,128)(2,1)}, bf16[528,128]{1,0:T(8,128)(2,1)S(1)}, u32[]{:S(2)}, u32[]{:S(2)}) %collective-permute-start.3) | collective-permute-done | bytes 135200 | tf_op jit(solution)/shard_map/ppermute | solution.py:640
  13.1 1.5 %collective-permute-start = (bf16[528,128]{1,0:T(8,128)(2,1)}, bf16[528,128]{1,0:T(8,128)(2,1)S(1)}, u32[]{:S(2)}, u32[]{:S(2)}) collective-permute-start(bf16[528,128]{1,0:T(8,128)(2,1)} %get-tuple-element.37), channel_id=1, source_target_pairs={{0,1},{1,0},{2,3},{3,2},{4,5},{5,4},{6,7},{7,6},{8,24},{9,16},{10,... | collective-permute-start | bytes 405512 | tf_op jit(solution)/shard_map/ppermute | solution.py:640
  14.6 1.2 %collective-permute-start.1 = (bf16[528,128]{1,0:T(8,128)(2,1)}, bf16[528,128]{1,0:T(8,128)(2,1)S(1)}, u32[]{:S(2)}, u32[]{:S(2)}) collective-permute-start(bf16[528,128]{1,0:T(8,128)(2,1)} %get-tuple-element.38), channel_id=1, source_target_pairs={{0,15},{1,8},{2,9},{3,10},{4,11},{5,12},{6,13},{7,14},{8,1},{9,2},... | collective-permute-start | bytes 405512 | tf_op jit(solution)/shard_map/ppermute | solution.py:640
  15.8 0.9 %copy-done.8 = bf16[528,128]{1,0:T(8,128)(2,1)S(1)} copy-done((bf16[528,128]{1,0:T(8,128)(2,1)S(1)}, bf16[528,128]{1,0:T(8,128)(2,1)}, u32[]{:S(2)}) %copy-start.8) | copy-done | bytes 135192
  16.7 1.0 %shard_map.101.refs_6_ = f32[1024,256]{1,0:T(8,128)S(1)} custom-call(bf16[528,128]{1,0:T(8,128)(2,1)S(1)} %copy-done.8), custom_call_target="tpu_custom_call" | custom-call | flops 800000000 | bytes 2000000 | tf_op jit(solution)/shard_map/pallas_call | solution.py:181
  17.7 0.0 copy-start.9
  17.8 1.0 %collective-permute-done.6.refs_4_ = bf16[528,128]{1,0:T(8,128)(2,1)S(1)} collective-permute-done((bf16[528,128]{1,0:T(8,128)(2,1)}, bf16[528,128]{1,0:T(8,128)(2,1)S(1)}, u32[]{:S(2)}, u32[]{:S(2)}) %collective-permute-start.6) | collective-permute-done | bytes 135200 | tf_op jit(solution)/shard_map/ppermute | solution.py:640
  18.8 1.8 %shard_map.102.refs_2_ = f32[1024,256]{1,0:T(8,128)S(1)} custom-call(bf16[528,128]{1,0:T(8,128)(2,1)S(1)} %collective-permute-done.2.refs_0_, bf16[528,128]{1,0:T(8,128)(2,1)S(1)} %collective-permute-done.3.refs_1_, bf16[528,128]{1,0:T(8,128)(2,1)S(1)} %collective-permute-done.4.refs_2_, bf16[528,128]{1,0:T(8,128)(2,1)S(1)} %collective-permute-done.5.refs_3_, ...), custom_call_target="tpu_custom_call" | custom-call | flops 800000000 | bytes 2000000 | tf_op jit(solution)/shard_map/pallas_call | solution.py:181
  20.6 1.7 %collective-permute-done.refs_0_ = bf16[528,128]{1,0:T(8,128)(2,1)S(1)} collective-permute-done((bf16[528,128]{1,0:T(8,128)(2,1)}, bf16[528,128]{1,0:T(8,128)(2,1)S(1)}, u32[]{:S(2)}, u32[]{:S(2)}) %collective-permute-start) | collective-permute-done | bytes 135200 | tf_op jit(solution)/shard_map/ppermute | solution.py:640
  22.4 1.0 %collective-permute-done.1.refs_1_ = bf16[528,128]{1,0:T(8,128)(2,1)S(1)} collective-permute-done((bf16[528,128]{1,0:T(8,128)(2,1)}, bf16[528,128]{1,0:T(8,128)(2,1)S(1)}, u32[]{:S(2)}, u32[]{:S(2)}) %collective-permute-start.1) | collective-permute-done | bytes 135200 | tf_op jit(solution)/shard_map/ppermute | solution.py:640
  23.4 0.6 shard_map.103
  24.0 0.0 copy-start.2
  24.0 2.3 %collective-permute-start.8 = (bf16[8,64,128]{2,1,0:T(8,128)(2,1)S(1)}, bf16[8,64,128]{2,1,0:T(8,128)(2,1)S(1)}, u32[]{:S(2)}, u32[]{:S(2)}) collective-permute-start(bf16[8,64,128]{2,1,0:T(8,128)(2,1)S(1)} %get-tuple-element.47), channel_id=1, source_target_pairs={{0,1},{1,0},{2,3},{3,2},{4,5},{5,4},{6,7},{7,6},{8,16},{9,17},{10,... | collective-permute-start | bytes 393224 | tf_op jit(solution)/shard_map/ppermute | solution.py:640
  26.3 0.2 collective-permute-start.9
  26.4 0.2 reduce-precision_convert_fusion
  26.7 0.1 pad.7.clone
  26.8 0.5 shard_map.104.middle_ref
  27.3 4.7 %collective-permute-done.8.one_ref = bf16[8,64,128]{2,1,0:T(8,128)(2,1)S(1)} collective-permute-done((bf16[8,64,128]{2,1,0:T(8,128)(2,1)S(1)}, bf16[8,64,128]{2,1,0:T(8,128)(2,1)S(1)}, u32[]{:S(2)}, u32[]{:S(2)}) %collective-permute-start.8) | collective-permute-done | bytes 131104 | tf_op jit(solution)/shard_map/ppermute | solution.py:640
  32.0 0.1 shard_map.105
  32.1 0.6 collective-permute-start.10
  32.8 0.1 maximum_maximum_fusion
  32.9 0.1 convert_element_type.13
  33.0 1.4 %shard_map.106 = (bf16[6,8,192,128]{3,2,1,0:T(8,128)(2,1)S(1)}, bf16[4,6,64,128]{3,2,1,0:T(8,128)(2,1)S(1)}) custom-call(bf16[2,8,64,128]{3,2,1,0:T(8,128)(2,1)S(1)} %get-tuple-element.46.outer_ref, bf16[2,8,64,128]{3,2,1,0:T(8,128)(2,1)S(1)} %shard_map.104.middle_ref, bf16[8,64,128]{2,1,0:T(8,128)(2,1)S(1)} %get-tuple-element.49.xl_ref, ...), custom_call_target="tpu_custom_call" | custom-call | flops 1000000000 | bytes 2000000 | tf_op jit(solution)/shard_map/pallas_call | solution.py:709
  34.4 2.4 %collective-permute-done.10.y_one_ref = bf16[6,64,128]{2,1,0:T(8,128)(2,1)S(1)} collective-permute-done((bf16[6,64,128]{2,1,0:T(8,128)(2,1)S(1)}, bf16[6,64,128]{2,1,0:T(8,128)(2,1)S(1)}, u32[]{:S(2)}, u32[]{:S(2)}) %collective-permute-start.10) | collective-permute-done | bytes 98336 | tf_op jit(solution)/shard_map/ppermute | solution.py:640
  36.8 1.0 %shard_map.107 = (bf16[4,8,64,128]{3,2,1,0:T(8,128)(2,1)S(1)}, bf16[2,4,64,128]{3,2,1,0:T(8,128)(2,1)S(1)}, bf16[9,64,128]{2,1,0:T(8,128)(2,1)S(1)}, bf16[9,64,128]{2,1,0:T(8,128)(2,1)S(1)}) custom-call(bf16[2,8,64,128]{3,2,1,0:T(8,128)(2,1)S(1)} %get-tuple-element.46.outer_ref, bf16[2,8,64,128]{3,2,1,0:T(8,128)(2,1)S(1)} %shard_map.104.middle_ref, ...), custom_call_target="tpu_custom_call" | custom-call | flops 600000000 | bytes 2000000 | tf_op jit(solution)/shard_map/pallas_call | solution.py:719
  37.9 1.8 %collective-permute-start.12 = (bf16[9,64,128]{2,1,0:T(8,128)(2,1)S(1)}, bf16[9,64,128]{2,1,0:T(8,128)(2,1)S(1)}, u32[]{:S(2)}, u32[]{:S(2)}) collective-permute-start(bf16[9,64,128]{2,1,0:T(8,128)(2,1)S(1)} %get-tuple-element.57), channel_id=1, source_target_pairs={{0,1},{1,0},{2,3},{3,2},{4,5},{5,4},{6,7},{7,6},{8,16},{9,17},{10,... | collective-permute-start | bytes 442376 | tf_op jit(solution)/shard_map/ppermute | solution.py:640
  39.7 0.3 shard_map.108
  40.0 5.2 %collective-permute-done.12.one_ref = bf16[9,64,128]{2,1,0:T(8,128)(2,1)S(1)} collective-permute-done((bf16[9,64,128]{2,1,0:T(8,128)(2,1)S(1)}, bf16[9,64,128]{2,1,0:T(8,128)(2,1)S(1)}, u32[]{:S(2)}, u32[]{:S(2)}) %collective-permute-start.12) | collective-permute-done | bytes 147488 | tf_op jit(solution)/shard_map/ppermute | solution.py:640
  45.2 0.1 shard_map.109
  45.4 0.1 collective-permute-start.14
  45.5 0.5 collective-permute-start.15
  45.9 1.5 %shard_map.110 = (bf16[6,4,192,128]{3,2,1,0:T(8,128)(2,1)S(1)}, f32[4,6,24,128]{3,2,1,0:T(8,128)S(1)}) custom-call(bf16[2,4,64,128]{3,2,1,0:T(8,128)(2,1)S(1)} %get-tuple-element.56.coarse_ref, bf16[9,64,128]{2,1,0:T(8,128)(2,1)S(1)} %get-tuple-element.61.xl_ref, bf16[9,64,128]{2,1,0:T(8,128)(2,1)S(1)} %get-tuple-element.62.xh_ref, ...), custom_call_target="tpu_custom_call" | custom-call | flops 1000000000 | bytes 2000000 | tf_op jit(solution)/shard_map/pallas_call | solution.py:753
  47.5 3.8 %collective-permute-done.14.y_one_ref = bf16[13,64,128]{2,1,0:T(8,128)(2,1)S(1)} collective-permute-done((bf16[13,64,128]{2,1,0:T(8,128)(2,1)S(1)}, bf16[13,64,128]{2,1,0:T(8,128)(2,1)S(1)}, u32[]{:S(2)}, u32[]{:S(2)}) %collective-permute-start.14) | collective-permute-done | bytes 213024 | tf_op jit(solution)/shard_map/ppermute | solution.py:640
  51.3 1.7 %shard_map.111 = (f32[3,32,128]{2,1,0:T(8,128)S(1)}, bf16[3,32,128]{2,1,0:T(8,128)(2,1)S(1)}) custom-call(bf16[4,8,64,128]{3,2,1,0:T(8,128)(2,1)S(1)} %get-tuple-element.55.act_ref, bf16[6,4,192,128]{3,2,1,0:T(8,128)(2,1)S(1)} %get-tuple-element.63.stack, f32[4,6,24,128]{3,2,1,0:T(8,128)S(1)} %get-tuple-element.64.share_ref, ...), custom_call_target="tpu_custom_call" | custom-call | flops 1300000000 | bytes 2000000 | tf_op jit(solution)/shard_map/pallas_call | solution.py:763
  53.1 0.1 collective-permute-start.17
  53.2 2.1 %collective-permute-start.16 = (bf16[3,32,128]{2,1,0:T(8,128)(2,1)S(1)}, bf16[3,32,128]{2,1,0:T(8,128)(2,1)S(1)}, u32[]{:S(2)}, u32[]{:S(2)}) collective-permute-start(bf16[3,32,128]{2,1,0:T(8,128)(2,1)S(1)} %get-tuple-element.68.own_ref), channel_id=1, source_target_pairs={{0,1},{1,0},{2,3},{3,2},{4,5},{5,4},{6,7},{7,6},{8,16},{9,17},{10,... | collective-permute-start | bytes 73736 | tf_op jit(solution)/shard_map/ppermute | solution.py:640
  55.2 1.8 %collective-permute-done.17.two_ref = bf16[3,32,128]{2,1,0:T(8,128)(2,1)S(1)} collective-permute-done((bf16[3,32,128]{2,1,0:T(8,128)(2,1)S(1)}, bf16[3,32,128]{2,1,0:T(8,128)(2,1)S(1)}, u32[]{:S(2)}, u32[]{:S(2)}) %collective-permute-start.17) | collective-permute-done | bytes 24608 | tf_op jit(solution)/shard_map/ppermute | solution.py:640
  57.0 2.2 %collective-permute-done.16.one_ref = bf16[3,32,128]{2,1,0:T(8,128)(2,1)S(1)} collective-permute-done((bf16[3,32,128]{2,1,0:T(8,128)(2,1)S(1)}, bf16[3,32,128]{2,1,0:T(8,128)(2,1)S(1)}, u32[]{:S(2)}, u32[]{:S(2)}) %collective-permute-start.16) | collective-permute-done | bytes 24608 | tf_op jit(solution)/shard_map/ppermute | solution.py:640
  59.2 0.1 collective-permute-start.18
  59.3 4.3 %collective-permute-done.19.y_one_ref = bf16[3,3,32,128]{3,2,1,0:T(8,128)(2,1)S(1)} collective-permute-done((bf16[3,3,32,128]{3,2,1,0:T(8,128)(2,1)S(1)}, bf16[3,3,32,128]{3,2,1,0:T(8,128)(2,1)S(1)}, u32[]{:S(2)}, u32[]{:S(2)}) %collective-permute-start.19) | collective-permute-done | bytes 73760 | tf_op jit(solution)/shard_map/ppermute | solution.py:640
  63.6 1.4 %shard_map.113 = f32[16,3,128]{2,1,0:T(4,128)S(1)} custom-call(s32[16]{0:T(128)S(1)} %copy-done.4, s32[32]{0:T(128)S(1)} %copy-done.5, s32[32]{0:T(128)S(1)} %bitcast.16, f32[3,32,128]{2,1,0:T(8,128)S(1)} %get-tuple-element.67.own_ref, bf16[3,3,32,128]{3,2,1,0:T(8,128)(2,1)S(1)} %shard_map.112.row_ref, ...), custom_call_target="tpu_custom_call" | custom-call | flops 70000000 | bytes 2000000 | tf_op jit(solution)/shard_map/pallas_call | solution.py:786
  65.0 0.6 copy.14
  (34 shorter events, 0.1 us)
Async XLA Ops:
  0.0 26.4 %copy-start = (bf16[3,64,576]{2,1,0:T(8,128)(2,1)S(1)}, bf16[3,64,576]{2,1,0:T(8,128)(2,1)}, u32[]{:S(2)}) copy-start(bf16[3,64,576]{2,1,0:T(8,128)(2,1)} %param.18) | copy-start | bytes 663556
  3.9 7.8 %collective-permute-start.2 = (bf16[528,128]{1,0:T(8,128)(2,1)}, bf16[528,128]{1,0:T(8,128)(2,1)S(1)}, u32[]{:S(2)}, u32[]{:S(2)}) collective-permute-start(bf16[528,128]{1,0:T(8,128)(2,1)} %get-tuple-element.39), channel_id=1, source_target_pairs={{0,1},{1,0},{2,3},{3,2},{4,5},{5,4},{6,7},{7,6},{8,16},{9,17},{10,... | collective-permute-start | bytes 405512 | tf_op jit(solution)/shard_map/ppermute | solution.py:640
  7.9 5.3 %collective-permute-start.3 = (bf16[528,128]{1,0:T(8,128)(2,1)}, bf16[528,128]{1,0:T(8,128)(2,1)S(1)}, u32[]{:S(2)}, u32[]{:S(2)}) collective-permute-start(bf16[528,128]{1,0:T(8,128)(2,1)} %get-tuple-element.40), channel_id=1, source_target_pairs={{0,8},{1,9},{2,10},{3,11},{4,12},{5,13},{6,14},{7,15},{8,0},{9,1},... | collective-permute-start | bytes 405512 | tf_op jit(solution)/shard_map/ppermute | solution.py:640
  7.9 6.8 %collective-permute-start.4 = (bf16[528,128]{1,0:T(8,128)(2,1)}, bf16[528,128]{1,0:T(8,128)(2,1)S(1)}, u32[]{:S(2)}, u32[]{:S(2)}) collective-permute-start(bf16[528,128]{1,0:T(8,128)(2,1)} %get-tuple-element.41), channel_id=1, source_target_pairs={{0,8},{1,2},{2,1},{3,4},{4,3},{5,6},{6,5},{7,15},{8,0},{9,10},{10,... | collective-permute-start | bytes 405512 | tf_op jit(solution)/shard_map/ppermute | solution.py:640
  9.9 7.9 %collective-permute-start.5 = (bf16[528,128]{1,0:T(8,128)(2,1)}, bf16[528,128]{1,0:T(8,128)(2,1)S(1)}, u32[]{:S(2)}, u32[]{:S(2)}) collective-permute-start(bf16[528,128]{1,0:T(8,128)(2,1)} %get-tuple-element.42), channel_id=1, source_target_pairs={{0,1},{1,0},{2,3},{3,2},{4,5},{5,4},{6,7},{7,6},{8,9},{9,8},{10,11... | collective-permute-start | bytes 405512 | tf_op jit(solution)/shard_map/ppermute | solution.py:640
  9.9 8.9 %collective-permute-start.6 = (bf16[528,128]{1,0:T(8,128)(2,1)}, bf16[528,128]{1,0:T(8,128)(2,1)S(1)}, u32[]{:S(2)}, u32[]{:S(2)}) collective-permute-start(bf16[528,128]{1,0:T(8,128)(2,1)} %get-tuple-element.43), channel_id=1, source_target_pairs={{0,1},{1,0},{2,3},{3,2},{4,5},{5,4},{6,7},{7,6},{8,17},{9,18},{10,... | collective-permute-start | bytes 405512 | tf_op jit(solution)/shard_map/ppermute | solution.py:640
  11.7 7.1 %collective-permute-start.7 = (bf16[528,128]{1,0:T(8,128)(2,1)}, bf16[528,128]{1,0:T(8,128)(2,1)S(1)}, u32[]{:S(2)}, u32[]{:S(2)}) collective-permute-start(bf16[528,128]{1,0:T(8,128)(2,1)} %get-tuple-element.44), channel_id=1, source_target_pairs={{0,9},{1,10},{2,11},{3,12},{4,13},{5,14},{6,15},{7,23},{8,24},{9,0... | collective-permute-start | bytes 405512 | tf_op jit(solution)/shard_map/ppermute | solution.py:640
  13.1 9.3 %collective-permute-start = (bf16[528,128]{1,0:T(8,128)(2,1)}, bf16[528,128]{1,0:T(8,128)(2,1)S(1)}, u32[]{:S(2)}, u32[]{:S(2)}) collective-permute-start(bf16[528,128]{1,0:T(8,128)(2,1)} %get-tuple-element.37), channel_id=1, source_target_pairs={{0,1},{1,0},{2,3},{3,2},{4,5},{5,4},{6,7},{7,6},{8,24},{9,16},{10,... | collective-permute-start | bytes 405512 | tf_op jit(solution)/shard_map/ppermute | solution.py:640
  14.6 8.8 %collective-permute-start.1 = (bf16[528,128]{1,0:T(8,128)(2,1)}, bf16[528,128]{1,0:T(8,128)(2,1)S(1)}, u32[]{:S(2)}, u32[]{:S(2)}) collective-permute-start(bf16[528,128]{1,0:T(8,128)(2,1)} %get-tuple-element.38), channel_id=1, source_target_pairs={{0,15},{1,8},{2,9},{3,10},{4,11},{5,12},{6,13},{7,14},{8,1},{9,2},... | collective-permute-start | bytes 405512 | tf_op jit(solution)/shard_map/ppermute | solution.py:640
  15.8 0.9 %copy-start.8 = (bf16[528,128]{1,0:T(8,128)(2,1)S(1)}, bf16[528,128]{1,0:T(8,128)(2,1)}, u32[]{:S(2)}) copy-start(bf16[528,128]{1,0:T(8,128)(2,1)} %get-tuple-element.45.refs_0_) | copy-start | bytes 405508
  17.7 8.7 %copy-start.9 = (f32[3,64]{1,0:T(4,128)S(1)}, f32[3,64]{1,0:T(4,128)}, u32[]{:S(2)}) copy-start(f32[3,64]{1,0:T(4,128)} %param.19) | copy-start | bytes 2308
  24.0 9.1 %copy-start.2 = (bf16[3,64,576]{2,1,0:T(8,128)(2,1)S(1)}, bf16[3,64,576]{2,1,0:T(8,128)(2,1)}, u32[]{:S(2)}) copy-start(bf16[3,64,576]{2,1,0:T(8,128)(2,1)} %param.16) | copy-start | bytes 663556
  24.0 8.1 %collective-permute-start.8 = (bf16[8,64,128]{2,1,0:T(8,128)(2,1)S(1)}, bf16[8,64,128]{2,1,0:T(8,128)(2,1)S(1)}, u32[]{:S(2)}, u32[]{:S(2)}) collective-permute-start(bf16[8,64,128]{2,1,0:T(8,128)(2,1)S(1)} %get-tuple-element.47), channel_id=1, source_target_pairs={{0,1},{1,0},{2,3},{3,2},{4,5},{5,4},{6,7},{7,6},{8,16},{9,17},{10,... | collective-permute-start | bytes 393224 | tf_op jit(solution)/shard_map/ppermute | solution.py:640
  26.3 5.8 %collective-permute-start.9 = (bf16[8,64,128]{2,1,0:T(8,128)(2,1)S(1)}, bf16[8,64,128]{2,1,0:T(8,128)(2,1)S(1)}, u32[]{:S(2)}, u32[]{:S(2)}) collective-permute-start(bf16[8,64,128]{2,1,0:T(8,128)(2,1)S(1)} %get-tuple-element.48), channel_id=1, source_target_pairs={{0,8},{1,9},{2,10},{3,11},{4,12},{5,13},{6,14},{7,15},{8,0},{9,1},... | collective-permute-start | bytes 393224 | tf_op jit(solution)/shard_map/ppermute | solution.py:640
  32.1 4.7 %collective-permute-start.10 = (bf16[6,64,128]{2,1,0:T(8,128)(2,1)S(1)}, bf16[6,64,128]{2,1,0:T(8,128)(2,1)S(1)}, u32[]{:S(2)}, u32[]{:S(2)}) collective-permute-start(bf16[6,64,128]{2,1,0:T(8,128)(2,1)S(1)} %get-tuple-element.53), channel_id=1, source_target_pairs={{0,8},{1,2},{2,1},{3,4},{4,3},{5,6},{6,5},{7,15},{8,0},{9,10},{10,... | collective-permute-start | bytes 294920 | tf_op jit(solution)/shard_map/ppermute | solution.py:640
  32.8 4.1 %collective-permute-start.11 = (bf16[6,64,128]{2,1,0:T(8,128)(2,1)S(1)}, bf16[6,64,128]{2,1,0:T(8,128)(2,1)S(1)}, u32[]{:S(2)}, u32[]{:S(2)}) collective-permute-start(bf16[6,64,128]{2,1,0:T(8,128)(2,1)S(1)} %get-tuple-element.54), channel_id=1, source_target_pairs={{0,1},{1,0},{2,3},{3,2},{4,5},{5,4},{6,7},{7,6},{8,9},{9,8},{10,11... | collective-permute-start | bytes 294920 | tf_op jit(solution)/shard_map/ppermute | solution.py:640
  37.9 8.1 %copy-start.7 = (bf16[3,64,576]{2,1,0:T(8,128)(2,1)S(1)}, bf16[3,64,576]{2,1,0:T(8,128)(2,1)}, u32[]{:S(2)}) copy-start(bf16[3,64,576]{2,1,0:T(8,128)(2,1)} %param.17) | copy-start | bytes 663556
  37.9 7.4 %collective-permute-start.12 = (bf16[9,64,128]{2,1,0:T(8,128)(2,1)S(1)}, bf16[9,64,128]{2,1,0:T(8,128)(2,1)S(1)}, u32[]{:S(2)}, u32[]{:S(2)}) collective-permute-start(bf16[9,64,128]{2,1,0:T(8,128)(2,1)S(1)} %get-tuple-element.57), channel_id=1, source_target_pairs={{0,1},{1,0},{2,3},{3,2},{4,5},{5,4},{6,7},{7,6},{8,16},{9,17},{10,... | collective-permute-start | bytes 442376 | tf_op jit(solution)/shard_map/ppermute | solution.py:640
  39.7 5.6 %collective-permute-start.13 = (bf16[9,64,128]{2,1,0:T(8,128)(2,1)S(1)}, bf16[9,64,128]{2,1,0:T(8,128)(2,1)S(1)}, u32[]{:S(2)}, u32[]{:S(2)}) collective-permute-start(bf16[9,64,128]{2,1,0:T(8,128)(2,1)S(1)} %get-tuple-element.58), channel_id=1, source_target_pairs={{0,8},{1,9},{2,10},{3,11},{4,12},{5,13},{6,14},{7,15},{8,0},{9,1},... | collective-permute-start | bytes 442376 | tf_op jit(solution)/shard_map/ppermute | solution.py:640
  45.4 5.9 %collective-permute-start.14 = (bf16[13,64,128]{2,1,0:T(8,128)(2,1)S(1)}, bf16[13,64,128]{2,1,0:T(8,128)(2,1)S(1)}, u32[]{:S(2)}, u32[]{:S(2)}) collective-permute-start(bf16[13,64,128]{2,1,0:T(8,128)(2,1)S(1)} %get-tuple-element.65), channel_id=1, source_target_pairs={{0,8},{1,2},{2,1},{3,4},{4,3},{5,6},{6,5},{7,15},{8,0},{9,10},{10,... | collective-permute-start | bytes 638984 | tf_op jit(solution)/shard_map/ppermute | solution.py:640
  45.5 5.8 %collective-permute-start.15 = (bf16[13,64,128]{2,1,0:T(8,128)(2,1)S(1)}, bf16[13,64,128]{2,1,0:T(8,128)(2,1)S(1)}, u32[]{:S(2)}, u32[]{:S(2)}) collective-permute-start(bf16[13,64,128]{2,1,0:T(8,128)(2,1)S(1)} %get-tuple-element.66), channel_id=1, source_target_pairs={{0,1},{1,0},{2,3},{3,2},{4,5},{5,4},{6,7},{7,6},{8,9},{9,8},{10,11... | collective-permute-start | bytes 638984 | tf_op jit(solution)/shard_map/ppermute | solution.py:640
  51.3 12.2 %copy-start.1 = (bf16[32,128,128]{2,1,0:T(8,128)(2,1)S(1)}, bf16[32,128,128]{2,1,0:T(8,128)(2,1)}, u32[]{:S(2)}) copy-start(bf16[32,128,128]{2,1,0:T(8,128)(2,1)} %weight_ref.1) | copy-start | bytes 3145732
  51.3 12.2 %copy-start.3 = (s32[32,128]{1,0:T(8,128)S(1)}, s32[32,128]{1,0:T(8,128)}, u32[]{:S(2)}) copy-start(s32[32,128]{1,0:T(8,128)} %nodes_ref.3) | copy-start | bytes 49156
  51.3 12.2 %copy-start.4 = (s32[16]{0:T(128)S(1)}, s32[16]{0:T(128)}, u32[]{:S(2)}) copy-start(s32[16]{0:T(128)} %counts_ref.3) | copy-start | bytes 196
  51.3 12.2 %copy-start.5 = (s32[32]{0:T(128)S(1)}, s32[32]{0:T(128)}, u32[]{:S(2)}) copy-start(s32[32]{0:T(128)} %block_ref.3) | copy-start | bytes 388
  51.3 12.2 %copy-start.6 = (s32[32,1]{0,1:T(1,128)S(1)}, s32[32,1]{0,1:T(1,128)}, u32[]{:S(2)}) copy-start(s32[32,1]{0,1:T(1,128)} %param.13) | copy-start | bytes 388
  53.1 3.9 %collective-permute-start.17 = (bf16[3,32,128]{2,1,0:T(8,128)(2,1)S(1)}, bf16[3,32,128]{2,1,0:T(8,128)(2,1)S(1)}, u32[]{:S(2)}, u32[]{:S(2)}) collective-permute-start(bf16[3,32,128]{2,1,0:T(8,128)(2,1)S(1)} %get-tuple-element.68.own_ref), channel_id=1, source_target_pairs={{0,8},{1,9},{2,10},{3,11},{4,12},{5,13},{6,14},{7,15},{8,0},{9,1},... | collective-permute-start | bytes 73736 | tf_op jit(solution)/shard_map/ppermute | solution.py:640
  53.2 6.0 %collective-permute-start.16 = (bf16[3,32,128]{2,1,0:T(8,128)(2,1)S(1)}, bf16[3,32,128]{2,1,0:T(8,128)(2,1)S(1)}, u32[]{:S(2)}, u32[]{:S(2)}) collective-permute-start(bf16[3,32,128]{2,1,0:T(8,128)(2,1)S(1)} %get-tuple-element.68.own_ref), channel_id=1, source_target_pairs={{0,1},{1,0},{2,3},{3,2},{4,5},{5,4},{6,7},{7,6},{8,16},{9,17},{10,... | collective-permute-start | bytes 73736 | tf_op jit(solution)/shard_map/ppermute | solution.py:640
  59.2 4.4 %collective-permute-start.19 = (bf16[3,3,32,128]{3,2,1,0:T(8,128)(2,1)S(1)}, bf16[3,3,32,128]{3,2,1,0:T(8,128)(2,1)S(1)}, u32[]{:S(2)}, u32[]{:S(2)}) collective-permute-start(bf16[3,3,32,128]{3,2,1,0:T(8,128)(2,1)S(1)} %shard_map.112.row_ref), channel_id=1, source_target_pairs={{0,8},{1,2},{2,1},{3,4},{4,3},{5,6},{6,5},{7,15},{8,0},{9,10},{10,... | collective-permute-start | bytes 221192 | tf_op jit(solution)/shard_map/ppermute | solution.py:640
  59.2 4.3 %collective-permute-start.18 = (bf16[3,3,32,128]{3,2,1,0:T(8,128)(2,1)S(1)}, bf16[3,3,32,128]{3,2,1,0:T(8,128)(2,1)S(1)}, u32[]{:S(2)}, u32[]{:S(2)}) collective-permute-start(bf16[3,3,32,128]{3,2,1,0:T(8,128)(2,1)S(1)} %shard_map.112.row_ref), channel_id=1, source_target_pairs={{0,1},{1,0},{2,3},{3,2},{4,5},{5,4},{6,7},{7,6},{8,9},{9,8},{10,11... | collective-permute-start | bytes 221192 | tf_op jit(solution)/shard_map/ppermute | solution.py:640
